TPU v7x, 1024 devices: a whole 8x8x8 slice. The times are simulated.
1024 devices in a mesh: pair: 32 (over x, y_hi, core), virt: 32 (over y_lo, z).
Axes of the slice: x: 8, y: 8 (y_hi: 2, y_lo: 4; y = y_hi * 4 + y_lo), z: 8, core: 2. Of those that a mesh axis runs over, the one named last changes fastest.
Arguments:
- amplitudes: bfloat16 [36864, 2048], P(('pair', 'virt')), may hold values from -6 to 6
- integrals: bfloat16 [2048, 16384], P(None, 'virt'), may hold values from -0.125 to 0.125
- amp_pattern: int32 [32, 32, 2], replicated, may hold values 0 or 1
- int_pattern: int32 [2, 16], replicated, may hold values 0 or 1
Outputs:
- residual: bfloat16 [36864, 16384], P('pair', 'virt')
All inputs are finite; a program needn't handle non-finite values.
Results may differ from a plain program's by a relative error of at most 0.005.
Values may be sent and summed in bfloat16 or wider, within the bound.
No kernel may reach another device: no remote copies, remote signals or barrier semaphores. Data moves between devices by JAX's collectives and lax.ppermute only.
A program may use at most 64 MiB of HBM per device.

v0:
```python
import jax
import jax.numpy as jnp
from jax import lax
from jax.sharding import PartitionSpec as P

TP = 1024
OCC_DEV = 6


def body(amplitudes, integrals, amp_pattern, int_pattern):
    pair_count = lax.axis_size("pair")
    occ_total = OCC_DEV * pair_count
    group_rows = amplitudes.shape[0] * lax.axis_size("virt")
    cd_width = amplitudes.shape[1]
    tile_count = cd_width // TP
    col_width = integrals.shape[1]
    pair_id = lax.axis_index("pair")
    col_ids = lax.axis_index("virt") * col_width + jnp.arange(col_width)
    tile_picks = (jnp.arange(int_pattern.shape[1])[:, None] == (col_ids // TP)[None, :]).astype(
        jnp.float32
    )
    col_mask = jnp.dot(int_pattern.astype(jnp.float32), tile_picks).astype(jnp.bfloat16)
    weighted = (integrals.reshape(tile_count, TP, col_width) * col_mask[:, None, :]).reshape(
        cd_width, col_width
    )
    block_mask = lax.dynamic_index_in_dim(amp_pattern, pair_id, 0, keepdims=False).astype(
        jnp.float32
    )
    shard_rows = lax.all_gather(amplitudes, "virt", axis=0, tiled=True)
    row_count = shard_rows.shape[0]
    occ_second = jnp.arange(row_count) % occ_total
    block_picks = (
        jnp.arange(block_mask.shape[0])[None, :] == (occ_second // OCC_DEV)[:, None]
    ).astype(jnp.float32)
    row_mask = jnp.dot(block_picks, block_mask).astype(jnp.bfloat16)
    ladder = jnp.dot(
        (shard_rows.reshape(row_count, tile_count, TP) * row_mask[:, :, None]).reshape(
            row_count, cd_width
        ),
        weighted,
        preferred_element_type=jnp.float32,
    ).astype(jnp.bfloat16)
    blocks = ladder.reshape(OCC_DEV, pair_count, OCC_DEV, col_width)
    swapped = lax.all_to_all(blocks, "pair", split_axis=1, concat_axis=1, tiled=True)
    result = ladder.astype(jnp.float32) - jnp.transpose(swapped, (2, 1, 0, 3)).reshape(
        group_rows, col_width
    ).astype(jnp.float32)
    return result.astype(jnp.bfloat16)


def solution(mesh):
    placed = (P(("pair", "virt"), None), P(None, "virt"), P(), P())
    return jax.shard_map(
        body, mesh=mesh, in_specs=placed, out_specs=P("pair", "virt"), check_vma=False
    )
```

profile of v0, /device:TPU:2, one launch (start us, length us, event | category | flops | bytes accessed | tf_op | source)
XLA Modules:
  0.0 269.4 jit_solution(4200917935902683837)
XLA Ops:
  6.5 0.0 all-gather.3.cloned.1.call-start
  6.5 0.7 all-gather.3.cloned.1.call-update
  7.3 1.0 convolution_convert_fusion
  8.3 0.2 copy.9
  8.5 3.2 %mul.25 = bf16[1152,2,1024]{2,1,0:T(2,128)(2,1)S(1)} broadcast(bf16[1152,2]{1,0:T(8,128)(2,1)S(1)} %copy.9), dimensions={0,1} | broadcast | bytes 4723200 | tf_op jit(solution)/shard_map/mul | solution.py:37
  11.7 0.0 copy-start.2
  11.7 0.0 copy-start.1
  11.8 4.2 %copy.12 = bf16[144,8,2,1024]{3,1,2,0:T(8,128)(2,1)} copy(bf16[144,8,2,1024]{3,2,1,0:T(2,128)(2,1)S(1)} %bitcast.13) | data formatting | bytes 9437184
  16.0 0.0 copy-done.2
  16.0 0.1 fusion.5
  16.1 0.0 copy-done.1
  16.1 1.5 bitcast_multiply_fusion
  17.6 171.1 %all-gather.3.cloned.1.call-done = bf16[32,36,2048]{2,1,0:T(8,128)(2,1)} async-done(((bf16[1,36,2048]{2,1,0:T(8,128)(2,1)}), bf16[32,36,2048]{2,1,0:T(8,128)(2,1)}) %all-gather.3.cloned.1.call-update) | async-done | bytes 4718608 | tf_op jit(solution)/shard_map/all_gather | solution.py:29
  188.7 7.2 %reshape.56 = bf16[1152,2048]{1,0:T(8,128)(2,1)} reshape(bf16[32,36,2048]{2,1,0:T(8,128)(2,1)} %all-gather.3.cloned.1.call-done) | data formatting | bytes 9437184
  195.9 7.0 %fusion.2 = bf16[1152,512]{1,0:T(8,128)(2,1)S(1)} fusion(bf16[2048,512]{1,0:T(8,128)(2,1)} %bitcast_multiply_fusion, bf16[1152,2048]{1,0:T(8,128)(2,1)} %reshape.56, bf16[1152,2048]{1,0:T(8,128)(2,1)} %bitcast.14), kind=kOutput, calls=%fused_computation.3 | convolution fusion | flops 2418868224 | bytes 12713984 | tf_op jit(solution)/shard_map/dot_general | solution.py:36
  202.9 0.0 copy-start
  202.9 0.4 reshape.53
  203.3 0.2 copy.10
  203.5 0.4 copy-done
  203.9 51.8 %all_to_all.5 = bf16[6,32,6,512]{3,2,0,1:T(8,128)(2,1)S(1)} all-to-all(bf16[6,32,6,512]{3,2,0,1:T(8,128)(2,1)S(1)} %copy.10), channel_id=1, replica_groups=mesh['pair'=32,'virt'=32] {'pair'}, dimensions={1} | all-to-all | bytes 2359296 | tf_op jit(solution)/shard_map/all_to_all | solution.py:44
  255.7 0.4 convert_bitcast_fusion
  256.2 1.4 copy.11
  257.6 1.6 reshape.54
  259.2 3.4 %subtract_convert_fusion = bf16[1152,512]{1,0:T(8,128)(2,1)} fusion(f32[1152,512]{1,0:T(8,128)} %reshape.54, bf16[1152,512]{1,0:T(8,128)(2,1)} %copy-done), kind=kLoop, calls=%fused_computation.4 | loop fusion | flops 1769472 | bytes 4718592 | tf_op jit(solution)/shard_map/convert_element_type | solution.py:48
  (2 shorter events, 0.0 us)
Async XLA Ops:
  6.5 182.2 %all-gather.3.cloned.1.call-start = ((), (), s32[]{:S(2)}) async-start(), calls=%async_computation.1 | async-start | bytes 5406720 | tf_op jit(solution)/shard_map/all_gather | solution.py:29
  11.7 4.2 %copy-start.2 = (s32[2,16]{1,0:T(2,128)S(1)}, s32[2,16]{1,0:T(2,128)}, u32[]{:S(2)}) copy-start(s32[2,16]{1,0:T(2,128)} %param.7) | copy-start | bytes 388
  11.7 4.4 %copy-start.1 = (bf16[2048,512]{1,0:T(8,128)(2,1)S(1)}, bf16[2048,512]{1,0:T(8,128)(2,1)}, u32[]{:S(2)}) copy-start(bf16[2048,512]{1,0:T(8,128)(2,1)} %param.5) | copy-start | bytes 6291460
  202.9 1.0 copy-start
Sparse Core Ops, SparseCore 0:
  10.0 178.6 all-gather.2
where the time goes:
time: 270 us; the launch traced here: 269 us
  waiting for transfers between devices  172 us (64%)
  blocking collectives  51.8 us (19%)
  local copies, waits for them, and re-layouts  18.8 us (7%)
  between operations  13.5 us (5%)
  matrix products  8.13 us (3%)
  other arithmetic  5.31 us (2%)
    all_gather x1, waiting for transfers between devices, body(): shard_rows = lax.all_gather(amplitudes, 'virt', axis=0, tiled=True)  171 us
    all_to_all x1, blocking collectives, body(): lax.all_to_all(blocks, 'pair', split_axis=1, concat_axis=1, tiled=True)  51.8 us
    unnamed x8, local copies, waits for them, and re-layouts  11.8 us
    dot_general x1, matrix products, body(): jnp.dot((shard_rows.reshape(row_count, tile_count, TP) * row_mask[:, :, N...  6.98 us
  transfers between devices with their start and end apart: 1, of which 1 were waited for; matrix products, arithmetic and copies ran while one was open for 4% of the time, Pallas kernels for 0%

commit v1 on v0

v1 whole, which is shorter than its diff:
```python
import jax
import jax.numpy as jnp
from jax import lax
from jax.sharding import Mesh, PartitionSpec as P

TP = 1024
OCC = 6
NY = 4
NZ = 8
NP = 32
AXES = ("x", "yh", "core", "y", "z")
PAIR = ("x", "yh", "core")
VIRT = ("y", "z")


def body(amplitudes, integrals, amp_pattern, int_pattern):
    rows, kcd = amplitudes.shape
    cols = integrals.shape[1]
    tiles = kcd // TP
    p = lax.axis_index(PAIR)
    v = lax.axis_index(VIRT)
    z = lax.axis_index("z")
    second = (v * rows + jnp.arange(rows)) % (OCC * NP) // OCC
    block_mask = lax.dynamic_index_in_dim(amp_pattern, p, 0, keepdims=False)
    picks = (second[:, None] == jnp.arange(NP)[None, :]).astype(jnp.float32)
    row_mask = jnp.dot(picks, block_mask.astype(jnp.float32)).astype(jnp.bfloat16)
    screened = amplitudes * jnp.repeat(row_mask, TP, axis=1)
    col_mask = lax.dynamic_index_in_dim(int_pattern, v * cols // TP, 1, keepdims=False)
    weighted = integrals * jnp.repeat(col_mask, TP).astype(jnp.bfloat16)[:, None]

    packed = jnp.concatenate([screened[:, t * TP : (t + 1) * TP] for t in range(tiles)], 0)
    gathered = lax.all_gather(packed, "y", axis=0, tiled=False)
    chunk = (
        gathered.reshape(NY, tiles, rows, TP).transpose(0, 2, 1, 3).reshape(NY * rows, kcd)
    )

    up = [(i, (i + 1) % NZ) for i in range(NZ)]
    down = [(i, (i - 1) % NZ) for i in range(NZ)]

    def ladder_of(c):
        return jnp.dot(c, weighted, preferred_element_type=jnp.float32).astype(jnp.bfloat16)

    parts = [None] * NZ
    a = b = chunk
    for step in range(1, NZ // 2):
        na = lax.ppermute(a, "z", up)
        nb = lax.ppermute(b, "z", down)
        if step == 1:
            parts[0] = ladder_of(chunk)
        else:
            parts[NZ - step + 1] = ladder_of(a)
            parts[step - 1] = ladder_of(b)
        a, b = na, nb
    half = NY * rows // 2
    fa = lax.ppermute(a[:half], "z", up)
    fb = lax.ppermute(b[half:], "z", down)
    parts[NZ - NZ // 2 + 1] = ladder_of(a)
    parts[NZ // 2 - 1] = ladder_of(b)
    parts[NZ // 2] = jnp.concatenate([ladder_of(fa), ladder_of(fb)], 0)
    rel = jnp.stack([q.reshape(NY, rows, cols) for q in parts], 1)
    rel = jnp.roll(rel, z, axis=1)
    ladder = rel.reshape(NY * NZ * rows, cols)

    blocks = ladder.reshape(OCC, NP, OCC, cols)
    swapped = lax.all_to_all(blocks, PAIR, split_axis=1, concat_axis=1, tiled=True)
    result = blocks.astype(jnp.float32) - jnp.transpose(swapped, (2, 1, 0, 3)).astype(jnp.float32)
    return result.astype(jnp.bfloat16).reshape(NY * NZ * rows, cols)


def solution(mesh):
    fine = Mesh(mesh.devices.reshape(8, 2, 2, NY, NZ), AXES)
    placed = (P(AXES, None), P(None, VIRT), P(), P())
    return jax.shard_map(
        body, mesh=fine, in_specs=placed, out_specs=P(PAIR, VIRT), check_vma=False
    )
```

time: 270 us -> 162 us (0.60)
  the two profiles are of different devices: /device:TPU:2 before, /device:TPU:16 now
where the time goes in v1:
time: 162 us; the launch traced here: 161 us
  blocking collectives  81.6 us (50%)
  starting transfers between devices  33.3 us (21%)
  matrix products  16.5 us (10%)
  local copies, waits for them, and re-layouts  16.5 us (10%)
  waiting for transfers between devices  10.6 us (7%)
  other arithmetic  2.29 us (1%)
    all_to_all x1, blocking collectives, body(): lax.all_to_all(blocks, PAIR, split_axis=1, concat_axis=1, tiled=True)  57.3 us
    all_gather x1, blocking collectives, body(): gathered = lax.all_gather(packed, 'y', axis=0, tiled=False)  24.3 us
    ppermute x3, starting transfers between devices, body(): nb = lax.ppermute(b, 'z', down)  20.4 us
    dot_general x9, matrix products, ladder_of(): jnp.dot(c, weighted, preferred_element_type=jnp.float32)  15.6 us
    ppermute x3, waiting for transfers between devices, body(): na = lax.ppermute(a, 'z', up)  10.6 us
    unnamed x26, local copies, waits for them, and re-layouts  10.5 us
    ppermute x3, starting transfers between devices, body(): na = lax.ppermute(a, 'z', up)  5.74 us
    ppermute x1, starting transfers between devices, body(): fb = lax.ppermute(b[half:], 'z', down)  5.16 us
  transfers between devices with their start and end apart: 8, of which 3 were waited for; matrix products, arithmetic and copies ran while one was open for 11% of the time, Pallas kernels for 0%

profile of v1, /device:TPU:16, one launch (start us, length us, event | category | flops | bytes accessed | tf_op | source)
XLA Modules:
  0.0 161.2 jit_solution(17221193832586895860)
XLA Ops:
  1.3 1.0 mul.30
  2.4 24.3 %all-gather = bf16[288,1024]{1,0:T(8,128)(2,1)S(1)} all-gather(bf16[72,1024]{1,0:T(8,128)(2,1)S(1)} %pad_maximum_fusion), channel_id=2, replica_groups=mesh['x'=8,'yh'=2,'core'=2,'y'=4,'z'=8] {'y'}, dimensions={0}, use_global_device_ids=true | all-gather | bytes 737280 | tf_op jit(solution)/shard_map/all_gather | solution.py:32
  27.6 1.9 %collective-permute-start.3 = (bf16[144,2048]{1,0:T(8,128)(2,1)S(1)}, bf16[144,2048]{1,0:T(8,128)(2,1)}, u32[]{:S(2)}, u32[]{:S(2)}) collective-permute-start(bf16[144,2048]{1,0:T(8,128)(2,1)S(1)} %bitcast.32), channel_id=1, source_target_pairs={{0,1},{1,2},{2,3},{3,4},{4,5},{5,6},{6,7},{7,0},{8,9},{9,10},{10,1... | collective-permute-start | bytes 1769480 | tf_op jit(solution)/shard_map/ppermute | solution.py:46
  29.5 10.2 %collective-permute-start = (bf16[144,2048]{1,0:T(8,128)(2,1)S(1)}, bf16[144,2048]{1,0:T(8,128)(2,1)}, u32[]{:S(2)}, u32[]{:S(2)}) collective-permute-start(bf16[144,2048]{1,0:T(8,128)(2,1)S(1)} %bitcast.33), channel_id=1, source_target_pairs={{0,7},{1,0},{2,1},{3,2},{4,3},{5,4},{6,5},{7,6},{8,15},{9,8},{10,9... | collective-permute-start | bytes 1769480 | tf_op jit(solution)/shard_map/ppermute | solution.py:47
  41.3 6.1 %collective-permute-done.3 = bf16[144,2048]{1,0:T(8,128)(2,1)} collective-permute-done((bf16[144,2048]{1,0:T(8,128)(2,1)S(1)}, bf16[144,2048]{1,0:T(8,128)(2,1)}, u32[]{:S(2)}, u32[]{:S(2)}) %collective-permute-start.3) | collective-permute-done | bytes 589856 | tf_op jit(solution)/shard_map/ppermute | solution.py:46
  47.4 1.9 %collective-permute-start.4 = (bf16[144,2048]{1,0:T(8,128)(2,1)}, bf16[144,2048]{1,0:T(8,128)(2,1)}, u32[]{:S(2)}, u32[]{:S(2)}) collective-permute-start(bf16[144,2048]{1,0:T(8,128)(2,1)} %collective-permute-done.3), channel_id=1, source_target_pairs={{0,1},{1,2},{2,3},{3,4},{4,5},{5,6},{6,7},{7,0},{8,9},{9,10},{10,1... | collective-permute-start | bytes 1769480 | tf_op jit(solution)/shard_map/ppermute | solution.py:46
  49.3 5.1 %collective-permute-start.1 = (bf16[144,2048]{1,0:T(8,128)(2,1)}, bf16[144,2048]{1,0:T(8,128)(2,1)}, u32[]{:S(2)}, u32[]{:S(2)}) collective-permute-start(bf16[144,2048]{1,0:T(8,128)(2,1)} %collective-permute-done), channel_id=1, source_target_pairs={{0,7},{1,0},{2,1},{3,2},{4,3},{5,4},{6,5},{7,6},{8,15},{9,8},{10,9... | collective-permute-start | bytes 1769480 | tf_op jit(solution)/shard_map/ppermute | solution.py:47
  54.4 1.6 %convolution_convert_fusion = bf16[144,512]{1,0:T(8,128)(2,1)S(1)} fusion(bf16[144,2048]{1,0:T(8,128)(2,1)} %collective-permute-done.3, bf16[2048,512]{1,0:T(8,128)(2,1)S(1)} %copy-done.1, bf16[2048]{0:T(1024)(128)(2,1)S(1)} %bitcast.36), kind=kOutput, calls=%fused_computation.2 | convolution fusion | flops 303112192 | bytes 2838528 | tf_op jit(solution)/shard_map/dot_general | solution.py:41
  56.1 1.6 %convolution_convert_fusion.5 = bf16[144,512]{1,0:T(8,128)(2,1)S(1)} fusion(bf16[144,2048]{1,0:T(8,128)(2,1)} %collective-permute-done, bf16[2048,512]{1,0:T(8,128)(2,1)S(1)} %copy-done.1, bf16[2048]{0:T(1024)(128)(2,1)S(1)} %bitcast.37), kind=kOutput, calls=%fused_computation.7 | convolution fusion | flops 303112192 | bytes 2838528 | tf_op jit(solution)/shard_map/dot_general | solution.py:41
  58.5 2.9 %collective-permute-done.4 = bf16[144,2048]{1,0:T(8,128)(2,1)} collective-permute-done((bf16[144,2048]{1,0:T(8,128)(2,1)}, bf16[144,2048]{1,0:T(8,128)(2,1)}, u32[]{:S(2)}, u32[]{:S(2)}) %collective-permute-start.4) | collective-permute-done | bytes 589856 | tf_op jit(solution)/shard_map/ppermute | solution.py:46
  61.4 1.9 %collective-permute-start.5 = (bf16[144,2048]{1,0:T(8,128)(2,1)}, bf16[144,2048]{1,0:T(8,128)(2,1)S(1)}, u32[]{:S(2)}, u32[]{:S(2)}) collective-permute-start(bf16[144,2048]{1,0:T(8,128)(2,1)} %collective-permute-done.4), channel_id=1, source_target_pairs={{0,1},{1,2},{2,3},{3,4},{4,5},{5,6},{6,7},{7,0},{8,9},{9,10},{10,1... | collective-permute-start | bytes 1769480 | tf_op jit(solution)/shard_map/ppermute | solution.py:46
  63.3 5.1 %collective-permute-start.2 = (bf16[144,2048]{1,0:T(8,128)(2,1)}, bf16[144,2048]{1,0:T(8,128)(2,1)S(1)}, u32[]{:S(2)}, u32[]{:S(2)}) collective-permute-start(bf16[144,2048]{1,0:T(8,128)(2,1)} %collective-permute-done.1), channel_id=1, source_target_pairs={{0,7},{1,0},{2,1},{3,2},{4,3},{5,4},{6,5},{7,6},{8,15},{9,8},{10,9... | collective-permute-start | bytes 1769480 | tf_op jit(solution)/shard_map/ppermute | solution.py:47
  68.4 2.3 %convolution_convert_fusion.1 = bf16[144,512]{1,0:T(8,128)(2,1)S(1)} fusion(bf16[144,2048]{1,0:T(8,128)(2,1)} %collective-permute-done.4, bf16[2048,512]{1,0:T(8,128)(2,1)} %param.5, bf16[2048]{0:T(1024)(128)(2,1)S(1)} %bitcast.38), kind=kOutput, calls=%fused_computation.3 | convolution fusion | flops 303112192 | bytes 2838528 | tf_op jit(solution)/shard_map/dot_general | solution.py:41
  70.8 2.3 %convolution_convert_fusion.4 = bf16[144,512]{1,0:T(8,128)(2,1)S(1)} fusion(bf16[144,2048]{1,0:T(8,128)(2,1)} %collective-permute-done.1, bf16[2048,512]{1,0:T(8,128)(2,1)} %param.5, bf16[2048]{0:T(1024)(128)(2,1)S(1)} %bitcast.39), kind=kOutput, calls=%fused_computation.6 | convolution fusion | flops 303112192 | bytes 2838528 | tf_op jit(solution)/shard_map/dot_general | solution.py:41
  73.9 1.6 collective-permute-done.5
  75.5 1.9 %collective-permute-start.6 = (bf16[72,2048]{1,0:T(8,128)(2,1)S(1)}, bf16[72,2048]{1,0:T(8,128)(2,1)S(1)}, u32[]{:S(2)}, u32[]{:S(2)}) collective-permute-start(bf16[72,2048]{1,0:T(8,128)(2,1)S(1)} %slice.18), channel_id=1, source_target_pairs={{0,1},{1,2},{2,3},{3,4},{4,5},{5,6},{6,7},{7,0},{8,9},{9,10},{10,1... | collective-permute-start | bytes 884744 | tf_op jit(solution)/shard_map/ppermute | solution.py:55
  77.4 2.1 %convolution_convert_fusion.3 = bf16[144,512]{1,0:T(8,128)(2,1)S(1)} fusion(bf16[144,2048]{1,0:T(8,128)(2,1)S(1)} %collective-permute-done.2, bf16[2048,512]{1,0:T(8,128)(2,1)} %param.5, bf16[2048]{0:T(1024)(128)(2,1)S(1)} %bitcast.40), kind=kOutput, calls=%fused_computation.5 | convolution fusion | flops 303112192 | bytes 2838528 | tf_op jit(solution)/shard_map/dot_general | solution.py:41
  79.7 5.2 %collective-permute-start.7 = (bf16[72,2048]{1,0:T(8,128)(2,1)S(1)}, bf16[72,2048]{1,0:T(8,128)(2,1)S(1)}, u32[]{:S(2)}, u32[]{:S(2)}) collective-permute-start(bf16[72,2048]{1,0:T(8,128)(2,1)S(1)} %slice.19), channel_id=1, source_target_pairs={{0,7},{1,0},{2,1},{3,2},{4,3},{5,4},{6,5},{7,6},{8,15},{9,8},{10,9... | collective-permute-start | bytes 884744 | tf_op jit(solution)/shard_map/ppermute | solution.py:56
  84.8 2.2 %convolution_convert_fusion.2 = bf16[144,512]{1,0:T(8,128)(2,1)S(1)} fusion(bf16[144,2048]{1,0:T(8,128)(2,1)S(1)} %collective-permute-done.5, bf16[2048,512]{1,0:T(8,128)(2,1)} %param.5, bf16[2048]{0:T(1024)(128)(2,1)S(1)} %bitcast.41), kind=kOutput, calls=%fused_computation.4 | convolution fusion | flops 303112192 | bytes 2838528 | tf_op jit(solution)/shard_map/dot_general | solution.py:41
  87.7 2.3 %convolution_convert_fusion.8 = bf16[72,512]{1,0:T(8,128)(2,1)S(1)} fusion(bf16[72,2048]{1,0:T(8,128)(2,1)S(1)} %collective-permute-done.6, bf16[2048,512]{1,0:T(8,128)(2,1)} %param.5, bf16[2048]{0:T(1024)(128)(2,1)S(1)} %bitcast.42), kind=kOutput, calls=%fused_computation.10 | convolution fusion | flops 152080384 | bytes 2469888 | tf_op jit(solution)/shard_map/dot_general | solution.py:41
  98.7 1.4 constant_dynamic-slice_fusion
  100.9 57.3 %all_to_all.5 = bf16[6,32,6,512]{3,2,0,1:T(8,128)(2,1)S(1)} all-to-all(bf16[6,32,6,512]{3,2,0,1:T(8,128)(2,1)S(1)} %copy.21), channel_id=1, replica_groups=mesh['x'=8,'yh'=2,'core'=2,'y'=4,'z'=8] {'x','yh','core'}, dimensions={1} | all-to-all | bytes 2359296 | tf_op jit(solution)/shard_map/all_to_all | solution.py:65
  158.1 1.1 fusion
  159.9 1.2 reshape.42
  (58 shorter events, 16.1 us)
Async XLA Ops:
  2.4 37.4 %copy-start = (s32[2,16]{1,0:T(2,128)S(1)}, s32[2,16]{1,0:T(2,128)}, u32[]{:S(2)}) copy-start(s32[2,16]{1,0:T(2,128)} %param.7) | copy-start | bytes 388
  2.4 37.6 %copy-start.1 = (bf16[2048,512]{1,0:T(8,128)(2,1)S(1)}, bf16[2048,512]{1,0:T(8,128)(2,1)}, u32[]{:S(2)}) copy-start(bf16[2048,512]{1,0:T(8,128)(2,1)} %param.5) | copy-start | bytes 6291460
  27.6 19.8 %collective-permute-start.3 = (bf16[144,2048]{1,0:T(8,128)(2,1)S(1)}, bf16[144,2048]{1,0:T(8,128)(2,1)}, u32[]{:S(2)}, u32[]{:S(2)}) collective-permute-start(bf16[144,2048]{1,0:T(8,128)(2,1)S(1)} %bitcast.32), channel_id=1, source_target_pairs={{0,1},{1,2},{2,3},{3,4},{4,5},{5,6},{6,7},{7,0},{8,9},{9,10},{10,1... | collective-permute-start | bytes 1769480 | tf_op jit(solution)/shard_map/ppermute | solution.py:46
  29.5 19.8 %collective-permute-start = (bf16[144,2048]{1,0:T(8,128)(2,1)S(1)}, bf16[144,2048]{1,0:T(8,128)(2,1)}, u32[]{:S(2)}, u32[]{:S(2)}) collective-permute-start(bf16[144,2048]{1,0:T(8,128)(2,1)S(1)} %bitcast.33), channel_id=1, source_target_pairs={{0,7},{1,0},{2,1},{3,2},{4,3},{5,4},{6,5},{7,6},{8,15},{9,8},{10,9... | collective-permute-start | bytes 1769480 | tf_op jit(solution)/shard_map/ppermute | solution.py:47
  47.4 14.0 %collective-permute-start.4 = (bf16[144,2048]{1,0:T(8,128)(2,1)}, bf16[144,2048]{1,0:T(8,128)(2,1)}, u32[]{:S(2)}, u32[]{:S(2)}) collective-permute-start(bf16[144,2048]{1,0:T(8,128)(2,1)} %collective-permute-done.3), channel_id=1, source_target_pairs={{0,1},{1,2},{2,3},{3,4},{4,5},{5,6},{6,7},{7,0},{8,9},{9,10},{10,1... | collective-permute-start | bytes 1769480 | tf_op jit(solution)/shard_map/ppermute | solution.py:46
  49.3 14.0 %collective-permute-start.1 = (bf16[144,2048]{1,0:T(8,128)(2,1)}, bf16[144,2048]{1,0:T(8,128)(2,1)}, u32[]{:S(2)}, u32[]{:S(2)}) collective-permute-start(bf16[144,2048]{1,0:T(8,128)(2,1)} %collective-permute-done), channel_id=1, source_target_pairs={{0,7},{1,0},{2,1},{3,2},{4,3},{5,4},{6,5},{7,6},{8,15},{9,8},{10,9... | collective-permute-start | bytes 1769480 | tf_op jit(solution)/shard_map/ppermute | solution.py:47
  61.4 14.1 %collective-permute-start.5 = (bf16[144,2048]{1,0:T(8,128)(2,1)}, bf16[144,2048]{1,0:T(8,128)(2,1)S(1)}, u32[]{:S(2)}, u32[]{:S(2)}) collective-permute-start(bf16[144,2048]{1,0:T(8,128)(2,1)} %collective-permute-done.4), channel_id=1, source_target_pairs={{0,1},{1,2},{2,3},{3,4},{4,5},{5,6},{6,7},{7,0},{8,9},{9,10},{10,1... | collective-permute-start | bytes 1769480 | tf_op jit(solution)/shard_map/ppermute | solution.py:46
  63.3 14.1 %collective-permute-start.2 = (bf16[144,2048]{1,0:T(8,128)(2,1)}, bf16[144,2048]{1,0:T(8,128)(2,1)S(1)}, u32[]{:S(2)}, u32[]{:S(2)}) collective-permute-start(bf16[144,2048]{1,0:T(8,128)(2,1)} %collective-permute-done.1), channel_id=1, source_target_pairs={{0,7},{1,0},{2,1},{3,2},{4,3},{5,4},{6,5},{7,6},{8,15},{9,8},{10,9... | collective-permute-start | bytes 1769480 | tf_op jit(solution)/shard_map/ppermute | solution.py:47
  75.5 12.2 %collective-permute-start.6 = (bf16[72,2048]{1,0:T(8,128)(2,1)S(1)}, bf16[72,2048]{1,0:T(8,128)(2,1)S(1)}, u32[]{:S(2)}, u32[]{:S(2)}) collective-permute-start(bf16[72,2048]{1,0:T(8,128)(2,1)S(1)} %slice.18), channel_id=1, source_target_pairs={{0,1},{1,2},{2,3},{3,4},{4,5},{5,6},{6,7},{7,0},{8,9},{9,10},{10,1... | collective-permute-start | bytes 884744 | tf_op jit(solution)/shard_map/ppermute | solution.py:55
  79.7 10.3 %collective-permute-start.7 = (bf16[72,2048]{1,0:T(8,128)(2,1)S(1)}, bf16[72,2048]{1,0:T(8,128)(2,1)S(1)}, u32[]{:S(2)}, u32[]{:S(2)}) collective-permute-start(bf16[72,2048]{1,0:T(8,128)(2,1)S(1)} %slice.19), channel_id=1, source_target_pairs={{0,7},{1,0},{2,1},{3,2},{4,3},{5,4},{6,5},{7,6},{8,15},{9,8},{10,9... | collective-permute-start | bytes 884744 | tf_op jit(solution)/shard_map/ppermute | solution.py:56
  87.7 2.3 %copy-start.2 = (bf16[2048,512]{1,0:T(8,128)(2,1)S(1)}, bf16[2048,512]{1,0:T(8,128)(2,1)}, u32[]{:S(2)}) copy-start(bf16[2048,512]{1,0:T(8,128)(2,1)} %param.5) | copy-start | bytes 6291460

commit v2 on v1

v2 whole, which is shorter than its diff:
```python
import jax
import jax.numpy as jnp
import numpy as np
from jax import lax
from jax.sharding import Mesh, PartitionSpec as P

TP = 1024
OCC = 6
NY = 4
NZ = 8
NP = 32
AXES = ("x", "yh", "core", "y", "z")
PAIR = ("x", "yh", "core")
VIRT = ("y", "z")
HALF = OCC // 2
PER = OCC * HALF
PAD = 24
LANES = 128


def one_hot(width, spots):
    out = np.zeros((len(spots), width), np.float32)
    out[np.arange(len(spots)), spots] = 1.0
    return out


def slot(il, q, m):
    c = NP * il + q
    return PAD * (c // OCC) + (c % OCC) * HALF + m


def tables():
    send = np.zeros((NP * PAD, NP * PAD), np.float32)
    for q in range(NP):
        for il in range(OCC):
            for m in range(HALF):
                send[PAD * q + il * HALF + m, slot(il, q, m)] = 1.0
    order = [(il, q, m) for il in range(OCC) for q in range(NP) for m in range(HALF)]
    own = one_hot(NP * PAD, [slot(*o) for o in order])
    mirror = np.stack(
        [
            one_hot(
                NP * PAD,
                [PAD * q + (2 * m + (il + rh) % 2) * HALF + il // 2 for il, q, m in order],
            )
            for rh in range(2)
        ]
    )
    place = np.zeros((OCC, NP * OCC, 2 * NP * HALF), np.float32)
    for il in range(OCC):
        for q in range(NP):
            for jl in range(OCC):
                rh = (il + jl) % 2
                place[il, q * OCC + jl, rh * NP * HALF + q * HALF + jl // 2] = 1.0
    blocks = one_hot(NP, [q for _, q, _ in order])
    return send, own, mirror, place, blocks


SEND, OWN, MIRROR, PLACE, BLOCKS = tables()


def dot(a, b):
    return jnp.dot(a, b, preferred_element_type=jnp.float32)


def body(amplitudes, integrals, amp_pattern, int_pattern):
    rows, kcd = amplitudes.shape
    cols = integrals.shape[1]
    bf = jnp.bfloat16
    p = lax.axis_index(PAIR)
    v = lax.axis_index(VIRT)
    y = lax.axis_index("y")
    z = lax.axis_index("z")
    width = kcd // NZ

    n = jnp.arange(2 * PAD)
    rh, n = n // PAD, n % PAD
    k, m = n // HALF, n % HALF
    il = (OCC * v + k) // NP
    source = jnp.where(n < PER, k * OCC + 2 * m + (il + rh) % 2, -1)
    pick = (source[:, None] == jnp.arange(rows)[None, :]).astype(bf)
    split = dot(pick, amplitudes).astype(bf)
    first = (
        split.reshape(2, PAD, NZ, 2, LANES).transpose(0, 3, 2, 1, 4).reshape(NP, PAD, LANES)
    )
    held = lax.all_to_all(first, VIRT, split_axis=0, concat_axis=0, tiled=True)
    held = held.reshape(NP * PAD, LANES)

    second = dot(jnp.asarray(SEND, bf), held).astype(bf).reshape(NP, PAD, LANES)
    other = lax.all_to_all(second, PAIR, split_axis=0, concat_axis=0, tiled=True)
    other = other.reshape(NP * PAD, LANES)

    pattern = lax.dynamic_index_in_dim(
        amp_pattern, z * width // TP, 2, keepdims=False
    ).astype(jnp.float32)
    mine = lax.dynamic_index_in_dim(pattern, p, 0, keepdims=False)
    theirs = lax.dynamic_index_in_dim(pattern, p, 1, keepdims=False)
    masks = dot(jnp.asarray(BLOCKS, bf), jnp.stack([mine, theirs], 1).astype(bf))
    mirror = lax.dynamic_index_in_dim(jnp.asarray(MIRROR, bf), y // 2, 0, keepdims=False)
    diff = dot(jnp.asarray(OWN, bf), held) * masks[:, :1] - dot(mirror, other) * masks[:, 1:]
    diff = diff.astype(bf)

    gathered = lax.all_gather(diff, "y", axis=0, tiled=False)
    gathered = (
        gathered.reshape(2, 2, OCC, NP * HALF, LANES)
        .transpose(2, 0, 3, 1, 4)
        .reshape(OCC, NP * OCC, width)
    )
    chunk = (
        jnp.einsum(
            "bij,bjk->bik", jnp.asarray(PLACE, bf), gathered, preferred_element_type=jnp.float32
        )
        .astype(bf)
        .reshape(OCC * NP * OCC, width)
    )

    col_mask = lax.dynamic_index_in_dim(int_pattern, v * cols // TP, 1, keepdims=False)
    weighted = integrals * jnp.repeat(col_mask, TP).astype(bf)[:, None]

    def term(c, distance):
        start = lax.rem(z + distance, NZ) * width
        return dot(c, lax.dynamic_slice_in_dim(weighted, start, width, 0))

    up = [(i, (i + 1) % NZ) for i in range(NZ)]
    down = [(i, (i - 1) % NZ) for i in range(NZ)]
    total = None
    a = b = chunk
    for step in range(1, NZ // 2):
        na = lax.ppermute(a, "z", up)
        nb = lax.ppermute(b, "z", down)
        if step == 1:
            total = term(chunk, 0)
        else:
            total = total + term(a, NZ - step + 1) + term(b, step - 1)
        a, b = na, nb
    half = chunk.shape[0] // 2
    fa = lax.ppermute(a[:half], "z", up)
    fb = lax.ppermute(b[half:], "z", down)
    total = total + term(a, NZ - NZ // 2 + 1) + term(b, NZ // 2 - 1)
    low = total[:half] + term(fa, NZ // 2)
    high = total[half:] + term(fb, NZ // 2)
    return jnp.concatenate([low.astype(bf), high.astype(bf)], 0)


def solution(mesh):
    fine = Mesh(mesh.devices.reshape(8, 2, 2, NY, NZ), AXES)
    placed = (P(AXES, None), P(None, VIRT), P(), P())
    return jax.shard_map(
        body, mesh=fine, in_specs=placed, out_specs=P(PAIR, VIRT), check_vma=False
    )
```

time: 162 us -> 143 us (0.88)
  the two profiles are of different devices: /device:TPU:16 before, /device:TPU:2 now
where the time goes in v2:
time: 143 us
  starting transfers between devices  60 us (42%)
  waiting for transfers between devices  50.3 us (35%)
  blocking collectives  16.1 us (11%)
  matrix products  8.45 us (6%)
  local copies, waits for them, and re-layouts  4.22 us (3%)
  other arithmetic  3.19 us (2%)
    all_to_all x1, starting transfers between devices, body(): held = lax.all_to_all(first, VIRT, split_axis=0, concat_axis=0, tiled=True)  20.5 us
    all_gather x1, blocking collectives, body(): gathered = lax.all_gather(diff, 'y', axis=0, tiled=False)  16.1 us
    ppermute x3, starting transfers between devices, body(): nb = lax.ppermute(b, 'z', down)  14.9 us
    ppermute x3, waiting for transfers between devices, body(): nb = lax.ppermute(b, 'z', down)  14.1 us
    all_to_all x1, waiting for transfers between devices, body(): lax.all_to_all(second, PAIR, split_axis=0, concat_axis=0, tiled=True)  13.3 us
    ppermute x3, waiting for transfers between devices, body(): na = lax.ppermute(a, 'z', up)  10.9 us
    all_to_all x1, starting transfers between devices, body(): lax.all_to_all(second, PAIR, split_axis=0, concat_axis=0, tiled=True)  10.5 us
    all_to_all x1, waiting for transfers between devices, body(): held = lax.all_to_all(first, VIRT, split_axis=0, concat_axis=0, tiled=True)  9.11 us
  transfers between devices with their start and end apart: 10, of which 7 were waited for; matrix products, arithmetic and copies ran while one was open for 5% of the time, Pallas kernels for 0%

profile of v2, /device:TPU:2, one launch (start us, length us, event | category | flops | bytes accessed | tf_op | source)
XLA Modules:
  0.0 142.6 jit_solution(4602225148430402142)
XLA Ops:
  0.0 0.9 copy-done
  2.0 20.5 %all-to-all-start = ((bf16[32,24,128]{2,1,0:T(8,128)(2,1)}), bf16[32,24,128]{2,1,0:T(8,128)(2,1)S(1)}, u32[]{:S(2)}, u32[]{:S(2)}) async-start(bf16[32,24,128]{2,1,0:T(8,128)(2,1)} %bitcast.1), calls=%async_computation | async-start | bytes 393216 | tf_op jit(solution)/shard_map/all_to_all | solution.py:86
  22.6 0.9 fusion.42
  24.4 9.1 %all-to-all-done = bf16[32,24,128]{2,1,0:T(8,128)(2,1)S(1)} async-done(((bf16[32,24,128]{2,1,0:T(8,128)(2,1)}), bf16[32,24,128]{2,1,0:T(8,128)(2,1)S(1)}, u32[]{:S(2)}, u32[]{:S(2)}) %all-to-all-start) | async-done | bytes 196640 | tf_op jit(solution)/shard_map/all_to_all | solution.py:86
  33.5 1.8 %fusion.7 = bf16[768,128]{0,1:T(8,128)(2,1)S(1)} fusion(bf16[768,128]{1,0:T(8,128)(2,1)S(1)} %bitcast.53, bf16[768,768]{1,0:T(8,128)(2,1)} %constant.174.clone), kind=kOutput, calls=%fused_computation.19 | convolution fusion | flops 151093248 | bytes 1572864 | tf_op jit(solution)/shard_map/dot_general | solution.py:63
  35.3 0.8 copy.12
  36.1 10.5 %all-to-all-start.1 = ((bf16[32,24,128]{2,1,0:T(8,128)(2,1)}), bf16[32,24,128]{2,1,0:T(8,128)(2,1)S(1)}, u32[]{:S(2)}, u32[]{:S(2)}) async-start(bf16[32,24,128]{2,1,0:T(8,128)(2,1)} %bitcast.7), calls=%async_computation.1 | async-start | bytes 393216 | tf_op jit(solution)/shard_map/all_to_all | solution.py:90
  47.4 13.3 %all-to-all-done.1 = bf16[32,24,128]{2,1,0:T(8,128)(2,1)S(1)} async-done(((bf16[32,24,128]{2,1,0:T(8,128)(2,1)}), bf16[32,24,128]{2,1,0:T(8,128)(2,1)S(1)}, u32[]{:S(2)}, u32[]{:S(2)}) %all-to-all-start.1) | async-done | bytes 196640 | tf_op jit(solution)/shard_map/all_to_all | solution.py:90
  61.5 16.1 %all-gather = bf16[2304,128]{1,0:T(8,128)(2,1)S(1)} all-gather(bf16[576,128]{1,0:T(8,128)(2,1)S(1)} %fusion.6), channel_id=2, replica_groups=mesh['x'=8,'yh'=2,'core'=2,'y'=4,'z'=8] {'y'}, dimensions={0}, use_global_device_ids=true | all-gather | bytes 737280 | tf_op jit(solution)/shard_map/all_gather | solution.py:103
  78.6 1.4 convolution_convert_fusion.1
  80.0 3.2 %collective-permute-start = (bf16[1152,256]{1,0:T(8,128)(2,1)S(1)}, bf16[1152,256]{1,0:T(8,128)(2,1)S(1)}, u32[]{:S(2)}, u32[]{:S(2)}) collective-permute-start(bf16[1152,256]{1,0:T(8,128)(2,1)S(1)} %bitcast.49), channel_id=1, source_target_pairs={{0,1},{1,2},{2,3},{3,4},{4,5},{5,6},{6,7},{7,0},{8,9},{9,10},{10,1... | collective-permute-start | bytes 1769480 | tf_op jit(solution)/shard_map/ppermute | solution.py:129
  83.2 3.8 %collective-permute-start.1 = (bf16[1152,256]{1,0:T(8,128)(2,1)S(1)}, bf16[1152,256]{1,0:T(8,128)(2,1)S(1)}, u32[]{:S(2)}, u32[]{:S(2)}) collective-permute-start(bf16[1152,256]{1,0:T(8,128)(2,1)S(1)} %bitcast.50), channel_id=1, source_target_pairs={{0,7},{1,0},{2,1},{3,2},{4,3},{5,4},{6,5},{7,6},{8,15},{9,8},{10,9... | collective-permute-start | bytes 1769480 | tf_op jit(solution)/shard_map/ppermute | solution.py:130
  87.9 8.6 %collective-permute-done.1 = bf16[1152,256]{1,0:T(8,128)(2,1)S(1)} collective-permute-done((bf16[1152,256]{1,0:T(8,128)(2,1)S(1)}, bf16[1152,256]{1,0:T(8,128)(2,1)S(1)}, u32[]{:S(2)}, u32[]{:S(2)}) %collective-permute-start.1) | collective-permute-done | bytes 589856 | tf_op jit(solution)/shard_map/ppermute | solution.py:130
  96.5 5.5 %collective-permute-start.3 = (bf16[1152,256]{1,0:T(8,128)(2,1)S(1)}, bf16[1152,256]{1,0:T(8,128)(2,1)S(1)}, u32[]{:S(2)}, u32[]{:S(2)}) collective-permute-start(bf16[1152,256]{1,0:T(8,128)(2,1)S(1)} %collective-permute-done.1), channel_id=1, source_target_pairs={{0,7},{1,0},{2,1},{3,2},{4,3},{5,4},{6,5},{7,6},{8,15},{9,8},{10,9... | collective-permute-start | bytes 1769480 | tf_op jit(solution)/shard_map/ppermute | solution.py:130
  102.0 1.9 %collective-permute-start.2 = (bf16[1152,256]{1,0:T(8,128)(2,1)S(1)}, bf16[1152,256]{1,0:T(8,128)(2,1)S(1)}, u32[]{:S(2)}, u32[]{:S(2)}) collective-permute-start(bf16[1152,256]{1,0:T(8,128)(2,1)S(1)} %collective-permute-done), channel_id=1, source_target_pairs={{0,1},{1,2},{2,3},{3,4},{4,5},{5,6},{6,7},{7,0},{8,9},{9,10},{10,1... | collective-permute-start | bytes 1769480 | tf_op jit(solution)/shard_map/ppermute | solution.py:129
  104.9 5.5 %collective-permute-done.3 = bf16[1152,256]{1,0:T(8,128)(2,1)S(1)} collective-permute-done((bf16[1152,256]{1,0:T(8,128)(2,1)S(1)}, bf16[1152,256]{1,0:T(8,128)(2,1)S(1)}, u32[]{:S(2)}, u32[]{:S(2)}) %collective-permute-start.3) | collective-permute-done | bytes 589856 | tf_op jit(solution)/shard_map/ppermute | solution.py:130
  110.4 5.6 %collective-permute-start.5 = (bf16[1152,256]{1,0:T(8,128)(2,1)S(1)}, bf16[1152,256]{1,0:T(8,128)(2,1)S(1)}, u32[]{:S(2)}, u32[]{:S(2)}) collective-permute-start(bf16[1152,256]{1,0:T(8,128)(2,1)S(1)} %collective-permute-done.3), channel_id=1, source_target_pairs={{0,7},{1,0},{2,1},{3,2},{4,3},{5,4},{6,5},{7,6},{8,15},{9,8},{10,9... | collective-permute-start | bytes 1769480 | tf_op jit(solution)/shard_map/ppermute | solution.py:130
  116.0 1.9 %collective-permute-start.4 = (bf16[1152,256]{1,0:T(8,128)(2,1)S(1)}, bf16[1152,256]{1,0:T(8,128)(2,1)S(1)}, u32[]{:S(2)}, u32[]{:S(2)}) collective-permute-start(bf16[1152,256]{1,0:T(8,128)(2,1)S(1)} %collective-permute-done.2), channel_id=1, source_target_pairs={{0,1},{1,2},{2,3},{3,4},{4,5},{5,6},{6,7},{7,0},{8,9},{9,10},{10,1... | collective-permute-start | bytes 1769480 | tf_op jit(solution)/shard_map/ppermute | solution.py:129
  119.0 10.9 %collective-permute-done.4 = bf16[1152,256]{1,0:T(8,128)(2,1)S(1)} collective-permute-done((bf16[1152,256]{1,0:T(8,128)(2,1)S(1)}, bf16[1152,256]{1,0:T(8,128)(2,1)S(1)}, u32[]{:S(2)}, u32[]{:S(2)}) %collective-permute-start.4) | collective-permute-done | bytes 589856 | tf_op jit(solution)/shard_map/ppermute | solution.py:129
  129.9 1.9 %collective-permute-start.6 = (bf16[576,256]{1,0:T(8,128)(2,1)S(1)}, bf16[576,256]{1,0:T(8,128)(2,1)S(1)}, u32[]{:S(2)}, u32[]{:S(2)}) collective-permute-start(bf16[576,256]{1,0:T(8,128)(2,1)S(1)} %slice.27), channel_id=1, source_target_pairs={{0,1},{1,2},{2,3},{3,4},{4,5},{5,6},{6,7},{7,0},{8,9},{9,10},{10,1... | collective-permute-start | bytes 884744 | tf_op jit(solution)/shard_map/ppermute | solution.py:137
  131.9 5.1 %collective-permute-start.7 = (bf16[576,256]{1,0:T(8,128)(2,1)S(1)}, bf16[576,256]{1,0:T(8,128)(2,1)S(1)}, u32[]{:S(2)}, u32[]{:S(2)}) collective-permute-start(bf16[576,256]{1,0:T(8,128)(2,1)S(1)} %slice.29), channel_id=1, source_target_pairs={{0,7},{1,0},{2,1},{3,2},{4,3},{5,4},{6,5},{7,6},{8,15},{9,8},{10,9... | collective-permute-start | bytes 884744 | tf_op jit(solution)/shard_map/ppermute | solution.py:138
  138.0 1.7 %collective-permute-done.6 = bf16[576,256]{1,0:T(8,128)(2,1)S(1)} collective-permute-done((bf16[576,256]{1,0:T(8,128)(2,1)S(1)}, bf16[576,256]{1,0:T(8,128)(2,1)S(1)}, u32[]{:S(2)}, u32[]{:S(2)}) %collective-permute-start.6) | collective-permute-done | bytes 294944 | tf_op jit(solution)/shard_map/ppermute | solution.py:137
  140.0 1.2 collective-permute-done.7
  141.5 1.1 pad_maximum_fusion
  (39 shorter events, 9.0 us)
Async XLA Ops:
  0.0 0.9 copy-start
  0.9 46.3 %copy-start.4 = (bf16[576,32]{1,0:T(8,128)(2,1)S(1)}, bf16[576,32]{1,0:T(8,128)(2,1)}, u32[]{:S(2)}) copy-start(bf16[576,32]{1,0:T(8,128)(2,1)} %constant.175.clone) | copy-start | bytes 110596
  1.2 59.5 %copy-start.3 = (bf16[2,576,768]{2,1,0:T(8,128)(2,1)S(1)}, bf16[2,576,768]{2,1,0:T(8,128)(2,1)}, u32[]{:S(2)}) copy-start(bf16[2,576,768]{2,1,0:T(8,128)(2,1)} %constant.176.clone) | copy-start | bytes 5308420
  2.0 31.4 %all-to-all-start = ((bf16[32,24,128]{2,1,0:T(8,128)(2,1)}), bf16[32,24,128]{2,1,0:T(8,128)(2,1)S(1)}, u32[]{:S(2)}, u32[]{:S(2)}) async-start(bf16[32,24,128]{2,1,0:T(8,128)(2,1)} %bitcast.1), calls=%async_computation | async-start | bytes 393216 | tf_op jit(solution)/shard_map/all_to_all | solution.py:86
  22.5 38.6 %copy-start.2 = (bf16[576,768]{1,0:T(8,128)(2,1)S(1)}, bf16[576,768]{1,0:T(8,128)(2,1)}, u32[]{:S(2)}) copy-start(bf16[576,768]{1,0:T(8,128)(2,1)} %constant.177.clone) | copy-start | bytes 2654212
  36.1 24.6 %all-to-all-start.1 = ((bf16[32,24,128]{2,1,0:T(8,128)(2,1)}), bf16[32,24,128]{2,1,0:T(8,128)(2,1)S(1)}, u32[]{:S(2)}, u32[]{:S(2)}) async-start(bf16[32,24,128]{2,1,0:T(8,128)(2,1)} %bitcast.7), calls=%async_computation.1 | async-start | bytes 393216 | tf_op jit(solution)/shard_map/all_to_all | solution.py:90
  77.6 9.4 %copy-start.1 = (bf16[2048,512]{1,0:T(8,128)(2,1)S(1)}, bf16[2048,512]{1,0:T(8,128)(2,1)}, u32[]{:S(2)}) copy-start(bf16[2048,512]{1,0:T(8,128)(2,1)} %param.10) | copy-start | bytes 6291460
  80.0 22.0 %collective-permute-start = (bf16[1152,256]{1,0:T(8,128)(2,1)S(1)}, bf16[1152,256]{1,0:T(8,128)(2,1)S(1)}, u32[]{:S(2)}, u32[]{:S(2)}) collective-permute-start(bf16[1152,256]{1,0:T(8,128)(2,1)S(1)} %bitcast.49), channel_id=1, source_target_pairs={{0,1},{1,2},{2,3},{3,4},{4,5},{5,6},{6,7},{7,0},{8,9},{9,10},{10,1... | collective-permute-start | bytes 1769480 | tf_op jit(solution)/shard_map/ppermute | solution.py:129
  83.2 13.2 %collective-permute-start.1 = (bf16[1152,256]{1,0:T(8,128)(2,1)S(1)}, bf16[1152,256]{1,0:T(8,128)(2,1)S(1)}, u32[]{:S(2)}, u32[]{:S(2)}) collective-permute-start(bf16[1152,256]{1,0:T(8,128)(2,1)S(1)} %bitcast.50), channel_id=1, source_target_pairs={{0,7},{1,0},{2,1},{3,2},{4,3},{5,4},{6,5},{7,6},{8,15},{9,8},{10,9... | collective-permute-start | bytes 1769480 | tf_op jit(solution)/shard_map/ppermute | solution.py:130
  96.5 14.0 %collective-permute-start.3 = (bf16[1152,256]{1,0:T(8,128)(2,1)S(1)}, bf16[1152,256]{1,0:T(8,128)(2,1)S(1)}, u32[]{:S(2)}, u32[]{:S(2)}) collective-permute-start(bf16[1152,256]{1,0:T(8,128)(2,1)S(1)} %collective-permute-done.1), channel_id=1, source_target_pairs={{0,7},{1,0},{2,1},{3,2},{4,3},{5,4},{6,5},{7,6},{8,15},{9,8},{10,9... | collective-permute-start | bytes 1769480 | tf_op jit(solution)/shard_map/ppermute | solution.py:130
  102.0 14.0 %collective-permute-start.2 = (bf16[1152,256]{1,0:T(8,128)(2,1)S(1)}, bf16[1152,256]{1,0:T(8,128)(2,1)S(1)}, u32[]{:S(2)}, u32[]{:S(2)}) collective-permute-start(bf16[1152,256]{1,0:T(8,128)(2,1)S(1)} %collective-permute-done), channel_id=1, source_target_pairs={{0,1},{1,2},{2,3},{3,4},{4,5},{5,6},{6,7},{7,0},{8,9},{9,10},{10,1... | collective-permute-start | bytes 1769480 | tf_op jit(solution)/shard_map/ppermute | solution.py:129
  110.4 21.4 %collective-permute-start.5 = (bf16[1152,256]{1,0:T(8,128)(2,1)S(1)}, bf16[1152,256]{1,0:T(8,128)(2,1)S(1)}, u32[]{:S(2)}, u32[]{:S(2)}) collective-permute-start(bf16[1152,256]{1,0:T(8,128)(2,1)S(1)} %collective-permute-done.3), channel_id=1, source_target_pairs={{0,7},{1,0},{2,1},{3,2},{4,3},{5,4},{6,5},{7,6},{8,15},{9,8},{10,9... | collective-permute-start | bytes 1769480 | tf_op jit(solution)/shard_map/ppermute | solution.py:130
  116.0 13.9 %collective-permute-start.4 = (bf16[1152,256]{1,0:T(8,128)(2,1)S(1)}, bf16[1152,256]{1,0:T(8,128)(2,1)S(1)}, u32[]{:S(2)}, u32[]{:S(2)}) collective-permute-start(bf16[1152,256]{1,0:T(8,128)(2,1)S(1)} %collective-permute-done.2), channel_id=1, source_target_pairs={{0,1},{1,2},{2,3},{3,4},{4,5},{5,6},{6,7},{7,0},{8,9},{9,10},{10,1... | collective-permute-start | bytes 1769480 | tf_op jit(solution)/shard_map/ppermute | solution.py:129
  129.9 9.8 %collective-permute-start.6 = (bf16[576,256]{1,0:T(8,128)(2,1)S(1)}, bf16[576,256]{1,0:T(8,128)(2,1)S(1)}, u32[]{:S(2)}, u32[]{:S(2)}) collective-permute-start(bf16[576,256]{1,0:T(8,128)(2,1)S(1)} %slice.27), channel_id=1, source_target_pairs={{0,1},{1,2},{2,3},{3,4},{4,5},{5,6},{6,7},{7,0},{8,9},{9,10},{10,1... | collective-permute-start | bytes 884744 | tf_op jit(solution)/shard_map/ppermute | solution.py:137
  131.9 9.4 %collective-permute-start.7 = (bf16[576,256]{1,0:T(8,128)(2,1)S(1)}, bf16[576,256]{1,0:T(8,128)(2,1)S(1)}, u32[]{:S(2)}, u32[]{:S(2)}) collective-permute-start(bf16[576,256]{1,0:T(8,128)(2,1)S(1)} %slice.29), channel_id=1, source_target_pairs={{0,7},{1,0},{2,1},{3,2},{4,3},{5,4},{6,5},{7,6},{8,15},{9,8},{10,9... | collective-permute-start | bytes 884744 | tf_op jit(solution)/shard_map/ppermute | solution.py:138

commit v3 on v2

--- a/solution.py
+++ b/solution.py
@@ -46,12 +46,13 @@
             for rh in range(2)
         ]
     )
-    place = np.zeros((OCC, NP * OCC, 2 * NP * HALF), np.float32)
-    for il in range(OCC):
-        for q in range(NP):
-            for jl in range(OCC):
-                rh = (il + jl) % 2
-                place[il, q * OCC + jl, rh * NP * HALF + q * HALF + jl // 2] = 1.0
+    place = np.zeros((2, OCC, NP * OCC, 2 * NP * HALF), np.float32)
+    for rh in range(2):
+        for il in range(OCC):
+            for q in range(NP):
+                for jl in range(OCC):
+                    part = (il + jl + rh) % 2
+                    place[rh, il, q * OCC + jl, part * NP * HALF + q * HALF + jl // 2] = 1.0
     blocks = one_hot(NP, [q for _, q, _ in order])
     return send, own, mirror, place, blocks
 
@@ -100,46 +101,47 @@
     diff = dot(jnp.asarray(OWN, bf), held) * masks[:, :1] - dot(mirror, other) * masks[:, 1:]
     diff = diff.astype(bf)
 
-    gathered = lax.all_gather(diff, "y", axis=0, tiled=False)
-    gathered = (
-        gathered.reshape(2, 2, OCC, NP * HALF, LANES)
-        .transpose(2, 0, 3, 1, 4)
-        .reshape(OCC, NP * OCC, width)
-    )
-    chunk = (
-        jnp.einsum(
-            "bij,bjk->bik", jnp.asarray(PLACE, bf), gathered, preferred_element_type=jnp.float32
-        )
-        .astype(bf)
-        .reshape(OCC * NP * OCC, width)
-    )
-
     col_mask = lax.dynamic_index_in_dim(int_pattern, v * cols // TP, 1, keepdims=False)
     weighted = integrals * jnp.repeat(col_mask, TP).astype(bf)[:, None]
+    weighted = weighted.reshape(NZ, 2, LANES, cols)
+    weighted = jnp.where(y % 2 == 0, weighted, weighted[:, ::-1]).reshape(kcd, cols)
+    core = lax.axis_index("core")
+    sign = 1 - 2 * core
 
     def term(c, distance):
-        start = lax.rem(z + distance, NZ) * width
+        start = lax.rem(z + sign * distance + NZ, NZ) * width
         return dot(c, lax.dynamic_slice_in_dim(weighted, start, width, 0))
 
-    up = [(i, (i + 1) % NZ) for i in range(NZ)]
-    down = [(i, (i - 1) % NZ) for i in range(NZ)]
-    total = None
-    a = b = chunk
-    for step in range(1, NZ // 2):
-        na = lax.ppermute(a, "z", up)
-        nb = lax.ppermute(b, "z", down)
-        if step == 1:
-            total = term(chunk, 0)
-        else:
-            total = total + term(a, NZ - step + 1) + term(b, step - 1)
-        a, b = na, nb
-    half = chunk.shape[0] // 2
-    fa = lax.ppermute(a[:half], "z", up)
-    fb = lax.ppermute(b[half:], "z", down)
-    total = total + term(a, NZ - NZ // 2 + 1) + term(b, NZ // 2 - 1)
-    low = total[:half] + term(fa, NZ // 2)
-    high = total[half:] + term(fb, NZ // 2)
-    return jnp.concatenate([low.astype(bf), high.astype(bf)], 0)
+    near = lax.ppermute(diff, "y", [(i, i ^ 1) for i in range(NY)])
+    piece = jnp.concatenate([diff, near], 1)
+    pieces = [piece, lax.ppermute(piece, "y", [(i, i ^ 2) for i in range(NY)])]
+
+    def shift(step):
+        return [
+            (c * NZ + i, c * NZ + (i + (1 - 2 * c) * step) % NZ)
+            for c in range(2)
+            for i in range(NZ)
+        ]
+
+    ways = (shift(1), shift(-1))
+    front = [list(pieces), list(pieces)]
+    totals = [None, None]
+    for step in range(1, NZ // 2 + 1):
+        for i in range(2):
+            last = step == NZ // 2
+            if totals[i] is None:
+                totals[i] = term(pieces[i], 0)
+            for w in range(2):
+                if last and w != i:
+                    continue
+                front[w][i] = lax.ppermute(front[w][i], ("core", "z"), ways[w])
+                totals[i] = totals[i] + term(front[w][i], -step if w == 0 else step)
+    both = jnp.concatenate(
+        [t.astype(bf).reshape(OCC, NP * HALF, cols) for t in totals], 1
+    )
+    place = lax.dynamic_index_in_dim(jnp.asarray(PLACE, bf), y // 2, 0, keepdims=False)
+    out = jnp.einsum("bij,bjk->bik", place, both, preferred_element_type=jnp.float32)
+    return out.astype(bf).reshape(OCC * NP * OCC, cols)
 
 
 def solution(mesh):

time: 143 us -> 150 us (1.049)
  the two profiles are of different devices: /device:TPU:2 before, /device:TPU:4 now
where the time goes in v3:
time: 150 us; the launch traced here: 149 us
  starting transfers between devices  83.6 us (56%)
  waiting for transfers between devices  51.5 us (34%)
  matrix products  9.16 us (6%)
  local copies, waits for them, and re-layouts  3.18 us (2%)
    ppermute x14, starting transfers between devices, body(): front[w][i] = lax.ppermute(front[w][i], ('core', 'z'), ways[w])  47.4 us
    all_to_all x1, starting transfers between devices, body(): held = lax.all_to_all(first, VIRT, split_axis=0, concat_axis=0, tiled=True)  20.4 us
    ppermute x14, waiting for transfers between devices, body(): front[w][i] = lax.ppermute(front[w][i], ('core', 'z'), ways[w])  12.6 us
    ppermute x1, waiting for transfers between devices, body(): pieces = [piece, lax.ppermute(piece, 'y', [(i, i ^ 2) for i in range(NY)])]  12 us
    all_to_all x1, waiting for transfers between devices, body(): lax.all_to_all(second, PAIR, split_axis=0, concat_axis=0, tiled=True)  11.7 us
    all_to_all x1, waiting for transfers between devices, body(): held = lax.all_to_all(first, VIRT, split_axis=0, concat_axis=0, tiled=True)  10.6 us
    all_to_all x1, starting transfers between devices, body(): lax.all_to_all(second, PAIR, split_axis=0, concat_axis=0, tiled=True)  10.4 us
    dot_general x21, matrix products, dot(): return jnp.dot(a, b, preferred_element_type=jnp.float32)  7.69 us
  transfers between devices with their start and end apart: 18, of which 8 were waited for; matrix products, arithmetic and copies ran while one was open for 5% of the time, Pallas kernels for 0%

profile of v3, /device:TPU:4, one launch (start us, length us, event | category | flops | bytes accessed | tf_op | source)
XLA Modules:
  0.0 149.1 jit_solution(1811126595993076944)
XLA Ops:
  2.0 20.4 %all-to-all-start = ((bf16[32,24,128]{2,1,0:T(8,128)(2,1)}), bf16[32,24,128]{2,1,0:T(8,128)(2,1)S(1)}, u32[]{:S(2)}, u32[]{:S(2)}) async-start(bf16[32,24,128]{2,1,0:T(8,128)(2,1)} %bitcast.2), calls=%async_computation | async-start | bytes 393216 | tf_op jit(solution)/shard_map/all_to_all | solution.py:87
  22.8 10.6 %all-to-all-done = bf16[32,24,128]{2,1,0:T(8,128)(2,1)S(1)} async-done(((bf16[32,24,128]{2,1,0:T(8,128)(2,1)}), bf16[32,24,128]{2,1,0:T(8,128)(2,1)S(1)}, u32[]{:S(2)}, u32[]{:S(2)}) %all-to-all-start) | async-done | bytes 196640 | tf_op jit(solution)/shard_map/all_to_all | solution.py:87
  34.8 10.4 %all-to-all-start.1 = ((bf16[32,24,128]{2,1,0:T(8,128)(2,1)}), bf16[32,24,128]{2,1,0:T(8,128)(2,1)S(1)}, u32[]{:S(2)}, u32[]{:S(2)}) async-start(bf16[32,24,128]{2,1,0:T(8,128)(2,1)} %bitcast.8), calls=%async_computation.1 | async-start | bytes 393216 | tf_op jit(solution)/shard_map/all_to_all | solution.py:91
  46.9 11.7 %all-to-all-done.1 = bf16[32,24,128]{2,1,0:T(8,128)(2,1)S(1)} async-done(((bf16[32,24,128]{2,1,0:T(8,128)(2,1)}), bf16[32,24,128]{2,1,0:T(8,128)(2,1)S(1)}, u32[]{:S(2)}, u32[]{:S(2)}) %all-to-all-start.1) | async-done | bytes 196640 | tf_op jit(solution)/shard_map/all_to_all | solution.py:91
  59.4 2.5 %collective-permute-start = (bf16[576,128]{1,0:T(8,128)(2,1)S(1)}, bf16[576,128]{1,0:T(8,128)(2,1)S(1)}, u32[]{:S(2)}, u32[]{:S(2)}) collective-permute-start(bf16[576,128]{1,0:T(8,128)(2,1)S(1)} %fusion.12), channel_id=1, source_target_pairs={{0,8},{8,0},{16,24},{24,16},{1,9},{9,1},{17,25},{25,17},{2,10},{10... | collective-permute-start | bytes 442376 | tf_op jit(solution)/shard_map/ppermute | solution.py:115
  62.4 4.6 %collective-permute-done = bf16[576,128]{1,0:T(8,128)(2,1)S(1)} collective-permute-done((bf16[576,128]{1,0:T(8,128)(2,1)S(1)}, bf16[576,128]{1,0:T(8,128)(2,1)S(1)}, u32[]{:S(2)}, u32[]{:S(2)}) %collective-permute-start) | collective-permute-done | bytes 147488 | tf_op jit(solution)/shard_map/ppermute | solution.py:115
  67.0 3.1 %collective-permute-start.1 = (bf16[576,256]{1,0:T(8,128)(2,1)S(1)}, bf16[576,256]{1,0:T(8,128)(2,1)S(1)}, u32[]{:S(2)}, u32[]{:S(2)}) collective-permute-start(bf16[576,256]{1,0:T(8,128)(2,1)S(1)} %pad_maximum_fusion), channel_id=1, source_target_pairs={{0,1},{1,2},{2,3},{3,4},{4,5},{5,6},{6,7},{7,0},{32,39},{33,32},{3... | collective-permute-start | bytes 884744 | tf_op jit(solution)/shard_map/ppermute | solution.py:137
  70.2 3.9 %collective-permute-start.2 = (bf16[576,256]{1,0:T(8,128)(2,1)S(1)}, bf16[576,256]{1,0:T(8,128)(2,1)S(1)}, u32[]{:S(2)}, u32[]{:S(2)}) collective-permute-start(bf16[576,256]{1,0:T(8,128)(2,1)S(1)} %pad_maximum_fusion), channel_id=1, source_target_pairs={{0,7},{1,0},{2,1},{3,2},{4,3},{5,4},{6,5},{7,6},{32,33},{33,34},{3... | collective-permute-start | bytes 884744 | tf_op jit(solution)/shard_map/ppermute | solution.py:137
  74.1 2.8 %collective-permute-start.8 = (bf16[576,256]{1,0:T(8,128)(2,1)S(1)}, bf16[576,256]{1,0:T(8,128)(2,1)S(1)}, u32[]{:S(2)}, u32[]{:S(2)}) collective-permute-start(bf16[576,256]{1,0:T(8,128)(2,1)S(1)} %pad_maximum_fusion), channel_id=1, source_target_pairs={{0,16},{8,24},{16,0},{24,8},{1,17},{9,25},{17,1},{25,9},{2,18},{10... | collective-permute-start | bytes 884744 | tf_op jit(solution)/shard_map/ppermute | solution.py:117
  77.4 12.0 %collective-permute-done.8 = bf16[576,256]{1,0:T(8,128)(2,1)S(1)} collective-permute-done((bf16[576,256]{1,0:T(8,128)(2,1)S(1)}, bf16[576,256]{1,0:T(8,128)(2,1)S(1)}, u32[]{:S(2)}, u32[]{:S(2)}) %collective-permute-start.8) | collective-permute-done | bytes 294944 | tf_op jit(solution)/shard_map/ppermute | solution.py:117
  89.4 3.1 %collective-permute-start.9 = (bf16[576,256]{1,0:T(8,128)(2,1)S(1)}, bf16[576,256]{1,0:T(8,128)(2,1)S(1)}, u32[]{:S(2)}, u32[]{:S(2)}) collective-permute-start(bf16[576,256]{1,0:T(8,128)(2,1)S(1)} %collective-permute-done.8), channel_id=1, source_target_pairs={{0,1},{1,2},{2,3},{3,4},{4,5},{5,6},{6,7},{7,0},{32,39},{33,32},{3... | collective-permute-start | bytes 884744 | tf_op jit(solution)/shard_map/ppermute | solution.py:137
  92.5 3.9 %collective-permute-start.10 = (bf16[576,256]{1,0:T(8,128)(2,1)S(1)}, bf16[576,256]{1,0:T(8,128)(2,1)S(1)}, u32[]{:S(2)}, u32[]{:S(2)}) collective-permute-start(bf16[576,256]{1,0:T(8,128)(2,1)S(1)} %collective-permute-done.8), channel_id=1, source_target_pairs={{0,7},{1,0},{2,1},{3,2},{4,3},{5,4},{6,5},{7,6},{32,33},{33,34},{3... | collective-permute-start | bytes 884744 | tf_op jit(solution)/shard_map/ppermute | solution.py:137
  96.5 2.6 %collective-permute-start.4 = (bf16[576,256]{1,0:T(8,128)(2,1)S(1)}, bf16[576,256]{1,0:T(8,128)(2,1)S(1)}, u32[]{:S(2)}, u32[]{:S(2)}) collective-permute-start(bf16[576,256]{1,0:T(8,128)(2,1)S(1)} %collective-permute-done.2), channel_id=1, source_target_pairs={{0,7},{1,0},{2,1},{3,2},{4,3},{5,4},{6,5},{7,6},{32,33},{33,34},{3... | collective-permute-start | bytes 884744 | tf_op jit(solution)/shard_map/ppermute | solution.py:137
  99.1 3.3 %collective-permute-start.3 = (bf16[576,256]{1,0:T(8,128)(2,1)S(1)}, bf16[576,256]{1,0:T(8,128)(2,1)S(1)}, u32[]{:S(2)}, u32[]{:S(2)}) collective-permute-start(bf16[576,256]{1,0:T(8,128)(2,1)S(1)} %collective-permute-done.1), channel_id=1, source_target_pairs={{0,1},{1,2},{2,3},{3,4},{4,5},{5,6},{6,7},{7,0},{32,39},{33,32},{3... | collective-permute-start | bytes 884744 | tf_op jit(solution)/shard_map/ppermute | solution.py:137
  103.6 4.4 %collective-permute-done.4 = bf16[576,256]{1,0:T(8,128)(2,1)S(1)} collective-permute-done((bf16[576,256]{1,0:T(8,128)(2,1)S(1)}, bf16[576,256]{1,0:T(8,128)(2,1)S(1)}, u32[]{:S(2)}, u32[]{:S(2)}) %collective-permute-start.4) | collective-permute-done | bytes 294944 | tf_op jit(solution)/shard_map/ppermute | solution.py:137
  108.1 3.5 %collective-permute-start.6 = (bf16[576,256]{1,0:T(8,128)(2,1)S(1)}, bf16[576,256]{1,0:T(8,128)(2,1)S(1)}, u32[]{:S(2)}, u32[]{:S(2)}) collective-permute-start(bf16[576,256]{1,0:T(8,128)(2,1)S(1)} %collective-permute-done.4), channel_id=1, source_target_pairs={{0,7},{1,0},{2,1},{3,2},{4,3},{5,4},{6,5},{7,6},{32,33},{33,34},{3... | collective-permute-start | bytes 884744 | tf_op jit(solution)/shard_map/ppermute | solution.py:137
  111.6 2.3 %collective-permute-start.5 = (bf16[576,256]{1,0:T(8,128)(2,1)S(1)}, bf16[576,256]{1,0:T(8,128)(2,1)S(1)}, u32[]{:S(2)}, u32[]{:S(2)}) collective-permute-start(bf16[576,256]{1,0:T(8,128)(2,1)S(1)} %collective-permute-done.3), channel_id=1, source_target_pairs={{0,1},{1,2},{2,3},{3,4},{4,5},{5,6},{6,7},{7,0},{32,39},{33,32},{3... | collective-permute-start | bytes 884744 | tf_op jit(solution)/shard_map/ppermute | solution.py:137
  113.9 4.8 %collective-permute-start.12 = (bf16[576,256]{1,0:T(8,128)(2,1)S(1)}, bf16[576,256]{1,0:T(8,128)(2,1)S(1)}, u32[]{:S(2)}, u32[]{:S(2)}) collective-permute-start(bf16[576,256]{1,0:T(8,128)(2,1)S(1)} %collective-permute-done.10), channel_id=1, source_target_pairs={{0,7},{1,0},{2,1},{3,2},{4,3},{5,4},{6,5},{7,6},{32,33},{33,34},{3... | collective-permute-start | bytes 884744 | tf_op jit(solution)/shard_map/ppermute | solution.py:137
  119.0 1.9 %collective-permute-start.11 = (bf16[576,256]{1,0:T(8,128)(2,1)S(1)}, bf16[576,256]{1,0:T(8,128)(2,1)S(1)}, u32[]{:S(2)}, u32[]{:S(2)}) collective-permute-start(bf16[576,256]{1,0:T(8,128)(2,1)S(1)} %collective-permute-done.9), channel_id=1, source_target_pairs={{0,1},{1,2},{2,3},{3,4},{4,5},{5,6},{6,7},{7,0},{32,39},{33,32},{3... | collective-permute-start | bytes 884744 | tf_op jit(solution)/shard_map/ppermute | solution.py:137
  121.9 2.2 %collective-permute-done.5 = bf16[576,256]{1,0:T(8,128)(2,1)S(1)} collective-permute-done((bf16[576,256]{1,0:T(8,128)(2,1)S(1)}, bf16[576,256]{1,0:T(8,128)(2,1)S(1)}, u32[]{:S(2)}, u32[]{:S(2)}) %collective-permute-start.5) | collective-permute-done | bytes 294944 | tf_op jit(solution)/shard_map/ppermute | solution.py:137
  126.1 5.5 %collective-permute-start.14 = (bf16[576,256]{1,0:T(8,128)(2,1)S(1)}, bf16[576,256]{1,0:T(8,128)(2,1)S(1)}, u32[]{:S(2)}, u32[]{:S(2)}) collective-permute-start(bf16[576,256]{1,0:T(8,128)(2,1)S(1)} %collective-permute-done.12), channel_id=1, source_target_pairs={{0,7},{1,0},{2,1},{3,2},{4,3},{5,4},{6,5},{7,6},{32,33},{33,34},{3... | collective-permute-start | bytes 884744 | tf_op jit(solution)/shard_map/ppermute | solution.py:137
  134.8 2.6 %collective-permute-done.14 = bf16[576,256]{1,0:T(8,128)(2,1)S(1)} collective-permute-done((bf16[576,256]{1,0:T(8,128)(2,1)S(1)}, bf16[576,256]{1,0:T(8,128)(2,1)S(1)}, u32[]{:S(2)}, u32[]{:S(2)}) %collective-permute-start.14) | collective-permute-done | bytes 294944 | tf_op jit(solution)/shard_map/ppermute | solution.py:137
  137.5 5.6 %collective-permute-start.15 = (bf16[576,256]{1,0:T(8,128)(2,1)S(1)}, bf16[576,256]{1,0:T(8,128)(2,1)S(1)}, u32[]{:S(2)}, u32[]{:S(2)}) collective-permute-start(bf16[576,256]{1,0:T(8,128)(2,1)S(1)} %collective-permute-done.14), channel_id=1, source_target_pairs={{0,7},{1,0},{2,1},{3,2},{4,3},{5,4},{6,5},{7,6},{32,33},{33,34},{3... | collective-permute-start | bytes 884744 | tf_op jit(solution)/shard_map/ppermute | solution.py:137
  144.1 3.2 %collective-permute-done.15 = bf16[576,256]{1,0:T(8,128)(2,1)S(1)} collective-permute-done((bf16[576,256]{1,0:T(8,128)(2,1)S(1)}, bf16[576,256]{1,0:T(8,128)(2,1)S(1)}, u32[]{:S(2)}, u32[]{:S(2)}) %collective-permute-start.15) | collective-permute-done | bytes 294944 | tf_op jit(solution)/shard_map/ppermute | solution.py:137
  (64 shorter events, 17.3 us)
Async XLA Ops:
  0.0 33.5 %copy-start.2 = (bf16[768,768]{1,0:T(8,128)(2,1)S(1)}, bf16[768,768]{1,0:T(8,128)(2,1)}, u32[]{:S(2)}) copy-start(bf16[768,768]{1,0:T(8,128)(2,1)} %constant.192.clone) | copy-start | bytes 3538948
  0.0 22.5 %copy-start.6 = (s32[2,16]{1,0:T(2,128)S(1)}, s32[2,16]{1,0:T(2,128)}, u32[]{:S(2)}) copy-start(s32[2,16]{1,0:T(2,128)} %param.12) | copy-start | bytes 388
  0.0 22.7 %copy-start.5 = (s32[32,32,2]{1,2,0:T(2,128)S(1)}, s32[32,32,2]{1,2,0:T(2,128)}, u32[]{:S(2)}) copy-start(s32[32,32,2]{1,2,0:T(2,128)} %param.11) | copy-start | bytes 24580
  2.0 31.4 %all-to-all-start = ((bf16[32,24,128]{2,1,0:T(8,128)(2,1)}), bf16[32,24,128]{2,1,0:T(8,128)(2,1)S(1)}, u32[]{:S(2)}, u32[]{:S(2)}) async-start(bf16[32,24,128]{2,1,0:T(8,128)(2,1)} %bitcast.2), calls=%async_computation | async-start | bytes 393216 | tf_op jit(solution)/shard_map/all_to_all | solution.py:87
  33.5 25.2 %copy-start.4 = (bf16[2,576,768]{2,1,0:T(8,128)(2,1)S(1)}, bf16[2,576,768]{2,1,0:T(8,128)(2,1)}, u32[]{:S(2)}) copy-start(bf16[2,576,768]{2,1,0:T(8,128)(2,1)} %constant.194.clone) | copy-start | bytes 5308420
  34.0 25.0 %copy-start.3 = (bf16[576,768]{1,0:T(8,128)(2,1)S(1)}, bf16[576,768]{1,0:T(8,128)(2,1)}, u32[]{:S(2)}) copy-start(bf16[576,768]{1,0:T(8,128)(2,1)} %constant.195.clone) | copy-start | bytes 2654212
  34.8 23.8 %all-to-all-start.1 = ((bf16[32,24,128]{2,1,0:T(8,128)(2,1)}), bf16[32,24,128]{2,1,0:T(8,128)(2,1)S(1)}, u32[]{:S(2)}, u32[]{:S(2)}) async-start(bf16[32,24,128]{2,1,0:T(8,128)(2,1)} %bitcast.8), calls=%async_computation.1 | async-start | bytes 393216 | tf_op jit(solution)/shard_map/all_to_all | solution.py:91
  59.4 7.5 %collective-permute-start = (bf16[576,128]{1,0:T(8,128)(2,1)S(1)}, bf16[576,128]{1,0:T(8,128)(2,1)S(1)}, u32[]{:S(2)}, u32[]{:S(2)}) collective-permute-start(bf16[576,128]{1,0:T(8,128)(2,1)S(1)} %fusion.12), channel_id=1, source_target_pairs={{0,8},{8,0},{16,24},{24,16},{1,9},{9,1},{17,25},{25,17},{2,10},{10... | collective-permute-start | bytes 442376 | tf_op jit(solution)/shard_map/ppermute | solution.py:115
  67.0 32.0 %collective-permute-start.1 = (bf16[576,256]{1,0:T(8,128)(2,1)S(1)}, bf16[576,256]{1,0:T(8,128)(2,1)S(1)}, u32[]{:S(2)}, u32[]{:S(2)}) collective-permute-start(bf16[576,256]{1,0:T(8,128)(2,1)S(1)} %pad_maximum_fusion), channel_id=1, source_target_pairs={{0,1},{1,2},{2,3},{3,4},{4,5},{5,6},{6,7},{7,0},{32,39},{33,32},{3... | collective-permute-start | bytes 884744 | tf_op jit(solution)/shard_map/ppermute | solution.py:137
  70.2 26.3 %collective-permute-start.2 = (bf16[576,256]{1,0:T(8,128)(2,1)S(1)}, bf16[576,256]{1,0:T(8,128)(2,1)S(1)}, u32[]{:S(2)}, u32[]{:S(2)}) collective-permute-start(bf16[576,256]{1,0:T(8,128)(2,1)S(1)} %pad_maximum_fusion), channel_id=1, source_target_pairs={{0,7},{1,0},{2,1},{3,2},{4,3},{5,4},{6,5},{7,6},{32,33},{33,34},{3... | collective-permute-start | bytes 884744 | tf_op jit(solution)/shard_map/ppermute | solution.py:137
  74.1 15.3 %collective-permute-start.8 = (bf16[576,256]{1,0:T(8,128)(2,1)S(1)}, bf16[576,256]{1,0:T(8,128)(2,1)S(1)}, u32[]{:S(2)}, u32[]{:S(2)}) collective-permute-start(bf16[576,256]{1,0:T(8,128)(2,1)S(1)} %pad_maximum_fusion), channel_id=1, source_target_pairs={{0,16},{8,24},{16,0},{24,8},{1,17},{9,25},{17,1},{25,9},{2,18},{10... | collective-permute-start | bytes 884744 | tf_op jit(solution)/shard_map/ppermute | solution.py:117
  89.4 29.6 %collective-permute-start.9 = (bf16[576,256]{1,0:T(8,128)(2,1)S(1)}, bf16[576,256]{1,0:T(8,128)(2,1)S(1)}, u32[]{:S(2)}, u32[]{:S(2)}) collective-permute-start(bf16[576,256]{1,0:T(8,128)(2,1)S(1)} %collective-permute-done.8), channel_id=1, source_target_pairs={{0,1},{1,2},{2,3},{3,4},{4,5},{5,6},{6,7},{7,0},{32,39},{33,32},{3... | collective-permute-start | bytes 884744 | tf_op jit(solution)/shard_map/ppermute | solution.py:137
  92.5 21.4 %collective-permute-start.10 = (bf16[576,256]{1,0:T(8,128)(2,1)S(1)}, bf16[576,256]{1,0:T(8,128)(2,1)S(1)}, u32[]{:S(2)}, u32[]{:S(2)}) collective-permute-start(bf16[576,256]{1,0:T(8,128)(2,1)S(1)} %collective-permute-done.8), channel_id=1, source_target_pairs={{0,7},{1,0},{2,1},{3,2},{4,3},{5,4},{6,5},{7,6},{32,33},{33,34},{3... | collective-permute-start | bytes 884744 | tf_op jit(solution)/shard_map/ppermute | solution.py:137
  96.5 11.6 %collective-permute-start.4 = (bf16[576,256]{1,0:T(8,128)(2,1)S(1)}, bf16[576,256]{1,0:T(8,128)(2,1)S(1)}, u32[]{:S(2)}, u32[]{:S(2)}) collective-permute-start(bf16[576,256]{1,0:T(8,128)(2,1)S(1)} %collective-permute-done.2), channel_id=1, source_target_pairs={{0,7},{1,0},{2,1},{3,2},{4,3},{5,4},{6,5},{7,6},{32,33},{33,34},{3... | collective-permute-start | bytes 884744 | tf_op jit(solution)/shard_map/ppermute | solution.py:137
  99.1 12.6 %collective-permute-start.3 = (bf16[576,256]{1,0:T(8,128)(2,1)S(1)}, bf16[576,256]{1,0:T(8,128)(2,1)S(1)}, u32[]{:S(2)}, u32[]{:S(2)}) collective-permute-start(bf16[576,256]{1,0:T(8,128)(2,1)S(1)} %collective-permute-done.1), channel_id=1, source_target_pairs={{0,1},{1,2},{2,3},{3,4},{4,5},{5,6},{6,7},{7,0},{32,39},{33,32},{3... | collective-permute-start | bytes 884744 | tf_op jit(solution)/shard_map/ppermute | solution.py:137
  108.1 25.8 %collective-permute-start.6 = (bf16[576,256]{1,0:T(8,128)(2,1)S(1)}, bf16[576,256]{1,0:T(8,128)(2,1)S(1)}, u32[]{:S(2)}, u32[]{:S(2)}) collective-permute-start(bf16[576,256]{1,0:T(8,128)(2,1)S(1)} %collective-permute-done.4), channel_id=1, source_target_pairs={{0,7},{1,0},{2,1},{3,2},{4,3},{5,4},{6,5},{7,6},{32,33},{33,34},{3... | collective-permute-start | bytes 884744 | tf_op jit(solution)/shard_map/ppermute | solution.py:137
  111.6 12.5 %collective-permute-start.5 = (bf16[576,256]{1,0:T(8,128)(2,1)S(1)}, bf16[576,256]{1,0:T(8,128)(2,1)S(1)}, u32[]{:S(2)}, u32[]{:S(2)}) collective-permute-start(bf16[576,256]{1,0:T(8,128)(2,1)S(1)} %collective-permute-done.3), channel_id=1, source_target_pairs={{0,1},{1,2},{2,3},{3,4},{4,5},{5,6},{6,7},{7,0},{32,39},{33,32},{3... | collective-permute-start | bytes 884744 | tf_op jit(solution)/shard_map/ppermute | solution.py:137
  113.9 12.1 %collective-permute-start.12 = (bf16[576,256]{1,0:T(8,128)(2,1)S(1)}, bf16[576,256]{1,0:T(8,128)(2,1)S(1)}, u32[]{:S(2)}, u32[]{:S(2)}) collective-permute-start(bf16[576,256]{1,0:T(8,128)(2,1)S(1)} %collective-permute-done.10), channel_id=1, source_target_pairs={{0,7},{1,0},{2,1},{3,2},{4,3},{5,4},{6,5},{7,6},{32,33},{33,34},{3... | collective-permute-start | bytes 884744 | tf_op jit(solution)/shard_map/ppermute | solution.py:137
  119.0 12.6 %collective-permute-start.11 = (bf16[576,256]{1,0:T(8,128)(2,1)S(1)}, bf16[576,256]{1,0:T(8,128)(2,1)S(1)}, u32[]{:S(2)}, u32[]{:S(2)}) collective-permute-start(bf16[576,256]{1,0:T(8,128)(2,1)S(1)} %collective-permute-done.9), channel_id=1, source_target_pairs={{0,1},{1,2},{2,3},{3,4},{4,5},{5,6},{6,7},{7,0},{32,39},{33,32},{3... | collective-permute-start | bytes 884744 | tf_op jit(solution)/shard_map/ppermute | solution.py:137
  124.2 19.6 %collective-permute-start.7 = (bf16[576,256]{1,0:T(8,128)(2,1)S(1)}, bf16[576,256]{1,0:T(8,128)(2,1)S(1)}, u32[]{:S(2)}, u32[]{:S(2)}) collective-permute-start(bf16[576,256]{1,0:T(8,128)(2,1)S(1)} %collective-permute-done.5), channel_id=1, source_target_pairs={{0,1},{1,2},{2,3},{3,4},{4,5},{5,6},{6,7},{7,0},{32,39},{33,32},{3... | collective-permute-start | bytes 884744 | tf_op jit(solution)/shard_map/ppermute | solution.py:137
  126.1 11.4 %collective-permute-start.14 = (bf16[576,256]{1,0:T(8,128)(2,1)S(1)}, bf16[576,256]{1,0:T(8,128)(2,1)S(1)}, u32[]{:S(2)}, u32[]{:S(2)}) collective-permute-start(bf16[576,256]{1,0:T(8,128)(2,1)S(1)} %collective-permute-done.12), channel_id=1, source_target_pairs={{0,7},{1,0},{2,1},{3,2},{4,3},{5,4},{6,5},{7,6},{32,33},{33,34},{3... | collective-permute-start | bytes 884744 | tf_op jit(solution)/shard_map/ppermute | solution.py:137
  131.6 11.8 %collective-permute-start.13 = (bf16[576,256]{1,0:T(8,128)(2,1)S(1)}, bf16[576,256]{1,0:T(8,128)(2,1)S(1)}, u32[]{:S(2)}, u32[]{:S(2)}) collective-permute-start(bf16[576,256]{1,0:T(8,128)(2,1)S(1)} %collective-permute-done.11), channel_id=1, source_target_pairs={{0,1},{1,2},{2,3},{3,4},{4,5},{5,6},{6,7},{7,0},{32,39},{33,32},{3... | collective-permute-start | bytes 884744 | tf_op jit(solution)/shard_map/ppermute | solution.py:137
  137.5 9.8 %collective-permute-start.15 = (bf16[576,256]{1,0:T(8,128)(2,1)S(1)}, bf16[576,256]{1,0:T(8,128)(2,1)S(1)}, u32[]{:S(2)}, u32[]{:S(2)}) collective-permute-start(bf16[576,256]{1,0:T(8,128)(2,1)S(1)} %collective-permute-done.14), channel_id=1, source_target_pairs={{0,7},{1,0},{2,1},{3,2},{4,3},{5,4},{6,5},{7,6},{32,33},{33,34},{3... | collective-permute-start | bytes 884744 | tf_op jit(solution)/shard_map/ppermute | solution.py:137
  144.1 3.5 %copy-start.7 = (bf16[2,6,192,192]{3,2,1,0:T(8,128)(2,1)S(1)}, bf16[2,6,192,192]{3,2,1,0:T(8,128)(2,1)}, u32[]{:S(2)}) copy-start(bf16[2,6,192,192]{3,2,1,0:T(8,128)(2,1)} %constant.196.clone) | copy-start | bytes 2654212
  (2 other events, 4.3 us)

commit v4 on v3

--- a/solution.py
+++ b/solution.py
@@ -46,13 +46,12 @@
             for rh in range(2)
         ]
     )
-    place = np.zeros((2, OCC, NP * OCC, 2 * NP * HALF), np.float32)
-    for rh in range(2):
-        for il in range(OCC):
-            for q in range(NP):
-                for jl in range(OCC):
-                    part = (il + jl + rh) % 2
-                    place[rh, il, q * OCC + jl, part * NP * HALF + q * HALF + jl // 2] = 1.0
+    place = np.zeros((OCC, NP * OCC, 2 * NP * HALF), np.float32)
+    for il in range(OCC):
+        for q in range(NP):
+            for jl in range(OCC):
+                rh = (il + jl) % 2
+                place[il, q * OCC + jl, rh * NP * HALF + q * HALF + jl // 2] = 1.0
     blocks = one_hot(NP, [q for _, q, _ in order])
     return send, own, mirror, place, blocks
 
@@ -101,20 +100,17 @@
     diff = dot(jnp.asarray(OWN, bf), held) * masks[:, :1] - dot(mirror, other) * masks[:, 1:]
     diff = diff.astype(bf)
 
+    gathered = lax.all_gather(diff, "y", axis=0, tiled=False)
+    pieces = [jnp.concatenate([gathered[2 * r], gathered[2 * r + 1]], 1) for r in range(2)]
+
     col_mask = lax.dynamic_index_in_dim(int_pattern, v * cols // TP, 1, keepdims=False)
     weighted = integrals * jnp.repeat(col_mask, TP).astype(bf)[:, None]
-    weighted = weighted.reshape(NZ, 2, LANES, cols)
-    weighted = jnp.where(y % 2 == 0, weighted, weighted[:, ::-1]).reshape(kcd, cols)
-    core = lax.axis_index("core")
-    sign = 1 - 2 * core
+
+    sign = 1 - 2 * lax.axis_index("core")
 
     def term(c, distance):
         start = lax.rem(z + sign * distance + NZ, NZ) * width
         return dot(c, lax.dynamic_slice_in_dim(weighted, start, width, 0))
-
-    near = lax.ppermute(diff, "y", [(i, i ^ 1) for i in range(NY)])
-    piece = jnp.concatenate([diff, near], 1)
-    pieces = [piece, lax.ppermute(piece, "y", [(i, i ^ 2) for i in range(NY)])]
 
     def shift(step):
         return [
@@ -125,22 +121,18 @@
 
     ways = (shift(1), shift(-1))
     front = [list(pieces), list(pieces)]
-    totals = [None, None]
+    totals = [term(c, 0) for c in pieces]
     for step in range(1, NZ // 2 + 1):
         for i in range(2):
-            last = step == NZ // 2
-            if totals[i] is None:
-                totals[i] = term(pieces[i], 0)
             for w in range(2):
-                if last and w != i:
+                if step == NZ // 2 and w != i:
                     continue
                 front[w][i] = lax.ppermute(front[w][i], ("core", "z"), ways[w])
                 totals[i] = totals[i] + term(front[w][i], -step if w == 0 else step)
-    both = jnp.concatenate(
-        [t.astype(bf).reshape(OCC, NP * HALF, cols) for t in totals], 1
+    both = jnp.concatenate([t.astype(bf).reshape(OCC, NP * HALF, cols) for t in totals], 1)
+    out = jnp.einsum(
+        "bij,bjk->bik", jnp.asarray(PLACE, bf), both, preferred_element_type=jnp.float32
     )
-    place = lax.dynamic_index_in_dim(jnp.asarray(PLACE, bf), y // 2, 0, keepdims=False)
-    out = jnp.einsum("bij,bjk->bik", place, both, preferred_element_type=jnp.float32)
     return out.astype(bf).reshape(OCC * NP * OCC, cols)
 
 

time: 150 us -> 143 us (0.953)
  the two profiles are of different devices: /device:TPU:4 before, /device:TPU:2 now
where the time goes in v4:
time: 143 us; the launch traced here: 142 us
  starting transfers between devices  78 us (55%)
  waiting for transfers between devices  31.7 us (22%)
  blocking collectives  16.1 us (11%)
  matrix products  10.1 us (7%)
  local copies, waits for them, and re-layouts  3.93 us (3%)
  other arithmetic  2.09 us (1%)
    ppermute x14, starting transfers between devices, body(): front[w][i] = lax.ppermute(front[w][i], ('core', 'z'), ways[w])  47.1 us
    all_to_all x1, starting transfers between devices, body(): held = lax.all_to_all(first, VIRT, split_axis=0, concat_axis=0, tiled=True)  20.5 us
    all_gather x1, blocking collectives, body(): gathered = lax.all_gather(diff, 'y', axis=0, tiled=False)  16.1 us
    all_to_all x1, waiting for transfers between devices, body(): lax.all_to_all(second, PAIR, split_axis=0, concat_axis=0, tiled=True)  12.5 us
    all_to_all x1, waiting for transfers between devices, body(): held = lax.all_to_all(first, VIRT, split_axis=0, concat_axis=0, tiled=True)  10.6 us
    all_to_all x1, starting transfers between devices, body(): lax.all_to_all(second, PAIR, split_axis=0, concat_axis=0, tiled=True)  10.5 us
    dot_general x21, matrix products, dot(): return jnp.dot(a, b, preferred_element_type=jnp.float32)  8.63 us
    ppermute x14, waiting for transfers between devices, body(): front[w][i] = lax.ppermute(front[w][i], ('core', 'z'), ways[w])  8.6 us
  transfers between devices with their start and end apart: 16, of which 4 were waited for; matrix products, arithmetic and copies ran while one was open for 6% of the time, Pallas kernels for 0%

profile of v4, /device:TPU:2, one launch (start us, length us, event | category | flops | bytes accessed | tf_op | source)
XLA Modules:
  0.0 142.5 jit_solution(14255175707698780134)
XLA Ops:
  2.0 20.5 %all-to-all-start = ((bf16[32,24,128]{2,1,0:T(8,128)(2,1)}), bf16[32,24,128]{2,1,0:T(8,128)(2,1)S(1)}, u32[]{:S(2)}, u32[]{:S(2)}) async-start(bf16[32,24,128]{2,1,0:T(8,128)(2,1)} %bitcast.1), calls=%async_computation | async-start | bytes 393216 | tf_op jit(solution)/shard_map/all_to_all | solution.py:86
  22.8 10.6 %all-to-all-done = bf16[32,24,128]{2,1,0:T(8,128)(2,1)S(1)} async-done(((bf16[32,24,128]{2,1,0:T(8,128)(2,1)}), bf16[32,24,128]{2,1,0:T(8,128)(2,1)S(1)}, u32[]{:S(2)}, u32[]{:S(2)}) %all-to-all-start) | async-done | bytes 196640 | tf_op jit(solution)/shard_map/all_to_all | solution.py:86
  34.8 10.5 %all-to-all-start.1 = ((bf16[32,24,128]{2,1,0:T(8,128)(2,1)}), bf16[32,24,128]{2,1,0:T(8,128)(2,1)S(1)}, u32[]{:S(2)}, u32[]{:S(2)}) async-start(bf16[32,24,128]{2,1,0:T(8,128)(2,1)} %bitcast.7), calls=%async_computation.1 | async-start | bytes 393216 | tf_op jit(solution)/shard_map/all_to_all | solution.py:90
  45.8 1.1 fusion.64
  47.0 12.5 %all-to-all-done.1 = bf16[32,24,128]{2,1,0:T(8,128)(2,1)S(1)} async-done(((bf16[32,24,128]{2,1,0:T(8,128)(2,1)}), bf16[32,24,128]{2,1,0:T(8,128)(2,1)S(1)}, u32[]{:S(2)}, u32[]{:S(2)}) %all-to-all-start.1) | async-done | bytes 196640 | tf_op jit(solution)/shard_map/all_to_all | solution.py:90
  60.3 16.1 %all-gather = bf16[2304,128]{1,0:T(8,128)(2,1)S(1)} all-gather(bf16[576,128]{1,0:T(8,128)(2,1)S(1)} %fusion.11), channel_id=2, replica_groups=mesh['x'=8,'yh'=2,'core'=2,'y'=4,'z'=8] {'y'}, dimensions={0}, use_global_device_ids=true | all-gather | bytes 737280 | tf_op jit(solution)/shard_map/all_gather | solution.py:103
  77.1 3.2 %collective-permute-start = (bf16[576,256]{1,0:T(8,128)(2,1)}, bf16[576,256]{1,0:T(8,128)(2,1)S(1)}, u32[]{:S(2)}, u32[]{:S(2)}) collective-permute-start(bf16[576,256]{1,0:T(8,128)(2,1)} %pad_maximum_fusion), channel_id=1, source_target_pairs={{0,1},{1,2},{2,3},{3,4},{4,5},{5,6},{6,7},{7,0},{32,39},{33,32},{3... | collective-permute-start | bytes 884744 | tf_op jit(solution)/shard_map/ppermute | solution.py:130
  80.4 3.8 %collective-permute-start.1 = (bf16[576,256]{1,0:T(8,128)(2,1)}, bf16[576,256]{1,0:T(8,128)(2,1)}, u32[]{:S(2)}, u32[]{:S(2)}) collective-permute-start(bf16[576,256]{1,0:T(8,128)(2,1)} %pad_maximum_fusion), channel_id=1, source_target_pairs={{0,7},{1,0},{2,1},{3,2},{4,3},{5,4},{6,5},{7,6},{32,33},{33,34},{3... | collective-permute-start | bytes 884744 | tf_op jit(solution)/shard_map/ppermute | solution.py:130
  84.9 2.0 %collective-permute-start.7 = (bf16[576,256]{1,0:T(8,128)(2,1)}, bf16[576,256]{1,0:T(8,128)(2,1)S(1)}, u32[]{:S(2)}, u32[]{:S(2)}) collective-permute-start(bf16[576,256]{1,0:T(8,128)(2,1)} %pad_maximum_fusion.1), channel_id=1, source_target_pairs={{0,1},{1,2},{2,3},{3,4},{4,5},{5,6},{6,7},{7,0},{32,39},{33,32},{3... | collective-permute-start | bytes 884744 | tf_op jit(solution)/shard_map/ppermute | solution.py:130
  87.4 5.0 %collective-permute-start.8 = (bf16[576,256]{1,0:T(8,128)(2,1)}, bf16[576,256]{1,0:T(8,128)(2,1)S(1)}, u32[]{:S(2)}, u32[]{:S(2)}) collective-permute-start(bf16[576,256]{1,0:T(8,128)(2,1)} %pad_maximum_fusion.1), channel_id=1, source_target_pairs={{0,7},{1,0},{2,1},{3,2},{4,3},{5,4},{6,5},{7,6},{32,33},{33,34},{3... | collective-permute-start | bytes 884744 | tf_op jit(solution)/shard_map/ppermute | solution.py:130
  93.0 3.1 %collective-permute-start.3 = (bf16[576,256]{1,0:T(8,128)(2,1)}, bf16[576,256]{1,0:T(8,128)(2,1)S(1)}, u32[]{:S(2)}, u32[]{:S(2)}) collective-permute-start(bf16[576,256]{1,0:T(8,128)(2,1)} %collective-permute-done.1), channel_id=1, source_target_pairs={{0,7},{1,0},{2,1},{3,2},{4,3},{5,4},{6,5},{7,6},{32,33},{33,34},{3... | collective-permute-start | bytes 884744 | tf_op jit(solution)/shard_map/ppermute | solution.py:130
  96.2 2.7 %collective-permute-start.2 = (bf16[576,256]{1,0:T(8,128)(2,1)S(1)}, bf16[576,256]{1,0:T(8,128)(2,1)S(1)}, u32[]{:S(2)}, u32[]{:S(2)}) collective-permute-start(bf16[576,256]{1,0:T(8,128)(2,1)S(1)} %collective-permute-done), channel_id=1, source_target_pairs={{0,1},{1,2},{2,3},{3,4},{4,5},{5,6},{6,7},{7,0},{32,39},{33,32},{3... | collective-permute-start | bytes 884744 | tf_op jit(solution)/shard_map/ppermute | solution.py:130
  98.9 1.9 %collective-permute-start.9 = (bf16[576,256]{1,0:T(8,128)(2,1)S(1)}, bf16[576,256]{1,0:T(8,128)(2,1)S(1)}, u32[]{:S(2)}, u32[]{:S(2)}) collective-permute-start(bf16[576,256]{1,0:T(8,128)(2,1)S(1)} %collective-permute-done.7), channel_id=1, source_target_pairs={{0,1},{1,2},{2,3},{3,4},{4,5},{5,6},{6,7},{7,0},{32,39},{33,32},{3... | collective-permute-start | bytes 884744 | tf_op jit(solution)/shard_map/ppermute | solution.py:130
  101.5 5.1 %collective-permute-start.10 = (bf16[576,256]{1,0:T(8,128)(2,1)S(1)}, bf16[576,256]{1,0:T(8,128)(2,1)S(1)}, u32[]{:S(2)}, u32[]{:S(2)}) collective-permute-start(bf16[576,256]{1,0:T(8,128)(2,1)S(1)} %collective-permute-done.8), channel_id=1, source_target_pairs={{0,7},{1,0},{2,1},{3,2},{4,3},{5,4},{6,5},{7,6},{32,33},{33,34},{3... | collective-permute-start | bytes 884744 | tf_op jit(solution)/shard_map/ppermute | solution.py:130
  106.7 1.3 convolution_add_fusion.8
  108.3 3.6 %collective-permute-start.5 = (bf16[576,256]{1,0:T(8,128)(2,1)S(1)}, bf16[576,256]{1,0:T(8,128)(2,1)S(1)}, u32[]{:S(2)}, u32[]{:S(2)}) collective-permute-start(bf16[576,256]{1,0:T(8,128)(2,1)S(1)} %collective-permute-done.3), channel_id=1, source_target_pairs={{0,7},{1,0},{2,1},{3,2},{4,3},{5,4},{6,5},{7,6},{32,33},{33,34},{3... | collective-permute-start | bytes 884744 | tf_op jit(solution)/shard_map/ppermute | solution.py:130
  112.2 2.3 %collective-permute-start.4 = (bf16[576,256]{1,0:T(8,128)(2,1)S(1)}, bf16[576,256]{1,0:T(8,128)(2,1)S(1)}, u32[]{:S(2)}, u32[]{:S(2)}) collective-permute-start(bf16[576,256]{1,0:T(8,128)(2,1)S(1)} %collective-permute-done.2), channel_id=1, source_target_pairs={{0,1},{1,2},{2,3},{3,4},{4,5},{5,6},{6,7},{7,0},{32,39},{33,32},{3... | collective-permute-start | bytes 884744 | tf_op jit(solution)/shard_map/ppermute | solution.py:130
  114.5 4.8 %collective-permute-start.12 = (bf16[576,256]{1,0:T(8,128)(2,1)S(1)}, bf16[576,256]{1,0:T(8,128)(2,1)S(1)}, u32[]{:S(2)}, u32[]{:S(2)}) collective-permute-start(bf16[576,256]{1,0:T(8,128)(2,1)S(1)} %collective-permute-done.10), channel_id=1, source_target_pairs={{0,7},{1,0},{2,1},{3,2},{4,3},{5,4},{6,5},{7,6},{32,33},{33,34},{3... | collective-permute-start | bytes 884744 | tf_op jit(solution)/shard_map/ppermute | solution.py:130
  119.6 1.9 %collective-permute-start.11 = (bf16[576,256]{1,0:T(8,128)(2,1)S(1)}, bf16[576,256]{1,0:T(8,128)(2,1)S(1)}, u32[]{:S(2)}, u32[]{:S(2)}) collective-permute-start(bf16[576,256]{1,0:T(8,128)(2,1)S(1)} %collective-permute-done.9), channel_id=1, source_target_pairs={{0,1},{1,2},{2,3},{3,4},{4,5},{5,6},{6,7},{7,0},{32,39},{33,32},{3... | collective-permute-start | bytes 884744 | tf_op jit(solution)/shard_map/ppermute | solution.py:130
  122.2 1.3 collective-permute-done.12
  123.5 5.6 %collective-permute-start.13 = (bf16[576,256]{1,0:T(8,128)(2,1)S(1)}, bf16[576,256]{1,0:T(8,128)(2,1)S(1)}, u32[]{:S(2)}, u32[]{:S(2)}) collective-permute-start(bf16[576,256]{1,0:T(8,128)(2,1)S(1)} %collective-permute-done.12), channel_id=1, source_target_pairs={{0,7},{1,0},{2,1},{3,2},{4,3},{5,4},{6,5},{7,6},{32,33},{33,34},{3... | collective-permute-start | bytes 884744 | tf_op jit(solution)/shard_map/ppermute | solution.py:130
  129.8 1.9 %collective-permute-start.6 = (bf16[576,256]{1,0:T(8,128)(2,1)S(1)}, bf16[576,256]{1,0:T(8,128)(2,1)S(1)}, u32[]{:S(2)}, u32[]{:S(2)}) collective-permute-start(bf16[576,256]{1,0:T(8,128)(2,1)S(1)} %collective-permute-done.4), channel_id=1, source_target_pairs={{0,1},{1,2},{2,3},{3,4},{4,5},{5,6},{6,7},{7,0},{32,39},{33,32},{3... | collective-permute-start | bytes 884744 | tf_op jit(solution)/shard_map/ppermute | solution.py:130
  132.4 7.2 %collective-permute-done.6 = bf16[576,256]{1,0:T(8,128)(2,1)S(1)} collective-permute-done((bf16[576,256]{1,0:T(8,128)(2,1)S(1)}, bf16[576,256]{1,0:T(8,128)(2,1)S(1)}, u32[]{:S(2)}, u32[]{:S(2)}) %collective-permute-start.6) | collective-permute-done | bytes 294944 | tf_op jit(solution)/shard_map/ppermute | solution.py:130
  141.0 1.5 %convolution_convert_fusion.1 = bf16[6,512,192]{1,2,0:T(8,128)(2,1)} fusion(bf16[6,192,192]{2,1,0:T(8,128)(2,1)S(1)} %copy-done.7, bf16[6,96,512]{2,1,0:T(8,128)(2,1)S(1)} %bitcast.56, bf16[6,96,512]{2,1,0:T(8,128)(2,1)S(1)} %bitcast.55), kind=kOutput, calls=%fused_computation.1 | convolution fusion | flops 229441536 | bytes 2801664 | tf_op jit(solution)/shard_map/bij,bjk->bik/dot_general | solution.py:133
  (62 shorter events, 12.3 us)
Async XLA Ops:
  0.0 0.9 copy-start
  0.0 33.5 %copy-start.2 = (bf16[768,768]{1,0:T(8,128)(2,1)S(1)}, bf16[768,768]{1,0:T(8,128)(2,1)}, u32[]{:S(2)}) copy-start(bf16[768,768]{1,0:T(8,128)(2,1)} %constant.180.clone) | copy-start | bytes 3538948
  0.0 22.5 %copy-start.6 = (s32[2,16]{1,0:T(2,128)S(1)}, s32[2,16]{1,0:T(2,128)}, u32[]{:S(2)}) copy-start(s32[2,16]{1,0:T(2,128)} %param.12) | copy-start | bytes 388
  0.0 22.7 %copy-start.5 = (s32[32,32,2]{1,2,0:T(2,128)S(1)}, s32[32,32,2]{1,2,0:T(2,128)}, u32[]{:S(2)}) copy-start(s32[32,32,2]{1,2,0:T(2,128)} %param.11) | copy-start | bytes 24580
  2.0 31.4 %all-to-all-start = ((bf16[32,24,128]{2,1,0:T(8,128)(2,1)}), bf16[32,24,128]{2,1,0:T(8,128)(2,1)S(1)}, u32[]{:S(2)}, u32[]{:S(2)}) async-start(bf16[32,24,128]{2,1,0:T(8,128)(2,1)} %bitcast.1), calls=%async_computation | async-start | bytes 393216 | tf_op jit(solution)/shard_map/all_to_all | solution.py:86
  33.5 26.0 %copy-start.4 = (bf16[2,576,768]{2,1,0:T(8,128)(2,1)S(1)}, bf16[2,576,768]{2,1,0:T(8,128)(2,1)}, u32[]{:S(2)}) copy-start(bf16[2,576,768]{2,1,0:T(8,128)(2,1)} %constant.182.clone) | copy-start | bytes 5308420
  34.0 25.8 %copy-start.3 = (bf16[576,768]{1,0:T(8,128)(2,1)S(1)}, bf16[576,768]{1,0:T(8,128)(2,1)}, u32[]{:S(2)}) copy-start(bf16[576,768]{1,0:T(8,128)(2,1)} %constant.183.clone) | copy-start | bytes 2654212
  34.8 24.6 %all-to-all-start.1 = ((bf16[32,24,128]{2,1,0:T(8,128)(2,1)}), bf16[32,24,128]{2,1,0:T(8,128)(2,1)S(1)}, u32[]{:S(2)}, u32[]{:S(2)}) async-start(bf16[32,24,128]{2,1,0:T(8,128)(2,1)} %bitcast.7), calls=%async_computation.1 | async-start | bytes 393216 | tf_op jit(solution)/shard_map/all_to_all | solution.py:90
  76.3 10.6 %copy-start.1 = (bf16[2048,512]{1,0:T(8,128)(2,1)S(1)}, bf16[2048,512]{1,0:T(8,128)(2,1)}, u32[]{:S(2)}) copy-start(bf16[2048,512]{1,0:T(8,128)(2,1)} %param.10) | copy-start | bytes 6291460
  77.1 19.1 %collective-permute-start = (bf16[576,256]{1,0:T(8,128)(2,1)}, bf16[576,256]{1,0:T(8,128)(2,1)S(1)}, u32[]{:S(2)}, u32[]{:S(2)}) collective-permute-start(bf16[576,256]{1,0:T(8,128)(2,1)} %pad_maximum_fusion), channel_id=1, source_target_pairs={{0,1},{1,2},{2,3},{3,4},{4,5},{5,6},{6,7},{7,0},{32,39},{33,32},{3... | collective-permute-start | bytes 884744 | tf_op jit(solution)/shard_map/ppermute | solution.py:130
  80.4 12.7 %collective-permute-start.1 = (bf16[576,256]{1,0:T(8,128)(2,1)}, bf16[576,256]{1,0:T(8,128)(2,1)}, u32[]{:S(2)}, u32[]{:S(2)}) collective-permute-start(bf16[576,256]{1,0:T(8,128)(2,1)} %pad_maximum_fusion), channel_id=1, source_target_pairs={{0,7},{1,0},{2,1},{3,2},{4,3},{5,4},{6,5},{7,6},{32,33},{33,34},{3... | collective-permute-start | bytes 884744 | tf_op jit(solution)/shard_map/ppermute | solution.py:130
  84.9 14.0 %collective-permute-start.7 = (bf16[576,256]{1,0:T(8,128)(2,1)}, bf16[576,256]{1,0:T(8,128)(2,1)S(1)}, u32[]{:S(2)}, u32[]{:S(2)}) collective-permute-start(bf16[576,256]{1,0:T(8,128)(2,1)} %pad_maximum_fusion.1), channel_id=1, source_target_pairs={{0,1},{1,2},{2,3},{3,4},{4,5},{5,6},{6,7},{7,0},{32,39},{33,32},{3... | collective-permute-start | bytes 884744 | tf_op jit(solution)/shard_map/ppermute | solution.py:130
  87.4 14.1 %collective-permute-start.8 = (bf16[576,256]{1,0:T(8,128)(2,1)}, bf16[576,256]{1,0:T(8,128)(2,1)S(1)}, u32[]{:S(2)}, u32[]{:S(2)}) collective-permute-start(bf16[576,256]{1,0:T(8,128)(2,1)} %pad_maximum_fusion.1), channel_id=1, source_target_pairs={{0,7},{1,0},{2,1},{3,2},{4,3},{5,4},{6,5},{7,6},{32,33},{33,34},{3... | collective-permute-start | bytes 884744 | tf_op jit(solution)/shard_map/ppermute | solution.py:130
  93.0 15.2 %collective-permute-start.3 = (bf16[576,256]{1,0:T(8,128)(2,1)}, bf16[576,256]{1,0:T(8,128)(2,1)S(1)}, u32[]{:S(2)}, u32[]{:S(2)}) collective-permute-start(bf16[576,256]{1,0:T(8,128)(2,1)} %collective-permute-done.1), channel_id=1, source_target_pairs={{0,7},{1,0},{2,1},{3,2},{4,3},{5,4},{6,5},{7,6},{32,33},{33,34},{3... | collective-permute-start | bytes 884744 | tf_op jit(solution)/shard_map/ppermute | solution.py:130
  96.2 16.0 %collective-permute-start.2 = (bf16[576,256]{1,0:T(8,128)(2,1)S(1)}, bf16[576,256]{1,0:T(8,128)(2,1)S(1)}, u32[]{:S(2)}, u32[]{:S(2)}) collective-permute-start(bf16[576,256]{1,0:T(8,128)(2,1)S(1)} %collective-permute-done), channel_id=1, source_target_pairs={{0,1},{1,2},{2,3},{3,4},{4,5},{5,6},{6,7},{7,0},{32,39},{33,32},{3... | collective-permute-start | bytes 884744 | tf_op jit(solution)/shard_map/ppermute | solution.py:130
  98.9 20.7 %collective-permute-start.9 = (bf16[576,256]{1,0:T(8,128)(2,1)S(1)}, bf16[576,256]{1,0:T(8,128)(2,1)S(1)}, u32[]{:S(2)}, u32[]{:S(2)}) collective-permute-start(bf16[576,256]{1,0:T(8,128)(2,1)S(1)} %collective-permute-done.7), channel_id=1, source_target_pairs={{0,1},{1,2},{2,3},{3,4},{4,5},{5,6},{6,7},{7,0},{32,39},{33,32},{3... | collective-permute-start | bytes 884744 | tf_op jit(solution)/shard_map/ppermute | solution.py:130
  101.5 13.0 %collective-permute-start.10 = (bf16[576,256]{1,0:T(8,128)(2,1)S(1)}, bf16[576,256]{1,0:T(8,128)(2,1)S(1)}, u32[]{:S(2)}, u32[]{:S(2)}) collective-permute-start(bf16[576,256]{1,0:T(8,128)(2,1)S(1)} %collective-permute-done.8), channel_id=1, source_target_pairs={{0,7},{1,0},{2,1},{3,2},{4,3},{5,4},{6,5},{7,6},{32,33},{33,34},{3... | collective-permute-start | bytes 884744 | tf_op jit(solution)/shard_map/ppermute | solution.py:130
  108.3 21.2 %collective-permute-start.5 = (bf16[576,256]{1,0:T(8,128)(2,1)S(1)}, bf16[576,256]{1,0:T(8,128)(2,1)S(1)}, u32[]{:S(2)}, u32[]{:S(2)}) collective-permute-start(bf16[576,256]{1,0:T(8,128)(2,1)S(1)} %collective-permute-done.3), channel_id=1, source_target_pairs={{0,7},{1,0},{2,1},{3,2},{4,3},{5,4},{6,5},{7,6},{32,33},{33,34},{3... | collective-permute-start | bytes 884744 | tf_op jit(solution)/shard_map/ppermute | solution.py:130
  112.2 17.6 %collective-permute-start.4 = (bf16[576,256]{1,0:T(8,128)(2,1)S(1)}, bf16[576,256]{1,0:T(8,128)(2,1)S(1)}, u32[]{:S(2)}, u32[]{:S(2)}) collective-permute-start(bf16[576,256]{1,0:T(8,128)(2,1)S(1)} %collective-permute-done.2), channel_id=1, source_target_pairs={{0,1},{1,2},{2,3},{3,4},{4,5},{5,6},{6,7},{7,0},{32,39},{33,32},{3... | collective-permute-start | bytes 884744 | tf_op jit(solution)/shard_map/ppermute | solution.py:130
  114.5 9.0 %collective-permute-start.12 = (bf16[576,256]{1,0:T(8,128)(2,1)S(1)}, bf16[576,256]{1,0:T(8,128)(2,1)S(1)}, u32[]{:S(2)}, u32[]{:S(2)}) collective-permute-start(bf16[576,256]{1,0:T(8,128)(2,1)S(1)} %collective-permute-done.10), channel_id=1, source_target_pairs={{0,7},{1,0},{2,1},{3,2},{4,3},{5,4},{6,5},{7,6},{32,33},{33,34},{3... | collective-permute-start | bytes 884744 | tf_op jit(solution)/shard_map/ppermute | solution.py:130
  119.6 12.4 %collective-permute-start.11 = (bf16[576,256]{1,0:T(8,128)(2,1)S(1)}, bf16[576,256]{1,0:T(8,128)(2,1)S(1)}, u32[]{:S(2)}, u32[]{:S(2)}) collective-permute-start(bf16[576,256]{1,0:T(8,128)(2,1)S(1)} %collective-permute-done.9), channel_id=1, source_target_pairs={{0,1},{1,2},{2,3},{3,4},{4,5},{5,6},{6,7},{7,0},{32,39},{33,32},{3... | collective-permute-start | bytes 884744 | tf_op jit(solution)/shard_map/ppermute | solution.py:130
  123.5 16.4 %collective-permute-start.13 = (bf16[576,256]{1,0:T(8,128)(2,1)S(1)}, bf16[576,256]{1,0:T(8,128)(2,1)S(1)}, u32[]{:S(2)}, u32[]{:S(2)}) collective-permute-start(bf16[576,256]{1,0:T(8,128)(2,1)S(1)} %collective-permute-done.12), channel_id=1, source_target_pairs={{0,7},{1,0},{2,1},{3,2},{4,3},{5,4},{6,5},{7,6},{32,33},{33,34},{3... | collective-permute-start | bytes 884744 | tf_op jit(solution)/shard_map/ppermute | solution.py:130
  129.8 9.8 %collective-permute-start.6 = (bf16[576,256]{1,0:T(8,128)(2,1)S(1)}, bf16[576,256]{1,0:T(8,128)(2,1)S(1)}, u32[]{:S(2)}, u32[]{:S(2)}) collective-permute-start(bf16[576,256]{1,0:T(8,128)(2,1)S(1)} %collective-permute-done.4), channel_id=1, source_target_pairs={{0,1},{1,2},{2,3},{3,4},{4,5},{5,6},{6,7},{7,0},{32,39},{33,32},{3... | collective-permute-start | bytes 884744 | tf_op jit(solution)/shard_map/ppermute | solution.py:130
  139.9 1.1 copy-start.7

commit v5 on v4

--- a/solution.py
+++ b/solution.py
@@ -2,6 +2,8 @@
 import jax.numpy as jnp
 import numpy as np
 from jax import lax
+from jax.experimental import pallas as pl
+from jax.experimental.pallas import tpu as pltpu
 from jax.sharding import Mesh, PartitionSpec as P
 
 TP = 1024
@@ -46,12 +48,13 @@
             for rh in range(2)
         ]
     )
-    place = np.zeros((OCC, NP * OCC, 2 * NP * HALF), np.float32)
-    for il in range(OCC):
-        for q in range(NP):
-            for jl in range(OCC):
-                rh = (il + jl) % 2
-                place[il, q * OCC + jl, rh * NP * HALF + q * HALF + jl // 2] = 1.0
+    place = np.array(
+        [
+            [((il + jl) % 2 * NP + q) * HALF + jl // 2 for q in range(NP) for jl in range(OCC)]
+            for il in range(OCC)
+        ],
+        np.int32,
+    )
     blocks = one_hot(NP, [q for _, q, _ in order])
     return send, own, mirror, place, blocks
 
@@ -61,6 +64,51 @@
 
 def dot(a, b):
     return jnp.dot(a, b, preferred_element_type=jnp.float32)
+
+
+TILE = 192
+
+
+def terms_kernel(starts_ref, weights_ref, *refs):
+    count = (len(refs) - 2) // 2
+    width = refs[0].shape[1]
+    for i in range(2):
+        chunks = refs[i * count : (i + 1) * count]
+        out = refs[2 * count + i]
+
+        def tile(t, carry, chunks=chunks, out=out):
+            rows = pl.ds(pl.multiple_of(t * TILE, TILE), TILE)
+            total = None
+            for j, chunk in enumerate(chunks):
+                here = pl.ds(pl.multiple_of(starts_ref[j], width), width)
+                part = jnp.dot(
+                    chunk[rows, :], weights_ref[here, :], preferred_element_type=jnp.float32
+                )
+                total = part if total is None else total + part
+            out[rows, :] = total
+            return carry
+
+        lax.fori_loop(0, out.shape[0] // TILE, tile, 0)
+
+
+def terms(starts, weights, chunks):
+    rows, width = chunks[0][0].shape
+    cols = weights.shape[1]
+    count = len(chunks[0])
+    out = jax.ShapeDtypeStruct((rows, cols), jnp.float32)
+    vmem = pl.BlockSpec(memory_space=pltpu.VMEM)
+    return pl.pallas_call(
+        terms_kernel,
+        out_shape=(out, out),
+        in_specs=[pl.BlockSpec(memory_space=pltpu.SMEM)] + [vmem] * (1 + 2 * count),
+        out_specs=(vmem, vmem),
+        compiler_params=pltpu.CompilerParams(vmem_limit_bytes=32 * 2**20),
+        cost_estimate=pl.CostEstimate(
+            flops=4 * count * rows * width * cols,
+            bytes_accessed=2 * weights.size + 4 * count * rows * width + 8 * rows * cols,
+            transcendentals=0,
+        ),
+    )(starts, weights, *chunks[0], *chunks[1])
 
 
 def body(amplitudes, integrals, amp_pattern, int_pattern):
@@ -106,6 +154,8 @@
     col_mask = lax.dynamic_index_in_dim(int_pattern, v * cols // TP, 1, keepdims=False)
     weighted = integrals * jnp.repeat(col_mask, TP).astype(bf)[:, None]
 
+    place = (jnp.asarray(PLACE)[:, :, None] == jnp.arange(NP * OCC)[None, None, :]).astype(bf)
+    weighted, place = lax.optimization_barrier((weighted, place))
     sign = 1 - 2 * lax.axis_index("core")
 
     def term(c, distance):
@@ -121,17 +171,19 @@
 
     ways = (shift(1), shift(-1))
     front = [list(pieces), list(pieces)]
-    totals = [term(c, 0) for c in pieces]
-    for step in range(1, NZ // 2 + 1):
+    held = [[(c, 0)] for c in pieces]
+    for step in range(1, NZ // 2):
         for i in range(2):
             for w in range(2):
-                if step == NZ // 2 and w != i:
-                    continue
                 front[w][i] = lax.ppermute(front[w][i], ("core", "z"), ways[w])
-                totals[i] = totals[i] + term(front[w][i], -step if w == 0 else step)
+                held[i].append((front[w][i], -step if w == 0 else step))
+    sent = [lax.ppermute(front[i][i], ("core", "z"), ways[i]) for i in range(2)]
+    starts = jnp.stack([lax.rem(z + sign * d + NZ, NZ) * width for _, d in held[0]])
+    sums = terms(starts.astype(jnp.int32), weighted, [[c for c, _ in h] for h in held])
+    totals = [sums[i] + term(sent[i], NZ // 2) for i in range(2)]
     both = jnp.concatenate([t.astype(bf).reshape(OCC, NP * HALF, cols) for t in totals], 1)
     out = jnp.einsum(
-        "bij,bjk->bik", jnp.asarray(PLACE, bf), both, preferred_element_type=jnp.float32
+        "bij,bjk->bik", place, both, preferred_element_type=jnp.float32
     )
     return out.astype(bf).reshape(OCC * NP * OCC, cols)
 

time: 143 us -> 145 us (1.014)
  waiting for transfers between devices: 31.7 us -> 26.1 us
  Pallas kernels: 0 us -> 4.75 us
  matrix products: 10.1 us -> 5.68 us
  local copies, waits for them, and re-layouts: 3.93 us -> 7.3 us
  starting transfers between devices: 78 us -> 80.7 us
    ppermute x0 -> x2, starting transfers between devices: none -> 7.5 us  [body(): sent = [lax.ppermute(front[i][i], ('core', 'z'), ways[i]) for i in range(2)]]
    ppermute x14 -> x12, waiting for transfers between devices: 8.6 us -> 2.61 us  [body(): front[w][i] = lax.ppermute(front[w][i], ('core', 'z'), ways[w])]
    pallas_call x0 -> x1, Pallas kernels: none -> 4.75 us  [terms(): pl.pallas_call(terms_kernel, out_shape=(out, out), in_specs=[pl.BlockSpec...]
    ppermute x14 -> x12, starting transfers between devices: 47.1 us -> 42.3 us  [body(): front[w][i] = lax.ppermute(front[w][i], ('core', 'z'), ways[w])]
    dot_general x21 -> x7, matrix products: 8.63 us -> 4.21 us  [dot(): return jnp.dot(a, b, preferred_element_type=jnp.float32)]
    unnamed x18 -> x26, local copies, waits for them, and re-layouts: 1.67 us -> 4.96 us
    mul x1, other arithmetic: 0.34 us -> 1.93 us  [body(): weighted = integrals * jnp.repeat(col_mask, TP).astype(bf)[:, None]]
  transfers between devices with their start and end apart: 16 -> 16, of which waited for: 4 -> 4; matrix products, arithmetic and copies ran while one was open for 6% -> 4% of each run, Pallas kernels for 0% -> 3%
where the time goes in v5:
time: 145 us; the launch traced here: 144 us
  starting transfers between devices  80.7 us (56%)
  waiting for transfers between devices  26.1 us (18%)
  blocking collectives  16.1 us (11%)
  local copies, waits for them, and re-layouts  7.3 us (5%)
  matrix products  5.68 us (4%)
  Pallas kernels  4.75 us (3%)
  other arithmetic  3.29 us (2%)
    ppermute x12, starting transfers between devices, body(): front[w][i] = lax.ppermute(front[w][i], ('core', 'z'), ways[w])  42.3 us
    all_to_all x1, starting transfers between devices, body(): held = lax.all_to_all(first, VIRT, split_axis=0, concat_axis=0, tiled=True)  20.5 us
    all_gather x1, blocking collectives, body(): gathered = lax.all_gather(diff, 'y', axis=0, tiled=False)  16.1 us
    all_to_all x1, waiting for transfers between devices, body(): lax.all_to_all(second, PAIR, split_axis=0, concat_axis=0, tiled=True)  12.5 us
    all_to_all x1, waiting for transfers between devices, body(): held = lax.all_to_all(first, VIRT, split_axis=0, concat_axis=0, tiled=True)  10.9 us
    all_to_all x1, starting transfers between devices, body(): lax.all_to_all(second, PAIR, split_axis=0, concat_axis=0, tiled=True)  10.5 us
    ppermute x2, starting transfers between devices, body(): sent = [lax.ppermute(front[i][i], ('core', 'z'), ways[i]) for i in range(2)]  7.5 us
    unnamed x26, local copies, waits for them, and re-layouts  4.96 us
  transfers between devices with their start and end apart: 16, of which 4 were waited for; matrix products, arithmetic and copies ran while one was open for 4% of the time, Pallas kernels for 3%

profile of v5, /device:TPU:2, one launch (start us, length us, event | category | flops | bytes accessed | tf_op | source)
XLA Modules:
  0.0 144.4 jit_solution(17285505716068657492)
XLA Ops:
  2.0 20.5 %all-to-all-start = ((bf16[32,24,128]{2,1,0:T(8,128)(2,1)}), bf16[32,24,128]{2,1,0:T(8,128)(2,1)S(1)}, u32[]{:S(2)}, u32[]{:S(2)}) async-start(bf16[32,24,128]{2,1,0:T(8,128)(2,1)} %bitcast.8), calls=%async_computation | async-start | bytes 393216 | tf_op jit(solution)/shard_map/all_to_all | solution.py:134
  22.6 10.9 %all-to-all-done = bf16[32,24,128]{2,1,0:T(8,128)(2,1)S(1)} async-done(((bf16[32,24,128]{2,1,0:T(8,128)(2,1)}), bf16[32,24,128]{2,1,0:T(8,128)(2,1)S(1)}, u32[]{:S(2)}, u32[]{:S(2)}) %all-to-all-start) | async-done | bytes 196640 | tf_op jit(solution)/shard_map/all_to_all | solution.py:134
  34.8 10.5 %all-to-all-start.1 = ((bf16[32,24,128]{2,1,0:T(8,128)(2,1)}), bf16[32,24,128]{2,1,0:T(8,128)(2,1)S(1)}, u32[]{:S(2)}, u32[]{:S(2)}) async-start(bf16[32,24,128]{2,1,0:T(8,128)(2,1)} %bitcast.14), calls=%async_computation.1 | async-start | bytes 393216 | tf_op jit(solution)/shard_map/all_to_all | solution.py:138
  46.9 12.5 %all-to-all-done.1 = bf16[32,24,128]{2,1,0:T(8,128)(2,1)S(1)} async-done(((bf16[32,24,128]{2,1,0:T(8,128)(2,1)}), bf16[32,24,128]{2,1,0:T(8,128)(2,1)S(1)}, u32[]{:S(2)}, u32[]{:S(2)}) %all-to-all-start.1) | async-done | bytes 196640 | tf_op jit(solution)/shard_map/all_to_all | solution.py:138
  60.3 16.1 %all-gather = bf16[2304,128]{1,0:T(8,128)(2,1)S(1)} all-gather(bf16[576,128]{1,0:T(8,128)(2,1)S(1)} %fusion.8), channel_id=2, replica_groups=mesh['x'=8,'yh'=2,'core'=2,'y'=4,'z'=8] {'y'}, dimensions={0}, use_global_device_ids=true | all-gather | bytes 737280 | tf_op jit(solution)/shard_map/all_gather | solution.py:151
  76.4 3.3 %collective-permute-start = (bf16[576,256]{1,0:T(8,128)(2,1)S(1)}, bf16[576,256]{1,0:T(8,128)(2,1)S(1)}, u32[]{:S(2)}, u32[]{:S(2)}) collective-permute-start(bf16[576,256]{1,0:T(8,128)(2,1)S(1)} %pad_maximum_fusion.refs_0_), channel_id=1, source_target_pairs={{0,1},{1,2},{2,3},{3,4},{4,5},{5,6},{6,7},{7,0},{32,39},{33,32},{3... | collective-permute-start | bytes 884744 | tf_op jit(solution)/shard_map/ppermute | solution.py:178
  79.7 3.8 %collective-permute-start.1 = (bf16[576,256]{1,0:T(8,128)(2,1)S(1)}, bf16[576,256]{1,0:T(8,128)(2,1)S(1)}, u32[]{:S(2)}, u32[]{:S(2)}) collective-permute-start(bf16[576,256]{1,0:T(8,128)(2,1)S(1)} %pad_maximum_fusion.refs_0_), channel_id=1, source_target_pairs={{0,7},{1,0},{2,1},{3,2},{4,3},{5,4},{6,5},{7,6},{32,33},{33,34},{3... | collective-permute-start | bytes 884744 | tf_op jit(solution)/shard_map/ppermute | solution.py:178
  83.5 2.1 %collective-permute-start.6 = (bf16[576,256]{1,0:T(8,128)(2,1)S(1)}, bf16[576,256]{1,0:T(8,128)(2,1)S(1)}, u32[]{:S(2)}, u32[]{:S(2)}) collective-permute-start(bf16[576,256]{1,0:T(8,128)(2,1)S(1)} %pad_maximum_fusion.1.refs_7_), channel_id=1, source_target_pairs={{0,1},{1,2},{2,3},{3,4},{4,5},{5,6},{6,7},{7,0},{32,39},{33,32},{3... | collective-permute-start | bytes 884744 | tf_op jit(solution)/shard_map/ppermute | solution.py:178
  85.6 5.0 %collective-permute-start.7 = (bf16[576,256]{1,0:T(8,128)(2,1)S(1)}, bf16[576,256]{1,0:T(8,128)(2,1)S(1)}, u32[]{:S(2)}, u32[]{:S(2)}) collective-permute-start(bf16[576,256]{1,0:T(8,128)(2,1)S(1)} %pad_maximum_fusion.1.refs_7_), channel_id=1, source_target_pairs={{0,7},{1,0},{2,1},{3,2},{4,3},{5,4},{6,5},{7,6},{32,33},{33,34},{3... | collective-permute-start | bytes 884744 | tf_op jit(solution)/shard_map/ppermute | solution.py:178
  90.6 1.9 %collective-permute-start.2 = (bf16[576,256]{1,0:T(8,128)(2,1)S(1)}, bf16[576,256]{1,0:T(8,128)(2,1)}, u32[]{:S(2)}, u32[]{:S(2)}) collective-permute-start(bf16[576,256]{1,0:T(8,128)(2,1)S(1)} %collective-permute-done.refs_1_), channel_id=1, source_target_pairs={{0,1},{1,2},{2,3},{3,4},{4,5},{5,6},{6,7},{7,0},{32,39},{33,32},{3... | collective-permute-start | bytes 884744 | tf_op jit(solution)/shard_map/ppermute | solution.py:178
  92.5 5.1 %collective-permute-start.3 = (bf16[576,256]{1,0:T(8,128)(2,1)S(1)}, bf16[576,256]{1,0:T(8,128)(2,1)}, u32[]{:S(2)}, u32[]{:S(2)}) collective-permute-start(bf16[576,256]{1,0:T(8,128)(2,1)S(1)} %collective-permute-done.1.refs_2_), channel_id=1, source_target_pairs={{0,7},{1,0},{2,1},{3,2},{4,3},{5,4},{6,5},{7,6},{32,33},{33,34},{3... | collective-permute-start | bytes 884744 | tf_op jit(solution)/shard_map/ppermute | solution.py:178
  97.7 1.9 %collective-permute-start.8 = (bf16[576,256]{1,0:T(8,128)(2,1)S(1)}, bf16[576,256]{1,0:T(8,128)(2,1)}, u32[]{:S(2)}, u32[]{:S(2)}) collective-permute-start(bf16[576,256]{1,0:T(8,128)(2,1)S(1)} %collective-permute-done.6.refs_8_), channel_id=1, source_target_pairs={{0,1},{1,2},{2,3},{3,4},{4,5},{5,6},{6,7},{7,0},{32,39},{33,32},{3... | collective-permute-start | bytes 884744 | tf_op jit(solution)/shard_map/ppermute | solution.py:178
  100.3 5.1 %collective-permute-start.9 = (bf16[576,256]{1,0:T(8,128)(2,1)S(1)}, bf16[576,256]{1,0:T(8,128)(2,1)}, u32[]{:S(2)}, u32[]{:S(2)}) collective-permute-start(bf16[576,256]{1,0:T(8,128)(2,1)S(1)} %collective-permute-done.7.refs_9_), channel_id=1, source_target_pairs={{0,7},{1,0},{2,1},{3,2},{4,3},{5,4},{6,5},{7,6},{32,33},{33,34},{3... | collective-permute-start | bytes 884744 | tf_op jit(solution)/shard_map/ppermute | solution.py:178
  106.5 1.9 %collective-permute-start.4 = (bf16[576,256]{1,0:T(8,128)(2,1)}, bf16[576,256]{1,0:T(8,128)(2,1)}, u32[]{:S(2)}, u32[]{:S(2)}) collective-permute-start(bf16[576,256]{1,0:T(8,128)(2,1)} %collective-permute-done.2.refs_3_), channel_id=1, source_target_pairs={{0,1},{1,2},{2,3},{3,4},{4,5},{5,6},{6,7},{7,0},{32,39},{33,32},{3... | collective-permute-start | bytes 884744 | tf_op jit(solution)/shard_map/ppermute | solution.py:178
  108.4 5.1 %collective-permute-start.5 = (bf16[576,256]{1,0:T(8,128)(2,1)}, bf16[576,256]{1,0:T(8,128)(2,1)}, u32[]{:S(2)}, u32[]{:S(2)}) collective-permute-start(bf16[576,256]{1,0:T(8,128)(2,1)} %collective-permute-done.3.refs_4_), channel_id=1, source_target_pairs={{0,7},{1,0},{2,1},{3,2},{4,3},{5,4},{6,5},{7,6},{32,33},{33,34},{3... | collective-permute-start | bytes 884744 | tf_op jit(solution)/shard_map/ppermute | solution.py:178
  113.6 1.9 %collective-permute-start.10 = (bf16[576,256]{1,0:T(8,128)(2,1)}, bf16[576,256]{1,0:T(8,128)(2,1)}, u32[]{:S(2)}, u32[]{:S(2)}) collective-permute-start(bf16[576,256]{1,0:T(8,128)(2,1)} %collective-permute-done.8.refs_10_), channel_id=1, source_target_pairs={{0,1},{1,2},{2,3},{3,4},{4,5},{5,6},{6,7},{7,0},{32,39},{33,32},{3... | collective-permute-start | bytes 884744 | tf_op jit(solution)/shard_map/ppermute | solution.py:178
  115.5 5.1 %collective-permute-start.11 = (bf16[576,256]{1,0:T(8,128)(2,1)}, bf16[576,256]{1,0:T(8,128)(2,1)}, u32[]{:S(2)}, u32[]{:S(2)}) collective-permute-start(bf16[576,256]{1,0:T(8,128)(2,1)} %collective-permute-done.9.refs_11_), channel_id=1, source_target_pairs={{0,7},{1,0},{2,1},{3,2},{4,3},{5,4},{6,5},{7,6},{32,33},{33,34},{3... | collective-permute-start | bytes 884744 | tf_op jit(solution)/shard_map/ppermute | solution.py:178
  120.7 1.9 %broadcast_multiply_fusion.weights_ref = bf16[2048,512]{1,0:T(8,128)(2,1)S(1)} fusion(bf16[2048,512]{1,0:T(8,128)(2,1)} %param.10, bf16[2048]{0:T(1024)(128)(2,1)S(1)} %bitcast.50), kind=kLoop, calls=%fused_computation.18 | loop fusion | flops 1048576 | bytes 4198400 | tf_op jit(solution)/shard_map/mul | solution.py:155
  122.6 2.6 %collective-permute-done.11.refs_13_ = bf16[576,256]{1,0:T(8,128)(2,1)} collective-permute-done((bf16[576,256]{1,0:T(8,128)(2,1)}, bf16[576,256]{1,0:T(8,128)(2,1)}, u32[]{:S(2)}, u32[]{:S(2)}) %collective-permute-start.11) | collective-permute-done | bytes 294944 | tf_op jit(solution)/shard_map/ppermute | solution.py:178
  125.2 5.6 %collective-permute-start.13 = (bf16[576,256]{1,0:T(8,128)(2,1)}, bf16[576,256]{1,0:T(8,128)(2,1)}, u32[]{:S(2)}, u32[]{:S(2)}) collective-permute-start(bf16[576,256]{1,0:T(8,128)(2,1)} %collective-permute-done.11.refs_13_), channel_id=1, source_target_pairs={{0,7},{1,0},{2,1},{3,2},{4,3},{5,4},{6,5},{7,6},{32,33},{33,34},{3... | collective-permute-start | bytes 884744 | tf_op jit(solution)/shard_map/ppermute | solution.py:180
  131.9 1.9 %collective-permute-start.12 = (bf16[576,256]{1,0:T(8,128)(2,1)}, bf16[576,256]{1,0:T(8,128)(2,1)S(1)}, u32[]{:S(2)}, u32[]{:S(2)}) collective-permute-start(bf16[576,256]{1,0:T(8,128)(2,1)} %collective-permute-done.4.refs_5_), channel_id=1, source_target_pairs={{0,1},{1,2},{2,3},{3,4},{4,5},{5,6},{6,7},{7,0},{32,39},{33,32},{3... | collective-permute-start | bytes 884744 | tf_op jit(solution)/shard_map/ppermute | solution.py:180
  135.8 4.8 %shard_map.91 = (f32[576,512]{1,0:T(8,128)S(1)}, f32[576,512]{1,0:T(8,128)S(1)}) custom-call(s32[7]{0:T(128)S(1)} %stack.40.starts_ref, bf16[2048,512]{1,0:T(8,128)(2,1)S(1)} %broadcast_multiply_fusion.weights_ref, bf16[576,256]{1,0:T(8,128)(2,1)S(1)} %pad_maximum_fusion.refs_0_, bf16[576,256]{1,0:T(8,128)(2,1)S(1)} %collective-permute-done.refs_1_, ...), custom_call_target="tpu_custom_call" | custom-call | flops 2113929216 | bytes 8585216 | tf_op jit(solution)/shard_map/pallas_call | solution.py:100
  140.6 1.3 fusion.1
  142.9 1.5 %convolution_convert_fusion.1 = bf16[6,192,512]{2,1,0:T(8,128)(2,1)} fusion(bf16[6,192,192]{2,1,0:T(8,128)(2,1)S(1)} %copy-done.7, bf16[6,96,512]{2,1,0:T(8,128)(2,1)S(1)} %bitcast.48, bf16[6,96,512]{2,1,0:T(8,128)(2,1)S(1)} %bitcast.49), kind=kOutput, calls=%fused_computation.1 | convolution fusion | flops 229441536 | bytes 2801664 | tf_op jit(solution)/shard_map/bij,bjk->bik/dot_general | solution.py:185
  (59 shorter events, 11.7 us)
Async XLA Ops:
  0.0 33.5 %copy-start.5 = (bf16[768,768]{1,0:T(8,128)(2,1)S(1)}, bf16[768,768]{1,0:T(8,128)(2,1)}, u32[]{:S(2)}) copy-start(bf16[768,768]{1,0:T(8,128)(2,1)} %constant.176.clone) | copy-start | bytes 3538948
  0.0 22.5 %copy-start.10 = (s32[32,32,2]{1,2,0:T(2,128)S(1)}, s32[32,32,2]{1,2,0:T(2,128)}, u32[]{:S(2)}) copy-start(s32[32,32,2]{1,2,0:T(2,128)} %param.11) | copy-start | bytes 24580
  2.0 31.4 %all-to-all-start = ((bf16[32,24,128]{2,1,0:T(8,128)(2,1)}), bf16[32,24,128]{2,1,0:T(8,128)(2,1)S(1)}, u32[]{:S(2)}, u32[]{:S(2)}) async-start(bf16[32,24,128]{2,1,0:T(8,128)(2,1)} %bitcast.8), calls=%async_computation | async-start | bytes 393216 | tf_op jit(solution)/shard_map/all_to_all | solution.py:134
  33.5 26.0 %copy-start.8 = (bf16[2,576,768]{2,1,0:T(8,128)(2,1)S(1)}, bf16[2,576,768]{2,1,0:T(8,128)(2,1)}, u32[]{:S(2)}) copy-start(bf16[2,576,768]{2,1,0:T(8,128)(2,1)} %constant.178.clone) | copy-start | bytes 5308420
  34.0 25.8 %copy-start.6 = (bf16[576,768]{1,0:T(8,128)(2,1)S(1)}, bf16[576,768]{1,0:T(8,128)(2,1)}, u32[]{:S(2)}) copy-start(bf16[576,768]{1,0:T(8,128)(2,1)} %constant.179.clone) | copy-start | bytes 2654212
  34.8 24.6 %all-to-all-start.1 = ((bf16[32,24,128]{2,1,0:T(8,128)(2,1)}), bf16[32,24,128]{2,1,0:T(8,128)(2,1)S(1)}, u32[]{:S(2)}, u32[]{:S(2)}) async-start(bf16[32,24,128]{2,1,0:T(8,128)(2,1)} %bitcast.14), calls=%async_computation.1 | async-start | bytes 393216 | tf_op jit(solution)/shard_map/all_to_all | solution.py:138
  76.3 29.9 %copy-start.11 = (s32[2,16]{1,0:T(2,128)S(1)}, s32[2,16]{1,0:T(2,128)}, u32[]{:S(2)}) copy-start(s32[2,16]{1,0:T(2,128)} %param.12) | copy-start | bytes 388
  76.4 14.2 %collective-permute-start = (bf16[576,256]{1,0:T(8,128)(2,1)S(1)}, bf16[576,256]{1,0:T(8,128)(2,1)S(1)}, u32[]{:S(2)}, u32[]{:S(2)}) collective-permute-start(bf16[576,256]{1,0:T(8,128)(2,1)S(1)} %pad_maximum_fusion.refs_0_), channel_id=1, source_target_pairs={{0,1},{1,2},{2,3},{3,4},{4,5},{5,6},{6,7},{7,0},{32,39},{33,32},{3... | collective-permute-start | bytes 884744 | tf_op jit(solution)/shard_map/ppermute | solution.py:178
  79.7 12.8 %collective-permute-start.1 = (bf16[576,256]{1,0:T(8,128)(2,1)S(1)}, bf16[576,256]{1,0:T(8,128)(2,1)S(1)}, u32[]{:S(2)}, u32[]{:S(2)}) collective-permute-start(bf16[576,256]{1,0:T(8,128)(2,1)S(1)} %pad_maximum_fusion.refs_0_), channel_id=1, source_target_pairs={{0,7},{1,0},{2,1},{3,2},{4,3},{5,4},{6,5},{7,6},{32,33},{33,34},{3... | collective-permute-start | bytes 884744 | tf_op jit(solution)/shard_map/ppermute | solution.py:178
  83.5 14.2 %collective-permute-start.6 = (bf16[576,256]{1,0:T(8,128)(2,1)S(1)}, bf16[576,256]{1,0:T(8,128)(2,1)S(1)}, u32[]{:S(2)}, u32[]{:S(2)}) collective-permute-start(bf16[576,256]{1,0:T(8,128)(2,1)S(1)} %pad_maximum_fusion.1.refs_7_), channel_id=1, source_target_pairs={{0,1},{1,2},{2,3},{3,4},{4,5},{5,6},{6,7},{7,0},{32,39},{33,32},{3... | collective-permute-start | bytes 884744 | tf_op jit(solution)/shard_map/ppermute | solution.py:178
  85.6 14.8 %collective-permute-start.7 = (bf16[576,256]{1,0:T(8,128)(2,1)S(1)}, bf16[576,256]{1,0:T(8,128)(2,1)S(1)}, u32[]{:S(2)}, u32[]{:S(2)}) collective-permute-start(bf16[576,256]{1,0:T(8,128)(2,1)S(1)} %pad_maximum_fusion.1.refs_7_), channel_id=1, source_target_pairs={{0,7},{1,0},{2,1},{3,2},{4,3},{5,4},{6,5},{7,6},{32,33},{33,34},{3... | collective-permute-start | bytes 884744 | tf_op jit(solution)/shard_map/ppermute | solution.py:178
  90.6 15.9 %collective-permute-start.2 = (bf16[576,256]{1,0:T(8,128)(2,1)S(1)}, bf16[576,256]{1,0:T(8,128)(2,1)}, u32[]{:S(2)}, u32[]{:S(2)}) collective-permute-start(bf16[576,256]{1,0:T(8,128)(2,1)S(1)} %collective-permute-done.refs_1_), channel_id=1, source_target_pairs={{0,1},{1,2},{2,3},{3,4},{4,5},{5,6},{6,7},{7,0},{32,39},{33,32},{3... | collective-permute-start | bytes 884744 | tf_op jit(solution)/shard_map/ppermute | solution.py:178
  92.5 15.9 %collective-permute-start.3 = (bf16[576,256]{1,0:T(8,128)(2,1)S(1)}, bf16[576,256]{1,0:T(8,128)(2,1)}, u32[]{:S(2)}, u32[]{:S(2)}) collective-permute-start(bf16[576,256]{1,0:T(8,128)(2,1)S(1)} %collective-permute-done.1.refs_2_), channel_id=1, source_target_pairs={{0,7},{1,0},{2,1},{3,2},{4,3},{5,4},{6,5},{7,6},{32,33},{33,34},{3... | collective-permute-start | bytes 884744 | tf_op jit(solution)/shard_map/ppermute | solution.py:178
  97.7 15.9 %collective-permute-start.8 = (bf16[576,256]{1,0:T(8,128)(2,1)S(1)}, bf16[576,256]{1,0:T(8,128)(2,1)}, u32[]{:S(2)}, u32[]{:S(2)}) collective-permute-start(bf16[576,256]{1,0:T(8,128)(2,1)S(1)} %collective-permute-done.6.refs_8_), channel_id=1, source_target_pairs={{0,1},{1,2},{2,3},{3,4},{4,5},{5,6},{6,7},{7,0},{32,39},{33,32},{3... | collective-permute-start | bytes 884744 | tf_op jit(solution)/shard_map/ppermute | solution.py:178
  100.3 15.2 %collective-permute-start.9 = (bf16[576,256]{1,0:T(8,128)(2,1)S(1)}, bf16[576,256]{1,0:T(8,128)(2,1)}, u32[]{:S(2)}, u32[]{:S(2)}) collective-permute-start(bf16[576,256]{1,0:T(8,128)(2,1)S(1)} %collective-permute-done.7.refs_9_), channel_id=1, source_target_pairs={{0,7},{1,0},{2,1},{3,2},{4,3},{5,4},{6,5},{7,6},{32,33},{33,34},{3... | collective-permute-start | bytes 884744 | tf_op jit(solution)/shard_map/ppermute | solution.py:178
  106.5 25.4 %collective-permute-start.4 = (bf16[576,256]{1,0:T(8,128)(2,1)}, bf16[576,256]{1,0:T(8,128)(2,1)}, u32[]{:S(2)}, u32[]{:S(2)}) collective-permute-start(bf16[576,256]{1,0:T(8,128)(2,1)} %collective-permute-done.2.refs_3_), channel_id=1, source_target_pairs={{0,1},{1,2},{2,3},{3,4},{4,5},{5,6},{6,7},{7,0},{32,39},{33,32},{3... | collective-permute-start | bytes 884744 | tf_op jit(solution)/shard_map/ppermute | solution.py:178
  108.4 25.4 %collective-permute-start.5 = (bf16[576,256]{1,0:T(8,128)(2,1)}, bf16[576,256]{1,0:T(8,128)(2,1)}, u32[]{:S(2)}, u32[]{:S(2)}) collective-permute-start(bf16[576,256]{1,0:T(8,128)(2,1)} %collective-permute-done.3.refs_4_), channel_id=1, source_target_pairs={{0,7},{1,0},{2,1},{3,2},{4,3},{5,4},{6,5},{7,6},{32,33},{33,34},{3... | collective-permute-start | bytes 884744 | tf_op jit(solution)/shard_map/ppermute | solution.py:178
  113.6 20.3 %collective-permute-start.10 = (bf16[576,256]{1,0:T(8,128)(2,1)}, bf16[576,256]{1,0:T(8,128)(2,1)}, u32[]{:S(2)}, u32[]{:S(2)}) collective-permute-start(bf16[576,256]{1,0:T(8,128)(2,1)} %collective-permute-done.8.refs_10_), channel_id=1, source_target_pairs={{0,1},{1,2},{2,3},{3,4},{4,5},{5,6},{6,7},{7,0},{32,39},{33,32},{3... | collective-permute-start | bytes 884744 | tf_op jit(solution)/shard_map/ppermute | solution.py:178
  115.5 9.7 %collective-permute-start.11 = (bf16[576,256]{1,0:T(8,128)(2,1)}, bf16[576,256]{1,0:T(8,128)(2,1)}, u32[]{:S(2)}, u32[]{:S(2)}) collective-permute-start(bf16[576,256]{1,0:T(8,128)(2,1)} %collective-permute-done.9.refs_11_), channel_id=1, source_target_pairs={{0,7},{1,0},{2,1},{3,2},{4,3},{5,4},{6,5},{7,6},{32,33},{33,34},{3... | collective-permute-start | bytes 884744 | tf_op jit(solution)/shard_map/ppermute | solution.py:178
  120.7 10.1 %copy-start.9 = (s32[6,192]{1,0:T(8,128)S(1)}, s32[6,192]{1,0:T(8,128)}, u32[]{:S(2)}) copy-start(s32[6,192]{1,0:T(8,128)} %constant.180.clone) | copy-start | bytes 13828
  125.2 15.4 %collective-permute-start.13 = (bf16[576,256]{1,0:T(8,128)(2,1)}, bf16[576,256]{1,0:T(8,128)(2,1)}, u32[]{:S(2)}, u32[]{:S(2)}) collective-permute-start(bf16[576,256]{1,0:T(8,128)(2,1)} %collective-permute-done.11.refs_13_), channel_id=1, source_target_pairs={{0,7},{1,0},{2,1},{3,2},{4,3},{5,4},{6,5},{7,6},{32,33},{33,34},{3... | collective-permute-start | bytes 884744 | tf_op jit(solution)/shard_map/ppermute | solution.py:180
  131.9 10.0 %collective-permute-start.12 = (bf16[576,256]{1,0:T(8,128)(2,1)}, bf16[576,256]{1,0:T(8,128)(2,1)S(1)}, u32[]{:S(2)}, u32[]{:S(2)}) collective-permute-start(bf16[576,256]{1,0:T(8,128)(2,1)} %collective-permute-done.4.refs_5_), channel_id=1, source_target_pairs={{0,1},{1,2},{2,3},{3,4},{4,5},{5,6},{6,7},{7,0},{32,39},{33,32},{3... | collective-permute-start | bytes 884744 | tf_op jit(solution)/shard_map/ppermute | solution.py:180
  133.9 1.0 copy-start.2
  141.8 1.1 copy-start.7
  (4 other events, 3.3 us)

commit v6 on v4

--- a/solution.py
+++ b/solution.py
@@ -101,16 +101,19 @@
     diff = diff.astype(bf)
 
     gathered = lax.all_gather(diff, "y", axis=0, tiled=False)
-    pieces = [jnp.concatenate([gathered[2 * r], gathered[2 * r + 1]], 1) for r in range(2)]
+    gathered = gathered.reshape(2, 2, NP * PER, LANES)
+    e = y % 2
+    mine = lax.dynamic_index_in_dim(gathered, e, 1, keepdims=False).reshape(-1, LANES)
+    pair = lax.dynamic_index_in_dim(gathered, 1 - e, 1, keepdims=False).reshape(-1, LANES)
 
     col_mask = lax.dynamic_index_in_dim(int_pattern, v * cols // TP, 1, keepdims=False)
     weighted = integrals * jnp.repeat(col_mask, TP).astype(bf)[:, None]
 
     sign = 1 - 2 * lax.axis_index("core")
 
-    def term(c, distance):
-        start = lax.rem(z + sign * distance + NZ, NZ) * width
-        return dot(c, lax.dynamic_slice_in_dim(weighted, start, width, 0))
+    def term(c, distance, half):
+        start = lax.rem(z + sign * distance + NZ, NZ) * width + half * LANES
+        return dot(c, lax.dynamic_slice_in_dim(weighted, start, LANES, 0))
 
     def shift(step):
         return [
@@ -120,16 +123,32 @@
         ]
 
     ways = (shift(1), shift(-1))
-    front = [list(pieces), list(pieces)]
-    totals = [term(c, 0) for c in pieces]
-    for step in range(1, NZ // 2 + 1):
-        for i in range(2):
-            for w in range(2):
-                if step == NZ // 2 and w != i:
-                    continue
-                front[w][i] = lax.ppermute(front[w][i], ("core", "z"), ways[w])
-                totals[i] = totals[i] + term(front[w][i], -step if w == 0 else step)
-    both = jnp.concatenate([t.astype(bf).reshape(OCC, NP * HALF, cols) for t in totals], 1)
+    def hop(c, w):
+        return lax.ppermute(c, ("core", "z"), ways[w])
+
+    def across(c):
+        return lax.ppermute(c, "y", [(i, i ^ 1) for i in range(NY)])
+
+    front, other = [mine, mine], [pair, pair]
+    total = term(mine, 0, e) + term(pair, 0, 1 - e)
+    for step in range(1, 4):
+        for w in range(2):
+            d = -step if w == 0 else step
+            front[w] = hop(front[w], w)
+            total = total + term(front[w], d, e)
+            if step < 3:
+                ready = other[w]
+                if step == 2:
+                    ready, _ = lax.optimization_barrier((ready, front[w]))
+                other[w] = hop(ready, w)
+            else:
+                other[w] = across(front[w])
+            total = total + term(other[w], d, 1 - e)
+    far = hop(front[0], 0)
+    total = total + term(far, NZ // 2, e) + term(across(far), NZ // 2, 1 - e)
+    both = (
+        total.astype(bf).reshape(2, OCC, NP * HALF, cols).transpose(1, 0, 2, 3)
+    ).reshape(OCC, NP * OCC, cols)
     out = jnp.einsum(
         "bij,bjk->bik", jnp.asarray(PLACE, bf), both, preferred_element_type=jnp.float32
     )

time: 143 us -> 152 us (1.063)
  the two profiles are of different devices: /device:TPU:2 before, /device:TPU:16 now
where the time goes in v6:
time: 152 us; the launch traced here: 151 us
  starting transfers between devices  75.2 us (49%)
  waiting for transfers between devices  39.5 us (26%)
  blocking collectives  15.8 us (10%)
  matrix products  12.7 us (8%)
  other arithmetic  3.69 us (2%)
  local copies, waits for them, and re-layouts  3.31 us (2%)
    ppermute x11, starting transfers between devices, hop(): return lax.ppermute(c, ('core', 'z'), ways[w])  36.1 us
    all_to_all x1, starting transfers between devices, body(): held = lax.all_to_all(first, VIRT, split_axis=0, concat_axis=0, tiled=True)  20.6 us
    all_gather x1, blocking collectives, body(): gathered = lax.all_gather(diff, 'y', axis=0, tiled=False)  15.8 us
    ppermute x11, waiting for transfers between devices, hop(): return lax.ppermute(c, ('core', 'z'), ways[w])  15.7 us
    all_to_all x1, waiting for transfers between devices, body(): lax.all_to_all(second, PAIR, split_axis=0, concat_axis=0, tiled=True)  12.4 us
    dot_general x21, matrix products, dot(): return jnp.dot(a, b, preferred_element_type=jnp.float32)  11.2 us
    all_to_all x1, starting transfers between devices, body(): lax.all_to_all(second, PAIR, split_axis=0, concat_axis=0, tiled=True)  10.2 us
    ppermute x3, starting transfers between devices, across(): return lax.ppermute(c, 'y', [(i, i ^ 1) for i in range(NY)])  8.35 us
  transfers between devices with their start and end apart: 16, of which 7 were waited for; matrix products, arithmetic and copies ran while one was open for 8% of the time, Pallas kernels for 0%

profile of v6, /device:TPU:16, one launch (start us, length us, event | category | flops | bytes accessed | tf_op | source)
XLA Modules:
  0.0 150.9 jit_solution(12015324849709732188)
XLA Ops:
  2.0 20.6 %all-to-all-start = ((bf16[32,24,128]{2,1,0:T(8,128)(2,1)}), bf16[32,24,128]{2,1,0:T(8,128)(2,1)S(1)}, u32[]{:S(2)}, u32[]{:S(2)}) async-start(bf16[32,24,128]{2,1,0:T(8,128)(2,1)} %bitcast.1), calls=%async_computation | async-start | bytes 393216 | tf_op jit(solution)/shard_map/all_to_all | solution.py:86
  26.2 6.2 %all-to-all-done = bf16[32,24,128]{2,1,0:T(8,128)(2,1)S(1)} async-done(((bf16[32,24,128]{2,1,0:T(8,128)(2,1)}), bf16[32,24,128]{2,1,0:T(8,128)(2,1)S(1)}, u32[]{:S(2)}, u32[]{:S(2)}) %all-to-all-start) | async-done | bytes 196640 | tf_op jit(solution)/shard_map/all_to_all | solution.py:86
  33.7 10.2 %all-to-all-start.1 = ((bf16[32,24,128]{2,1,0:T(8,128)(2,1)}), bf16[32,24,128]{2,1,0:T(8,128)(2,1)S(1)}, u32[]{:S(2)}, u32[]{:S(2)}) async-start(bf16[32,24,128]{2,1,0:T(8,128)(2,1)} %bitcast.7), calls=%async_computation.1 | async-start | bytes 393216 | tf_op jit(solution)/shard_map/all_to_all | solution.py:90
  43.9 2.0 %broadcast_multiply_fusion = bf16[2048,512]{1,0:T(8,128)(2,1)S(1)} fusion(bf16[2048,512]{1,0:T(8,128)(2,1)} %param.10, bf16[2048]{0:T(1024)(128)(2,1)S(1)} %bitcast.72), kind=kLoop, calls=%fused_computation.25 | loop fusion | flops 1048576 | bytes 4198400 | tf_op jit(solution)/shard_map/mul | solution.py:110
  45.9 12.4 %all-to-all-done.1 = bf16[32,24,128]{2,1,0:T(8,128)(2,1)S(1)} async-done(((bf16[32,24,128]{2,1,0:T(8,128)(2,1)}), bf16[32,24,128]{2,1,0:T(8,128)(2,1)S(1)}, u32[]{:S(2)}, u32[]{:S(2)}) %all-to-all-start.1) | async-done | bytes 196640 | tf_op jit(solution)/shard_map/all_to_all | solution.py:90
  60.3 15.8 %all-gather = bf16[2304,128]{1,0:T(8,128)(2,1)S(1)} all-gather(bf16[576,128]{1,0:T(8,128)(2,1)S(1)} %fusion.10), channel_id=2, replica_groups=mesh['x'=8,'yh'=2,'core'=2,'y'=4,'z'=8] {'y'}, dimensions={0}, use_global_device_ids=true | all-gather | bytes 737280 | tf_op jit(solution)/shard_map/all_gather | solution.py:103
  76.2 3.0 %collective-permute-start.1 = (bf16[1152,128]{1,0:T(8,128)(2,1)S(1)}, bf16[1152,128]{1,0:T(8,128)(2,1)S(1)}, u32[]{:S(2)}, u32[]{:S(2)}) collective-permute-start(bf16[1152,128]{1,0:T(8,128)(2,1)S(1)} %bitcast.68), channel_id=1, source_target_pairs={{0,1},{1,2},{2,3},{3,4},{4,5},{5,6},{6,7},{7,0},{32,39},{33,32},{3... | collective-permute-start | bytes 884744 | tf_op jit(solution)/shard_map/ppermute | solution.py:127
  79.1 4.1 %collective-permute-start.3 = (bf16[1152,128]{1,0:T(8,128)(2,1)S(1)}, bf16[1152,128]{1,0:T(8,128)(2,1)S(1)}, u32[]{:S(2)}, u32[]{:S(2)}) collective-permute-start(bf16[1152,128]{1,0:T(8,128)(2,1)S(1)} %bitcast.69), channel_id=1, source_target_pairs={{0,7},{1,0},{2,1},{3,2},{4,3},{5,4},{6,5},{7,6},{32,33},{33,34},{3... | collective-permute-start | bytes 884744 | tf_op jit(solution)/shard_map/ppermute | solution.py:127
  83.2 1.9 %collective-permute-start.2 = (bf16[1152,128]{1,0:T(8,128)(2,1)S(1)}, bf16[1152,128]{1,0:T(8,128)(2,1)S(1)}, u32[]{:S(2)}, u32[]{:S(2)}) collective-permute-start(bf16[1152,128]{1,0:T(8,128)(2,1)S(1)} %bitcast.65), channel_id=1, source_target_pairs={{0,7},{1,0},{2,1},{3,2},{4,3},{5,4},{6,5},{7,6},{32,33},{33,34},{3... | collective-permute-start | bytes 884744 | tf_op jit(solution)/shard_map/ppermute | solution.py:127
  85.2 3.9 %collective-permute-start = (bf16[1152,128]{1,0:T(8,128)(2,1)S(1)}, bf16[1152,128]{1,0:T(8,128)(2,1)S(1)}, u32[]{:S(2)}, u32[]{:S(2)}) collective-permute-start(bf16[1152,128]{1,0:T(8,128)(2,1)S(1)} %bitcast.66), channel_id=1, source_target_pairs={{0,1},{1,2},{2,3},{3,4},{4,5},{5,6},{6,7},{7,0},{32,39},{33,32},{3... | collective-permute-start | bytes 884744 | tf_op jit(solution)/shard_map/ppermute | solution.py:127
  90.0 4.1 %collective-permute-done.2 = bf16[1152,128]{1,0:T(8,128)(2,1)S(1)} collective-permute-done((bf16[1152,128]{1,0:T(8,128)(2,1)S(1)}, bf16[1152,128]{1,0:T(8,128)(2,1)S(1)}, u32[]{:S(2)}, u32[]{:S(2)}) %collective-permute-start.2) | collective-permute-done | bytes 294944 | tf_op jit(solution)/shard_map/ppermute | solution.py:127
  94.1 5.3 %collective-permute-start.6 = (bf16[1152,128]{1,0:T(8,128)(2,1)S(1)}, bf16[1152,128]{1,0:T(8,128)(2,1)S(1)}, u32[]{:S(2)}, u32[]{:S(2)}) collective-permute-start(bf16[1152,128]{1,0:T(8,128)(2,1)S(1)} %collective-permute-done.2), channel_id=1, source_target_pairs={{0,7},{1,0},{2,1},{3,2},{4,3},{5,4},{6,5},{7,6},{32,33},{33,34},{3... | collective-permute-start | bytes 884744 | tf_op jit(solution)/shard_map/ppermute | solution.py:127
  99.9 1.9 %collective-permute-start.4 = (bf16[1152,128]{1,0:T(8,128)(2,1)S(1)}, bf16[1152,128]{1,0:T(8,128)(2,1)S(1)}, u32[]{:S(2)}, u32[]{:S(2)}) collective-permute-start(bf16[1152,128]{1,0:T(8,128)(2,1)S(1)} %collective-permute-done), channel_id=1, source_target_pairs={{0,1},{1,2},{2,3},{3,4},{4,5},{5,6},{6,7},{7,0},{32,39},{33,32},{3... | collective-permute-start | bytes 884744 | tf_op jit(solution)/shard_map/ppermute | solution.py:127
  102.7 7.0 %collective-permute-done.4 = bf16[1152,128]{1,0:T(8,128)(2,1)S(1)} collective-permute-done((bf16[1152,128]{1,0:T(8,128)(2,1)S(1)}, bf16[1152,128]{1,0:T(8,128)(2,1)S(1)}, u32[]{:S(2)}, u32[]{:S(2)}) %collective-permute-start.4) | collective-permute-done | bytes 294944 | tf_op jit(solution)/shard_map/ppermute | solution.py:127
  111.6 5.1 %collective-permute-start.7 = (bf16[1152,128]{1,0:T(8,128)(2,1)S(1)}, bf16[1152,128]{1,0:T(8,128)(2,1)S(1)}, u32[]{:S(2)}, u32[]{:S(2)}) collective-permute-start(bf16[1152,128]{1,0:T(8,128)(2,1)S(1)} %collective-permute-done.3), channel_id=1, source_target_pairs={{0,7},{1,0},{2,1},{3,2},{4,3},{5,4},{6,5},{7,6},{32,33},{33,34},{3... | collective-permute-start | bytes 884744 | tf_op jit(solution)/shard_map/ppermute | solution.py:127
  116.7 1.9 %collective-permute-start.8 = (bf16[1152,128]{1,0:T(8,128)(2,1)S(1)}, bf16[1152,128]{1,0:T(8,128)(2,1)S(1)}, u32[]{:S(2)}, u32[]{:S(2)}) collective-permute-start(bf16[1152,128]{1,0:T(8,128)(2,1)S(1)} %collective-permute-done.4), channel_id=1, source_target_pairs={{0,1},{1,2},{2,3},{3,4},{4,5},{5,6},{6,7},{7,0},{32,39},{33,32},{3... | collective-permute-start | bytes 884744 | tf_op jit(solution)/shard_map/ppermute | solution.py:127
  118.7 5.1 %collective-permute-start.10 = (bf16[1152,128]{1,0:T(8,128)(2,1)S(1)}, bf16[1152,128]{1,0:T(8,128)(2,1)S(1)}, u32[]{:S(2)}, u32[]{:S(2)}) collective-permute-start(bf16[1152,128]{1,0:T(8,128)(2,1)S(1)} %collective-permute-done.6), channel_id=1, source_target_pairs={{0,7},{1,0},{2,1},{3,2},{4,3},{5,4},{6,5},{7,6},{32,33},{33,34},{3... | collective-permute-start | bytes 884744 | tf_op jit(solution)/shard_map/ppermute | solution.py:127
  124.4 2.2 %collective-permute-done.8 = bf16[1152,128]{1,0:T(8,128)(2,1)S(1)} collective-permute-done((bf16[1152,128]{1,0:T(8,128)(2,1)S(1)}, bf16[1152,128]{1,0:T(8,128)(2,1)S(1)}, u32[]{:S(2)}, u32[]{:S(2)}) %collective-permute-start.8) | collective-permute-done | bytes 294944 | tf_op jit(solution)/shard_map/ppermute | solution.py:127
  126.6 3.9 %collective-permute-start.9 = (bf16[1152,128]{1,0:T(8,128)(2,1)S(1)}, bf16[1152,128]{1,0:T(8,128)(2,1)S(1)}, u32[]{:S(2)}, u32[]{:S(2)}) collective-permute-start(bf16[1152,128]{1,0:T(8,128)(2,1)S(1)} %collective-permute-done.8), channel_id=1, source_target_pairs={{0,8},{8,0},{16,24},{24,16},{1,9},{9,1},{17,25},{25,17},{2,10},{10... | collective-permute-start | bytes 884744 | tf_op jit(solution)/shard_map/ppermute | solution.py:130
  130.5 1.9 %collective-permute-start.12 = (bf16[1152,128]{1,0:T(8,128)(2,1)S(1)}, bf16[1152,128]{1,0:T(8,128)(2,1)S(1)}, u32[]{:S(2)}, u32[]{:S(2)}) collective-permute-start(bf16[1152,128]{1,0:T(8,128)(2,1)S(1)} %collective-permute-done.8), channel_id=1, source_target_pairs={{0,1},{1,2},{2,3},{3,4},{4,5},{5,6},{6,7},{7,0},{32,39},{33,32},{3... | collective-permute-start | bytes 884744 | tf_op jit(solution)/shard_map/ppermute | solution.py:127
  132.4 2.5 %collective-permute-start.11 = (bf16[1152,128]{1,0:T(8,128)(2,1)S(1)}, bf16[1152,128]{1,0:T(8,128)(2,1)S(1)}, u32[]{:S(2)}, u32[]{:S(2)}) collective-permute-start(bf16[1152,128]{1,0:T(8,128)(2,1)S(1)} %collective-permute-done.10), channel_id=1, source_target_pairs={{0,8},{8,0},{16,24},{24,16},{1,9},{9,1},{17,25},{25,17},{2,10},{10... | collective-permute-start | bytes 884744 | tf_op jit(solution)/shard_map/ppermute | solution.py:130
  137.8 2.5 %collective-permute-done.12 = bf16[1152,128]{1,0:T(8,128)(2,1)S(1)} collective-permute-done((bf16[1152,128]{1,0:T(8,128)(2,1)S(1)}, bf16[1152,128]{1,0:T(8,128)(2,1)S(1)}, u32[]{:S(2)}, u32[]{:S(2)}) %collective-permute-start.12) | collective-permute-done | bytes 294944 | tf_op jit(solution)/shard_map/ppermute | solution.py:127
  140.3 1.9 %collective-permute-start.13 = (bf16[1152,128]{1,0:T(8,128)(2,1)S(1)}, bf16[1152,128]{1,0:T(8,128)(2,1)S(1)}, u32[]{:S(2)}, u32[]{:S(2)}) collective-permute-start(bf16[1152,128]{1,0:T(8,128)(2,1)S(1)} %collective-permute-done.12), channel_id=1, source_target_pairs={{0,8},{8,0},{16,24},{24,16},{1,9},{9,1},{17,25},{25,17},{2,10},{10... | collective-permute-start | bytes 884744 | tf_op jit(solution)/shard_map/ppermute | solution.py:130
  143.7 5.2 %collective-permute-done.13 = bf16[1152,128]{1,0:T(8,128)(2,1)S(1)} collective-permute-done((bf16[1152,128]{1,0:T(8,128)(2,1)S(1)}, bf16[1152,128]{1,0:T(8,128)(2,1)S(1)}, u32[]{:S(2)}, u32[]{:S(2)}) %collective-permute-start.13) | collective-permute-done | bytes 294944 | tf_op jit(solution)/shard_map/ppermute | solution.py:130
  (53 shorter events, 19.6 us)
Async XLA Ops:
  0.0 0.9 copy-start
  0.0 32.4 %copy-start.1 = (bf16[768,768]{1,0:T(8,128)(2,1)S(1)}, bf16[768,768]{1,0:T(8,128)(2,1)}, u32[]{:S(2)}) copy-start(bf16[768,768]{1,0:T(8,128)(2,1)} %constant.191.clone) | copy-start | bytes 3538948
  2.0 30.4 %all-to-all-start = ((bf16[32,24,128]{2,1,0:T(8,128)(2,1)}), bf16[32,24,128]{2,1,0:T(8,128)(2,1)S(1)}, u32[]{:S(2)}, u32[]{:S(2)}) async-start(bf16[32,24,128]{2,1,0:T(8,128)(2,1)} %bitcast.1), calls=%async_computation | async-start | bytes 393216 | tf_op jit(solution)/shard_map/all_to_all | solution.py:86
  33.7 24.6 %all-to-all-start.1 = ((bf16[32,24,128]{2,1,0:T(8,128)(2,1)}), bf16[32,24,128]{2,1,0:T(8,128)(2,1)S(1)}, u32[]{:S(2)}, u32[]{:S(2)}) async-start(bf16[32,24,128]{2,1,0:T(8,128)(2,1)} %bitcast.7), calls=%async_computation.1 | async-start | bytes 393216 | tf_op jit(solution)/shard_map/all_to_all | solution.py:90
  43.9 16.0 %copy-start.2 = (bf16[576,768]{1,0:T(8,128)(2,1)S(1)}, bf16[576,768]{1,0:T(8,128)(2,1)}, u32[]{:S(2)}) copy-start(bf16[576,768]{1,0:T(8,128)(2,1)} %constant.194.clone) | copy-start | bytes 2654212
  76.2 25.6 %collective-permute-start.1 = (bf16[1152,128]{1,0:T(8,128)(2,1)S(1)}, bf16[1152,128]{1,0:T(8,128)(2,1)S(1)}, u32[]{:S(2)}, u32[]{:S(2)}) collective-permute-start(bf16[1152,128]{1,0:T(8,128)(2,1)S(1)} %bitcast.68), channel_id=1, source_target_pairs={{0,1},{1,2},{2,3},{3,4},{4,5},{5,6},{6,7},{7,0},{32,39},{33,32},{3... | collective-permute-start | bytes 884744 | tf_op jit(solution)/shard_map/ppermute | solution.py:127
  79.1 23.1 %collective-permute-start.3 = (bf16[1152,128]{1,0:T(8,128)(2,1)S(1)}, bf16[1152,128]{1,0:T(8,128)(2,1)S(1)}, u32[]{:S(2)}, u32[]{:S(2)}) collective-permute-start(bf16[1152,128]{1,0:T(8,128)(2,1)S(1)} %bitcast.69), channel_id=1, source_target_pairs={{0,7},{1,0},{2,1},{3,2},{4,3},{5,4},{6,5},{7,6},{32,33},{33,34},{3... | collective-permute-start | bytes 884744 | tf_op jit(solution)/shard_map/ppermute | solution.py:127
  83.2 10.8 %collective-permute-start.2 = (bf16[1152,128]{1,0:T(8,128)(2,1)S(1)}, bf16[1152,128]{1,0:T(8,128)(2,1)S(1)}, u32[]{:S(2)}, u32[]{:S(2)}) collective-permute-start(bf16[1152,128]{1,0:T(8,128)(2,1)S(1)} %bitcast.65), channel_id=1, source_target_pairs={{0,7},{1,0},{2,1},{3,2},{4,3},{5,4},{6,5},{7,6},{32,33},{33,34},{3... | collective-permute-start | bytes 884744 | tf_op jit(solution)/shard_map/ppermute | solution.py:127
  85.2 14.7 %collective-permute-start = (bf16[1152,128]{1,0:T(8,128)(2,1)S(1)}, bf16[1152,128]{1,0:T(8,128)(2,1)S(1)}, u32[]{:S(2)}, u32[]{:S(2)}) collective-permute-start(bf16[1152,128]{1,0:T(8,128)(2,1)S(1)} %bitcast.66), channel_id=1, source_target_pairs={{0,1},{1,2},{2,3},{3,4},{4,5},{5,6},{6,7},{7,0},{32,39},{33,32},{3... | collective-permute-start | bytes 884744 | tf_op jit(solution)/shard_map/ppermute | solution.py:127
  94.1 17.5 %collective-permute-start.6 = (bf16[1152,128]{1,0:T(8,128)(2,1)S(1)}, bf16[1152,128]{1,0:T(8,128)(2,1)S(1)}, u32[]{:S(2)}, u32[]{:S(2)}) collective-permute-start(bf16[1152,128]{1,0:T(8,128)(2,1)S(1)} %collective-permute-done.2), channel_id=1, source_target_pairs={{0,7},{1,0},{2,1},{3,2},{4,3},{5,4},{6,5},{7,6},{32,33},{33,34},{3... | collective-permute-start | bytes 884744 | tf_op jit(solution)/shard_map/ppermute | solution.py:127
  99.9 9.8 %collective-permute-start.4 = (bf16[1152,128]{1,0:T(8,128)(2,1)S(1)}, bf16[1152,128]{1,0:T(8,128)(2,1)S(1)}, u32[]{:S(2)}, u32[]{:S(2)}) collective-permute-start(bf16[1152,128]{1,0:T(8,128)(2,1)S(1)} %collective-permute-done), channel_id=1, source_target_pairs={{0,1},{1,2},{2,3},{3,4},{4,5},{5,6},{6,7},{7,0},{32,39},{33,32},{3... | collective-permute-start | bytes 884744 | tf_op jit(solution)/shard_map/ppermute | solution.py:127
  109.7 25.3 %collective-permute-start.5 = (bf16[1152,128]{1,0:T(8,128)(2,1)S(1)}, bf16[1152,128]{1,0:T(8,128)(2,1)S(1)}, u32[]{:S(2)}, u32[]{:S(2)}) collective-permute-start(bf16[1152,128]{1,0:T(8,128)(2,1)S(1)} %collective-permute-done.1), channel_id=1, source_target_pairs={{0,1},{1,2},{2,3},{3,4},{4,5},{5,6},{6,7},{7,0},{32,39},{33,32},{3... | collective-permute-start | bytes 884744 | tf_op jit(solution)/shard_map/ppermute | solution.py:127
  111.6 23.8 %collective-permute-start.7 = (bf16[1152,128]{1,0:T(8,128)(2,1)S(1)}, bf16[1152,128]{1,0:T(8,128)(2,1)S(1)}, u32[]{:S(2)}, u32[]{:S(2)}) collective-permute-start(bf16[1152,128]{1,0:T(8,128)(2,1)S(1)} %collective-permute-done.3), channel_id=1, source_target_pairs={{0,7},{1,0},{2,1},{3,2},{4,3},{5,4},{6,5},{7,6},{32,33},{33,34},{3... | collective-permute-start | bytes 884744 | tf_op jit(solution)/shard_map/ppermute | solution.py:127
  116.7 9.8 %collective-permute-start.8 = (bf16[1152,128]{1,0:T(8,128)(2,1)S(1)}, bf16[1152,128]{1,0:T(8,128)(2,1)S(1)}, u32[]{:S(2)}, u32[]{:S(2)}) collective-permute-start(bf16[1152,128]{1,0:T(8,128)(2,1)S(1)} %collective-permute-done.4), channel_id=1, source_target_pairs={{0,1},{1,2},{2,3},{3,4},{4,5},{5,6},{6,7},{7,0},{32,39},{33,32},{3... | collective-permute-start | bytes 884744 | tf_op jit(solution)/shard_map/ppermute | solution.py:127
  118.7 13.7 %collective-permute-start.10 = (bf16[1152,128]{1,0:T(8,128)(2,1)S(1)}, bf16[1152,128]{1,0:T(8,128)(2,1)S(1)}, u32[]{:S(2)}, u32[]{:S(2)}) collective-permute-start(bf16[1152,128]{1,0:T(8,128)(2,1)S(1)} %collective-permute-done.6), channel_id=1, source_target_pairs={{0,7},{1,0},{2,1},{3,2},{4,3},{5,4},{6,5},{7,6},{32,33},{33,34},{3... | collective-permute-start | bytes 884744 | tf_op jit(solution)/shard_map/ppermute | solution.py:127
  126.6 15.7 %collective-permute-start.9 = (bf16[1152,128]{1,0:T(8,128)(2,1)S(1)}, bf16[1152,128]{1,0:T(8,128)(2,1)S(1)}, u32[]{:S(2)}, u32[]{:S(2)}) collective-permute-start(bf16[1152,128]{1,0:T(8,128)(2,1)S(1)} %collective-permute-done.8), channel_id=1, source_target_pairs={{0,8},{8,0},{16,24},{24,16},{1,9},{9,1},{17,25},{25,17},{2,10},{10... | collective-permute-start | bytes 884744 | tf_op jit(solution)/shard_map/ppermute | solution.py:130
  130.5 9.8 %collective-permute-start.12 = (bf16[1152,128]{1,0:T(8,128)(2,1)S(1)}, bf16[1152,128]{1,0:T(8,128)(2,1)S(1)}, u32[]{:S(2)}, u32[]{:S(2)}) collective-permute-start(bf16[1152,128]{1,0:T(8,128)(2,1)S(1)} %collective-permute-done.8), channel_id=1, source_target_pairs={{0,1},{1,2},{2,3},{3,4},{4,5},{5,6},{6,7},{7,0},{32,39},{33,32},{3... | collective-permute-start | bytes 884744 | tf_op jit(solution)/shard_map/ppermute | solution.py:127
  132.4 10.8 %collective-permute-start.11 = (bf16[1152,128]{1,0:T(8,128)(2,1)S(1)}, bf16[1152,128]{1,0:T(8,128)(2,1)S(1)}, u32[]{:S(2)}, u32[]{:S(2)}) collective-permute-start(bf16[1152,128]{1,0:T(8,128)(2,1)S(1)} %collective-permute-done.10), channel_id=1, source_target_pairs={{0,8},{8,0},{16,24},{24,16},{1,9},{9,1},{17,25},{25,17},{2,10},{10... | collective-permute-start | bytes 884744 | tf_op jit(solution)/shard_map/ppermute | solution.py:130
  140.3 8.6 %collective-permute-start.13 = (bf16[1152,128]{1,0:T(8,128)(2,1)S(1)}, bf16[1152,128]{1,0:T(8,128)(2,1)S(1)}, u32[]{:S(2)}, u32[]{:S(2)}) collective-permute-start(bf16[1152,128]{1,0:T(8,128)(2,1)S(1)} %collective-permute-done.12), channel_id=1, source_target_pairs={{0,8},{8,0},{16,24},{24,16},{1,9},{9,1},{17,25},{25,17},{2,10},{10... | collective-permute-start | bytes 884744 | tf_op jit(solution)/shard_map/ppermute | solution.py:130
  143.7 5.8 %copy-start.3 = (bf16[6,192,192]{2,1,0:T(8,128)(2,1)S(1)}, bf16[6,192,192]{2,1,0:T(8,128)(2,1)}, u32[]{:S(2)}) copy-start(bf16[6,192,192]{2,1,0:T(8,128)(2,1)} %constant.195.clone) | copy-start | bytes 1327108

commit v7 on v6

--- a/solution.py
+++ b/solution.py
@@ -136,13 +136,7 @@
             d = -step if w == 0 else step
             front[w] = hop(front[w], w)
             total = total + term(front[w], d, e)
-            if step < 3:
-                ready = other[w]
-                if step == 2:
-                    ready, _ = lax.optimization_barrier((ready, front[w]))
-                other[w] = hop(ready, w)
-            else:
-                other[w] = across(front[w])
+            other[w] = across(front[w]) if step == 3 else hop(other[w], w)
             total = total + term(other[w], d, 1 - e)
     far = hop(front[0], 0)
     total = total + term(far, NZ // 2, e) + term(across(far), NZ // 2, 1 - e)

time: 152 us -> 150 us (0.987)
  the two profiles are of different devices: /device:TPU:16 before, /device:TPU:2 now
where the time goes in v7:
time: 150 us; the launch traced here: 149 us
  starting transfers between devices  74.6 us (50%)
  waiting for transfers between devices  37.9 us (25%)
  blocking collectives  16.1 us (11%)
  matrix products  12.8 us (9%)
  other arithmetic  3.69 us (2%)
  local copies, waits for them, and re-layouts  3.31 us (2%)
    ppermute x11, starting transfers between devices, hop(): return lax.ppermute(c, ('core', 'z'), ways[w])  35.2 us
    all_to_all x1, starting transfers between devices, body(): held = lax.all_to_all(first, VIRT, split_axis=0, concat_axis=0, tiled=True)  20.4 us
    all_gather x1, blocking collectives, body(): gathered = lax.all_gather(diff, 'y', axis=0, tiled=False)  16.1 us
    ppermute x11, waiting for transfers between devices, hop(): return lax.ppermute(c, ('core', 'z'), ways[w])  13.9 us
    all_to_all x1, waiting for transfers between devices, body(): lax.all_to_all(second, PAIR, split_axis=0, concat_axis=0, tiled=True)  12.1 us
    dot_general x21, matrix products, dot(): return jnp.dot(a, b, preferred_element_type=jnp.float32)  11.3 us
    all_to_all x1, starting transfers between devices, body(): lax.all_to_all(second, PAIR, split_axis=0, concat_axis=0, tiled=True)  10.5 us
    ppermute x3, starting transfers between devices, across(): return lax.ppermute(c, 'y', [(i, i ^ 1) for i in range(NY)])  8.43 us
  transfers between devices with their start and end apart: 16, of which 6 were waited for; matrix products, arithmetic and copies ran while one was open for 8% of the time, Pallas kernels for 0%

profile of v7, /device:TPU:2, one launch (start us, length us, event | category | flops | bytes accessed | tf_op | source)
XLA Modules:
  0.0 149.0 jit_solution(470027593732777555)
XLA Ops:
  2.0 20.4 %all-to-all-start = ((bf16[32,24,128]{2,1,0:T(8,128)(2,1)}), bf16[32,24,128]{2,1,0:T(8,128)(2,1)S(1)}, u32[]{:S(2)}, u32[]{:S(2)}) async-start(bf16[32,24,128]{2,1,0:T(8,128)(2,1)} %bitcast.1), calls=%async_computation | async-start | bytes 393216 | tf_op jit(solution)/shard_map/all_to_all | solution.py:86
  26.1 7.3 %all-to-all-done = bf16[32,24,128]{2,1,0:T(8,128)(2,1)S(1)} async-done(((bf16[32,24,128]{2,1,0:T(8,128)(2,1)}), bf16[32,24,128]{2,1,0:T(8,128)(2,1)S(1)}, u32[]{:S(2)}, u32[]{:S(2)}) %all-to-all-start) | async-done | bytes 196640 | tf_op jit(solution)/shard_map/all_to_all | solution.py:86
  34.8 10.5 %all-to-all-start.1 = ((bf16[32,24,128]{2,1,0:T(8,128)(2,1)}), bf16[32,24,128]{2,1,0:T(8,128)(2,1)S(1)}, u32[]{:S(2)}, u32[]{:S(2)}) async-start(bf16[32,24,128]{2,1,0:T(8,128)(2,1)} %bitcast.7), calls=%async_computation.1 | async-start | bytes 393216 | tf_op jit(solution)/shard_map/all_to_all | solution.py:90
  45.3 2.0 %broadcast_multiply_fusion = bf16[2048,512]{1,0:T(8,128)(2,1)S(1)} fusion(bf16[2048,512]{1,0:T(8,128)(2,1)} %param.10, bf16[2048]{0:T(1024)(128)(2,1)S(1)} %bitcast.72), kind=kLoop, calls=%fused_computation.25 | loop fusion | flops 1048576 | bytes 4198400 | tf_op jit(solution)/shard_map/mul | solution.py:110
  47.3 12.1 %all-to-all-done.1 = bf16[32,24,128]{2,1,0:T(8,128)(2,1)S(1)} async-done(((bf16[32,24,128]{2,1,0:T(8,128)(2,1)}), bf16[32,24,128]{2,1,0:T(8,128)(2,1)S(1)}, u32[]{:S(2)}, u32[]{:S(2)}) %all-to-all-start.1) | async-done | bytes 196640 | tf_op jit(solution)/shard_map/all_to_all | solution.py:90
  61.4 16.1 %all-gather = bf16[2304,128]{1,0:T(8,128)(2,1)S(1)} all-gather(bf16[576,128]{1,0:T(8,128)(2,1)S(1)} %fusion.11), channel_id=2, replica_groups=mesh['x'=8,'yh'=2,'core'=2,'y'=4,'z'=8] {'y'}, dimensions={0}, use_global_device_ids=true | all-gather | bytes 737280 | tf_op jit(solution)/shard_map/all_gather | solution.py:103
  77.5 3.3 %collective-permute-start.1 = (bf16[1152,128]{1,0:T(8,128)(2,1)S(1)}, bf16[1152,128]{1,0:T(8,128)(2,1)S(1)}, u32[]{:S(2)}, u32[]{:S(2)}) collective-permute-start(bf16[1152,128]{1,0:T(8,128)(2,1)S(1)} %bitcast.68), channel_id=1, source_target_pairs={{0,1},{1,2},{2,3},{3,4},{4,5},{5,6},{6,7},{7,0},{32,39},{33,32},{3... | collective-permute-start | bytes 884744 | tf_op jit(solution)/shard_map/ppermute | solution.py:127
  80.8 3.8 %collective-permute-start.3 = (bf16[1152,128]{1,0:T(8,128)(2,1)S(1)}, bf16[1152,128]{1,0:T(8,128)(2,1)S(1)}, u32[]{:S(2)}, u32[]{:S(2)}) collective-permute-start(bf16[1152,128]{1,0:T(8,128)(2,1)S(1)} %bitcast.69), channel_id=1, source_target_pairs={{0,7},{1,0},{2,1},{3,2},{4,3},{5,4},{6,5},{7,6},{32,33},{33,34},{3... | collective-permute-start | bytes 884744 | tf_op jit(solution)/shard_map/ppermute | solution.py:127
  84.6 1.9 %collective-permute-start.2 = (bf16[1152,128]{1,0:T(8,128)(2,1)S(1)}, bf16[1152,128]{1,0:T(8,128)(2,1)S(1)}, u32[]{:S(2)}, u32[]{:S(2)}) collective-permute-start(bf16[1152,128]{1,0:T(8,128)(2,1)S(1)} %bitcast.65), channel_id=1, source_target_pairs={{0,7},{1,0},{2,1},{3,2},{4,3},{5,4},{6,5},{7,6},{32,33},{33,34},{3... | collective-permute-start | bytes 884744 | tf_op jit(solution)/shard_map/ppermute | solution.py:127
  86.5 3.9 %collective-permute-start = (bf16[1152,128]{1,0:T(8,128)(2,1)S(1)}, bf16[1152,128]{1,0:T(8,128)(2,1)S(1)}, u32[]{:S(2)}, u32[]{:S(2)}) collective-permute-start(bf16[1152,128]{1,0:T(8,128)(2,1)S(1)} %bitcast.66), channel_id=1, source_target_pairs={{0,1},{1,2},{2,3},{3,4},{4,5},{5,6},{6,7},{7,0},{32,39},{33,32},{3... | collective-permute-start | bytes 884744 | tf_op jit(solution)/shard_map/ppermute | solution.py:127
  91.4 2.1 %collective-permute-start.5 = (bf16[1152,128]{1,0:T(8,128)(2,1)S(1)}, bf16[1152,128]{1,0:T(8,128)(2,1)S(1)}, u32[]{:S(2)}, u32[]{:S(2)}) collective-permute-start(bf16[1152,128]{1,0:T(8,128)(2,1)S(1)} %collective-permute-done.1), channel_id=1, source_target_pairs={{0,1},{1,2},{2,3},{3,4},{4,5},{5,6},{6,7},{7,0},{32,39},{33,32},{3... | collective-permute-start | bytes 884744 | tf_op jit(solution)/shard_map/ppermute | solution.py:127
  93.9 5.0 %collective-permute-start.7 = (bf16[1152,128]{1,0:T(8,128)(2,1)S(1)}, bf16[1152,128]{1,0:T(8,128)(2,1)S(1)}, u32[]{:S(2)}, u32[]{:S(2)}) collective-permute-start(bf16[1152,128]{1,0:T(8,128)(2,1)S(1)} %collective-permute-done.3), channel_id=1, source_target_pairs={{0,7},{1,0},{2,1},{3,2},{4,3},{5,4},{6,5},{7,6},{32,33},{33,34},{3... | collective-permute-start | bytes 884744 | tf_op jit(solution)/shard_map/ppermute | solution.py:127
  99.4 3.5 %collective-permute-start.6 = (bf16[1152,128]{1,0:T(8,128)(2,1)S(1)}, bf16[1152,128]{1,0:T(8,128)(2,1)S(1)}, u32[]{:S(2)}, u32[]{:S(2)}) collective-permute-start(bf16[1152,128]{1,0:T(8,128)(2,1)S(1)} %collective-permute-done.2), channel_id=1, source_target_pairs={{0,7},{1,0},{2,1},{3,2},{4,3},{5,4},{6,5},{7,6},{32,33},{33,34},{3... | collective-permute-start | bytes 884744 | tf_op jit(solution)/shard_map/ppermute | solution.py:127
  103.4 2.3 %collective-permute-start.4 = (bf16[1152,128]{1,0:T(8,128)(2,1)S(1)}, bf16[1152,128]{1,0:T(8,128)(2,1)S(1)}, u32[]{:S(2)}, u32[]{:S(2)}) collective-permute-start(bf16[1152,128]{1,0:T(8,128)(2,1)S(1)} %collective-permute-done), channel_id=1, source_target_pairs={{0,1},{1,2},{2,3},{3,4},{4,5},{5,6},{6,7},{7,0},{32,39},{33,32},{3... | collective-permute-start | bytes 884744 | tf_op jit(solution)/shard_map/ppermute | solution.py:127
  106.3 3.2 %collective-permute-done.6 = bf16[1152,128]{1,0:T(8,128)(2,1)S(1)} collective-permute-done((bf16[1152,128]{1,0:T(8,128)(2,1)S(1)}, bf16[1152,128]{1,0:T(8,128)(2,1)S(1)}, u32[]{:S(2)}, u32[]{:S(2)}) %collective-permute-start.6) | collective-permute-done | bytes 294944 | tf_op jit(solution)/shard_map/ppermute | solution.py:127
  109.4 5.6 %collective-permute-start.10 = (bf16[1152,128]{1,0:T(8,128)(2,1)S(1)}, bf16[1152,128]{1,0:T(8,128)(2,1)S(1)}, u32[]{:S(2)}, u32[]{:S(2)}) collective-permute-start(bf16[1152,128]{1,0:T(8,128)(2,1)S(1)} %collective-permute-done.6), channel_id=1, source_target_pairs={{0,7},{1,0},{2,1},{3,2},{4,3},{5,4},{6,5},{7,6},{32,33},{33,34},{3... | collective-permute-start | bytes 884744 | tf_op jit(solution)/shard_map/ppermute | solution.py:127
  115.5 1.9 %collective-permute-start.8 = (bf16[1152,128]{1,0:T(8,128)(2,1)S(1)}, bf16[1152,128]{1,0:T(8,128)(2,1)S(1)}, u32[]{:S(2)}, u32[]{:S(2)}) collective-permute-start(bf16[1152,128]{1,0:T(8,128)(2,1)S(1)} %collective-permute-done.4), channel_id=1, source_target_pairs={{0,1},{1,2},{2,3},{3,4},{4,5},{5,6},{6,7},{7,0},{32,39},{33,32},{3... | collective-permute-start | bytes 884744 | tf_op jit(solution)/shard_map/ppermute | solution.py:127
  118.9 6.4 %collective-permute-done.8 = bf16[1152,128]{1,0:T(8,128)(2,1)S(1)} collective-permute-done((bf16[1152,128]{1,0:T(8,128)(2,1)S(1)}, bf16[1152,128]{1,0:T(8,128)(2,1)S(1)}, u32[]{:S(2)}, u32[]{:S(2)}) %collective-permute-start.8) | collective-permute-done | bytes 294944 | tf_op jit(solution)/shard_map/ppermute | solution.py:127
  125.3 3.2 %collective-permute-start.9 = (bf16[1152,128]{1,0:T(8,128)(2,1)S(1)}, bf16[1152,128]{1,0:T(8,128)(2,1)S(1)}, u32[]{:S(2)}, u32[]{:S(2)}) collective-permute-start(bf16[1152,128]{1,0:T(8,128)(2,1)S(1)} %collective-permute-done.8), channel_id=1, source_target_pairs={{0,8},{8,0},{16,24},{24,16},{1,9},{9,1},{17,25},{25,17},{2,10},{10... | collective-permute-start | bytes 884744 | tf_op jit(solution)/shard_map/ppermute | solution.py:130
  128.5 1.9 %collective-permute-start.12 = (bf16[1152,128]{1,0:T(8,128)(2,1)S(1)}, bf16[1152,128]{1,0:T(8,128)(2,1)S(1)}, u32[]{:S(2)}, u32[]{:S(2)}) collective-permute-start(bf16[1152,128]{1,0:T(8,128)(2,1)S(1)} %collective-permute-done.8), channel_id=1, source_target_pairs={{0,1},{1,2},{2,3},{3,4},{4,5},{5,6},{6,7},{7,0},{32,39},{33,32},{3... | collective-permute-start | bytes 884744 | tf_op jit(solution)/shard_map/ppermute | solution.py:127
  130.5 2.6 %collective-permute-start.11 = (bf16[1152,128]{1,0:T(8,128)(2,1)S(1)}, bf16[1152,128]{1,0:T(8,128)(2,1)S(1)}, u32[]{:S(2)}, u32[]{:S(2)}) collective-permute-start(bf16[1152,128]{1,0:T(8,128)(2,1)S(1)} %collective-permute-done.10), channel_id=1, source_target_pairs={{0,8},{8,0},{16,24},{24,16},{1,9},{9,1},{17,25},{25,17},{2,10},{10... | collective-permute-start | bytes 884744 | tf_op jit(solution)/shard_map/ppermute | solution.py:130
  134.0 4.3 %collective-permute-done.12 = bf16[1152,128]{1,0:T(8,128)(2,1)S(1)} collective-permute-done((bf16[1152,128]{1,0:T(8,128)(2,1)S(1)}, bf16[1152,128]{1,0:T(8,128)(2,1)S(1)}, u32[]{:S(2)}, u32[]{:S(2)}) %collective-permute-start.12) | collective-permute-done | bytes 294944 | tf_op jit(solution)/shard_map/ppermute | solution.py:127
  138.4 2.6 %collective-permute-start.13 = (bf16[1152,128]{1,0:T(8,128)(2,1)S(1)}, bf16[1152,128]{1,0:T(8,128)(2,1)S(1)}, u32[]{:S(2)}, u32[]{:S(2)}) collective-permute-start(bf16[1152,128]{1,0:T(8,128)(2,1)S(1)} %collective-permute-done.12), channel_id=1, source_target_pairs={{0,8},{8,0},{16,24},{24,16},{1,9},{9,1},{17,25},{25,17},{2,10},{10... | collective-permute-start | bytes 884744 | tf_op jit(solution)/shard_map/ppermute | solution.py:130
  142.4 4.6 %collective-permute-done.13 = bf16[1152,128]{1,0:T(8,128)(2,1)S(1)} collective-permute-done((bf16[1152,128]{1,0:T(8,128)(2,1)S(1)}, bf16[1152,128]{1,0:T(8,128)(2,1)S(1)}, u32[]{:S(2)}, u32[]{:S(2)}) %collective-permute-start.13) | collective-permute-done | bytes 294944 | tf_op jit(solution)/shard_map/ppermute | solution.py:130
  (53 shorter events, 17.8 us)
Async XLA Ops:
  0.0 0.9 copy-start
  0.0 33.5 %copy-start.1 = (bf16[768,768]{1,0:T(8,128)(2,1)S(1)}, bf16[768,768]{1,0:T(8,128)(2,1)}, u32[]{:S(2)}) copy-start(bf16[768,768]{1,0:T(8,128)(2,1)} %constant.191.clone) | copy-start | bytes 3538948
  2.0 31.4 %all-to-all-start = ((bf16[32,24,128]{2,1,0:T(8,128)(2,1)}), bf16[32,24,128]{2,1,0:T(8,128)(2,1)S(1)}, u32[]{:S(2)}, u32[]{:S(2)}) async-start(bf16[32,24,128]{2,1,0:T(8,128)(2,1)} %bitcast.1), calls=%async_computation | async-start | bytes 393216 | tf_op jit(solution)/shard_map/all_to_all | solution.py:86
  34.8 24.6 %all-to-all-start.1 = ((bf16[32,24,128]{2,1,0:T(8,128)(2,1)}), bf16[32,24,128]{2,1,0:T(8,128)(2,1)S(1)}, u32[]{:S(2)}, u32[]{:S(2)}) async-start(bf16[32,24,128]{2,1,0:T(8,128)(2,1)} %bitcast.7), calls=%async_computation.1 | async-start | bytes 393216 | tf_op jit(solution)/shard_map/all_to_all | solution.py:90
  45.3 15.7 %copy-start.2 = (bf16[576,768]{1,0:T(8,128)(2,1)S(1)}, bf16[576,768]{1,0:T(8,128)(2,1)}, u32[]{:S(2)}) copy-start(bf16[576,768]{1,0:T(8,128)(2,1)} %constant.194.clone) | copy-start | bytes 2654212
  77.5 13.9 %collective-permute-start.1 = (bf16[1152,128]{1,0:T(8,128)(2,1)S(1)}, bf16[1152,128]{1,0:T(8,128)(2,1)S(1)}, u32[]{:S(2)}, u32[]{:S(2)}) collective-permute-start(bf16[1152,128]{1,0:T(8,128)(2,1)S(1)} %bitcast.68), channel_id=1, source_target_pairs={{0,1},{1,2},{2,3},{3,4},{4,5},{5,6},{6,7},{7,0},{32,39},{33,32},{3... | collective-permute-start | bytes 884744 | tf_op jit(solution)/shard_map/ppermute | solution.py:127
  80.8 13.1 %collective-permute-start.3 = (bf16[1152,128]{1,0:T(8,128)(2,1)S(1)}, bf16[1152,128]{1,0:T(8,128)(2,1)S(1)}, u32[]{:S(2)}, u32[]{:S(2)}) collective-permute-start(bf16[1152,128]{1,0:T(8,128)(2,1)S(1)} %bitcast.69), channel_id=1, source_target_pairs={{0,7},{1,0},{2,1},{3,2},{4,3},{5,4},{6,5},{7,6},{32,33},{33,34},{3... | collective-permute-start | bytes 884744 | tf_op jit(solution)/shard_map/ppermute | solution.py:127
  84.6 14.8 %collective-permute-start.2 = (bf16[1152,128]{1,0:T(8,128)(2,1)S(1)}, bf16[1152,128]{1,0:T(8,128)(2,1)S(1)}, u32[]{:S(2)}, u32[]{:S(2)}) collective-permute-start(bf16[1152,128]{1,0:T(8,128)(2,1)S(1)} %bitcast.65), channel_id=1, source_target_pairs={{0,7},{1,0},{2,1},{3,2},{4,3},{5,4},{6,5},{7,6},{32,33},{33,34},{3... | collective-permute-start | bytes 884744 | tf_op jit(solution)/shard_map/ppermute | solution.py:127
  86.5 16.9 %collective-permute-start = (bf16[1152,128]{1,0:T(8,128)(2,1)S(1)}, bf16[1152,128]{1,0:T(8,128)(2,1)S(1)}, u32[]{:S(2)}, u32[]{:S(2)}) collective-permute-start(bf16[1152,128]{1,0:T(8,128)(2,1)S(1)} %bitcast.66), channel_id=1, source_target_pairs={{0,1},{1,2},{2,3},{3,4},{4,5},{5,6},{6,7},{7,0},{32,39},{33,32},{3... | collective-permute-start | bytes 884744 | tf_op jit(solution)/shard_map/ppermute | solution.py:127
  91.4 26.5 %collective-permute-start.5 = (bf16[1152,128]{1,0:T(8,128)(2,1)S(1)}, bf16[1152,128]{1,0:T(8,128)(2,1)S(1)}, u32[]{:S(2)}, u32[]{:S(2)}) collective-permute-start(bf16[1152,128]{1,0:T(8,128)(2,1)S(1)} %collective-permute-done.1), channel_id=1, source_target_pairs={{0,1},{1,2},{2,3},{3,4},{4,5},{5,6},{6,7},{7,0},{32,39},{33,32},{3... | collective-permute-start | bytes 884744 | tf_op jit(solution)/shard_map/ppermute | solution.py:127
  93.9 23.5 %collective-permute-start.7 = (bf16[1152,128]{1,0:T(8,128)(2,1)S(1)}, bf16[1152,128]{1,0:T(8,128)(2,1)S(1)}, u32[]{:S(2)}, u32[]{:S(2)}) collective-permute-start(bf16[1152,128]{1,0:T(8,128)(2,1)S(1)} %collective-permute-done.3), channel_id=1, source_target_pairs={{0,7},{1,0},{2,1},{3,2},{4,3},{5,4},{6,5},{7,6},{32,33},{33,34},{3... | collective-permute-start | bytes 884744 | tf_op jit(solution)/shard_map/ppermute | solution.py:127
  99.4 10.1 %collective-permute-start.6 = (bf16[1152,128]{1,0:T(8,128)(2,1)S(1)}, bf16[1152,128]{1,0:T(8,128)(2,1)S(1)}, u32[]{:S(2)}, u32[]{:S(2)}) collective-permute-start(bf16[1152,128]{1,0:T(8,128)(2,1)S(1)} %collective-permute-done.2), channel_id=1, source_target_pairs={{0,7},{1,0},{2,1},{3,2},{4,3},{5,4},{6,5},{7,6},{32,33},{33,34},{3... | collective-permute-start | bytes 884744 | tf_op jit(solution)/shard_map/ppermute | solution.py:127
  103.4 12.1 %collective-permute-start.4 = (bf16[1152,128]{1,0:T(8,128)(2,1)S(1)}, bf16[1152,128]{1,0:T(8,128)(2,1)S(1)}, u32[]{:S(2)}, u32[]{:S(2)}) collective-permute-start(bf16[1152,128]{1,0:T(8,128)(2,1)S(1)} %collective-permute-done), channel_id=1, source_target_pairs={{0,1},{1,2},{2,3},{3,4},{4,5},{5,6},{6,7},{7,0},{32,39},{33,32},{3... | collective-permute-start | bytes 884744 | tf_op jit(solution)/shard_map/ppermute | solution.py:127
  109.4 21.0 %collective-permute-start.10 = (bf16[1152,128]{1,0:T(8,128)(2,1)S(1)}, bf16[1152,128]{1,0:T(8,128)(2,1)S(1)}, u32[]{:S(2)}, u32[]{:S(2)}) collective-permute-start(bf16[1152,128]{1,0:T(8,128)(2,1)S(1)} %collective-permute-done.6), channel_id=1, source_target_pairs={{0,7},{1,0},{2,1},{3,2},{4,3},{5,4},{6,5},{7,6},{32,33},{33,34},{3... | collective-permute-start | bytes 884744 | tf_op jit(solution)/shard_map/ppermute | solution.py:127
  115.5 9.8 %collective-permute-start.8 = (bf16[1152,128]{1,0:T(8,128)(2,1)S(1)}, bf16[1152,128]{1,0:T(8,128)(2,1)S(1)}, u32[]{:S(2)}, u32[]{:S(2)}) collective-permute-start(bf16[1152,128]{1,0:T(8,128)(2,1)S(1)} %collective-permute-done.4), channel_id=1, source_target_pairs={{0,1},{1,2},{2,3},{3,4},{4,5},{5,6},{6,7},{7,0},{32,39},{33,32},{3... | collective-permute-start | bytes 884744 | tf_op jit(solution)/shard_map/ppermute | solution.py:127
  125.3 15.7 %collective-permute-start.9 = (bf16[1152,128]{1,0:T(8,128)(2,1)S(1)}, bf16[1152,128]{1,0:T(8,128)(2,1)S(1)}, u32[]{:S(2)}, u32[]{:S(2)}) collective-permute-start(bf16[1152,128]{1,0:T(8,128)(2,1)S(1)} %collective-permute-done.8), channel_id=1, source_target_pairs={{0,8},{8,0},{16,24},{24,16},{1,9},{9,1},{17,25},{25,17},{2,10},{10... | collective-permute-start | bytes 884744 | tf_op jit(solution)/shard_map/ppermute | solution.py:130
  128.5 9.8 %collective-permute-start.12 = (bf16[1152,128]{1,0:T(8,128)(2,1)S(1)}, bf16[1152,128]{1,0:T(8,128)(2,1)S(1)}, u32[]{:S(2)}, u32[]{:S(2)}) collective-permute-start(bf16[1152,128]{1,0:T(8,128)(2,1)S(1)} %collective-permute-done.8), channel_id=1, source_target_pairs={{0,1},{1,2},{2,3},{3,4},{4,5},{5,6},{6,7},{7,0},{32,39},{33,32},{3... | collective-permute-start | bytes 884744 | tf_op jit(solution)/shard_map/ppermute | solution.py:127
  130.5 11.4 %collective-permute-start.11 = (bf16[1152,128]{1,0:T(8,128)(2,1)S(1)}, bf16[1152,128]{1,0:T(8,128)(2,1)S(1)}, u32[]{:S(2)}, u32[]{:S(2)}) collective-permute-start(bf16[1152,128]{1,0:T(8,128)(2,1)S(1)} %collective-permute-done.10), channel_id=1, source_target_pairs={{0,8},{8,0},{16,24},{24,16},{1,9},{9,1},{17,25},{25,17},{2,10},{10... | collective-permute-start | bytes 884744 | tf_op jit(solution)/shard_map/ppermute | solution.py:130
  138.4 8.6 %collective-permute-start.13 = (bf16[1152,128]{1,0:T(8,128)(2,1)S(1)}, bf16[1152,128]{1,0:T(8,128)(2,1)S(1)}, u32[]{:S(2)}, u32[]{:S(2)}) collective-permute-start(bf16[1152,128]{1,0:T(8,128)(2,1)S(1)} %collective-permute-done.12), channel_id=1, source_target_pairs={{0,8},{8,0},{16,24},{24,16},{1,9},{9,1},{17,25},{25,17},{2,10},{10... | collective-permute-start | bytes 884744 | tf_op jit(solution)/shard_map/ppermute | solution.py:130
  142.4 5.1 %copy-start.3 = (bf16[6,192,192]{2,1,0:T(8,128)(2,1)S(1)}, bf16[6,192,192]{2,1,0:T(8,128)(2,1)}, u32[]{:S(2)}) copy-start(bf16[6,192,192]{2,1,0:T(8,128)(2,1)} %constant.195.clone) | copy-start | bytes 1327108

commit v8 on v4

--- a/solution.py
+++ b/solution.py
@@ -101,7 +101,9 @@
     diff = diff.astype(bf)
 
     gathered = lax.all_gather(diff, "y", axis=0, tiled=False)
-    pieces = [jnp.concatenate([gathered[2 * r], gathered[2 * r + 1]], 1) for r in range(2)]
+    chunk = jnp.concatenate(
+        [jnp.concatenate([gathered[2 * r], gathered[2 * r + 1]], 1) for r in range(2)], 0
+    )
 
     col_mask = lax.dynamic_index_in_dim(int_pattern, v * cols // TP, 1, keepdims=False)
     weighted = integrals * jnp.repeat(col_mask, TP).astype(bf)[:, None]
@@ -120,16 +122,15 @@
         ]
 
     ways = (shift(1), shift(-1))
-    front = [list(pieces), list(pieces)]
-    totals = [term(c, 0) for c in pieces]
+    front = [chunk, chunk]
+    total = term(chunk, 0)
     for step in range(1, NZ // 2 + 1):
-        for i in range(2):
-            for w in range(2):
-                if step == NZ // 2 and w != i:
-                    continue
-                front[w][i] = lax.ppermute(front[w][i], ("core", "z"), ways[w])
-                totals[i] = totals[i] + term(front[w][i], -step if w == 0 else step)
-    both = jnp.concatenate([t.astype(bf).reshape(OCC, NP * HALF, cols) for t in totals], 1)
+        for w in range(2 if step < NZ // 2 else 1):
+            front[w] = lax.ppermute(front[w], ("core", "z"), ways[w])
+            total = total + term(front[w], -step if w == 0 else step)
+    both = (
+        total.astype(bf).reshape(2, OCC, NP * HALF, cols).transpose(1, 0, 2, 3)
+    ).reshape(OCC, NP * OCC, cols)
     out = jnp.einsum(
         "bij,bjk->bik", jnp.asarray(PLACE, bf), both, preferred_element_type=jnp.float32
     )

time: 143 us -> 146 us (1.021)
  the two profiles are of different devices: /device:TPU:2 before, /device:TPU:1 now
where the time goes in v8:
time: 146 us; the launch traced here: 145 us
  waiting for transfers between devices  59.4 us (41%)
  starting transfers between devices  57 us (39%)
  blocking collectives  13.6 us (9%)
  matrix products  8.27 us (6%)
  local copies, waits for them, and re-layouts  4.29 us (3%)
  other arithmetic  2.09 us (1%)
    ppermute x7, waiting for transfers between devices, body(): front[w] = lax.ppermute(front[w], ('core', 'z'), ways[w])  38.1 us
    ppermute x7, starting transfers between devices, body(): front[w] = lax.ppermute(front[w], ('core', 'z'), ways[w])  23.9 us
    all_to_all x1, starting transfers between devices, body(): held = lax.all_to_all(first, VIRT, split_axis=0, concat_axis=0, tiled=True)  21 us
    all_gather x1, blocking collectives, body(): gathered = lax.all_gather(diff, 'y', axis=0, tiled=False)  13.6 us
    all_to_all x1, waiting for transfers between devices, body(): lax.all_to_all(second, PAIR, split_axis=0, concat_axis=0, tiled=True)  13.4 us
    all_to_all x1, starting transfers between devices, body(): lax.all_to_all(second, PAIR, split_axis=0, concat_axis=0, tiled=True)  12.2 us
    all_to_all x1, waiting for transfers between devices, body(): held = lax.all_to_all(first, VIRT, split_axis=0, concat_axis=0, tiled=True)  7.92 us
    dot_general x13, matrix products, dot(): return jnp.dot(a, b, preferred_element_type=jnp.float32)  6.8 us
  transfers between devices with their start and end apart: 9, of which 7 were waited for; matrix products, arithmetic and copies ran while one was open for 4% of the time, Pallas kernels for 0%

profile of v8, /device:TPU:1, one launch (start us, length us, event | category | flops | bytes accessed | tf_op | source)
XLA Modules:
  0.0 145.1 jit_solution(10920279596248948539)
XLA Ops:
  0.0 0.9 copy-done
  2.0 21.0 %all-to-all-start = ((bf16[32,24,128]{2,1,0:T(8,128)(2,1)}), bf16[32,24,128]{2,1,0:T(8,128)(2,1)S(1)}, u32[]{:S(2)}, u32[]{:S(2)}) async-start(bf16[32,24,128]{2,1,0:T(8,128)(2,1)} %bitcast.1), calls=%async_computation | async-start | bytes 393216 | tf_op jit(solution)/shard_map/all_to_all | solution.py:86
  23.1 0.9 fusion.33
  24.0 0.8 dynamic-slice_convert_fusion
  24.8 7.9 %all-to-all-done = bf16[32,24,128]{2,1,0:T(8,128)(2,1)S(1)} async-done(((bf16[32,24,128]{2,1,0:T(8,128)(2,1)}), bf16[32,24,128]{2,1,0:T(8,128)(2,1)S(1)}, u32[]{:S(2)}, u32[]{:S(2)}) %all-to-all-start) | async-done | bytes 196640 | tf_op jit(solution)/shard_map/all_to_all | solution.py:86
  32.8 1.8 %fusion.6 = bf16[768,128]{0,1:T(8,128)(2,1)S(1)} fusion(bf16[768,128]{1,0:T(8,128)(2,1)S(1)} %bitcast.50, bf16[768,768]{1,0:T(8,128)(2,1)} %constant.178.clone), kind=kOutput, calls=%fused_computation.16 | convolution fusion | flops 151093248 | bytes 1572864 | tf_op jit(solution)/shard_map/dot_general | solution.py:63
  34.6 0.8 copy.12
  35.4 12.2 %all-to-all-start.1 = ((bf16[32,24,128]{2,1,0:T(8,128)(2,1)}), bf16[32,24,128]{2,1,0:T(8,128)(2,1)S(1)}, u32[]{:S(2)}, u32[]{:S(2)}) async-start(bf16[32,24,128]{2,1,0:T(8,128)(2,1)} %bitcast.7), calls=%async_computation.1 | async-start | bytes 393216 | tf_op jit(solution)/shard_map/all_to_all | solution.py:90
  48.4 13.4 %all-to-all-done.1 = bf16[32,24,128]{2,1,0:T(8,128)(2,1)S(1)} async-done(((bf16[32,24,128]{2,1,0:T(8,128)(2,1)}), bf16[32,24,128]{2,1,0:T(8,128)(2,1)S(1)}, u32[]{:S(2)}, u32[]{:S(2)}) %all-to-all-start.1) | async-done | bytes 196640 | tf_op jit(solution)/shard_map/all_to_all | solution.py:90
  62.6 13.6 %all-gather = bf16[2304,128]{1,0:T(8,128)(2,1)S(1)} all-gather(bf16[576,128]{1,0:T(8,128)(2,1)S(1)} %fusion.5), channel_id=2, replica_groups=mesh['x'=8,'yh'=2,'core'=2,'y'=4,'z'=8] {'y'}, dimensions={0}, use_global_device_ids=true | all-gather | bytes 737280 | tf_op jit(solution)/shard_map/all_gather | solution.py:103
  76.3 2.3 %collective-permute-start = (bf16[1152,256]{1,0:T(8,128)(2,1)S(1)}, bf16[1152,256]{1,0:T(8,128)(2,1)S(1)}, u32[]{:S(2)}, u32[]{:S(2)}) collective-permute-start(bf16[1152,256]{1,0:T(8,128)(2,1)S(1)} %maximum_maximum_fusion), channel_id=1, source_target_pairs={{0,1},{1,2},{2,3},{3,4},{4,5},{5,6},{6,7},{7,0},{32,39},{33,32},{3... | collective-permute-start | bytes 1769480 | tf_op jit(solution)/shard_map/ppermute | solution.py:129
  78.6 3.0 %collective-permute-start.1 = (bf16[1152,256]{1,0:T(8,128)(2,1)S(1)}, bf16[1152,256]{1,0:T(8,128)(2,1)S(1)}, u32[]{:S(2)}, u32[]{:S(2)}) collective-permute-start(bf16[1152,256]{1,0:T(8,128)(2,1)S(1)} %maximum_maximum_fusion), channel_id=1, source_target_pairs={{0,7},{1,0},{2,1},{3,2},{4,3},{5,4},{6,5},{7,6},{32,33},{33,34},{3... | collective-permute-start | bytes 1769480 | tf_op jit(solution)/shard_map/ppermute | solution.py:129
  82.4 13.0 %collective-permute-done.1 = bf16[1152,256]{1,0:T(8,128)(2,1)S(1)} collective-permute-done((bf16[1152,256]{1,0:T(8,128)(2,1)S(1)}, bf16[1152,256]{1,0:T(8,128)(2,1)S(1)}, u32[]{:S(2)}, u32[]{:S(2)}) %collective-permute-start.1) | collective-permute-done | bytes 589856 | tf_op jit(solution)/shard_map/ppermute | solution.py:129
  95.4 1.9 %collective-permute-start.3 = (bf16[1152,256]{1,0:T(8,128)(2,1)S(1)}, bf16[1152,256]{1,0:T(8,128)(2,1)S(1)}, u32[]{:S(2)}, u32[]{:S(2)}) collective-permute-start(bf16[1152,256]{1,0:T(8,128)(2,1)S(1)} %collective-permute-done.1), channel_id=1, source_target_pairs={{0,7},{1,0},{2,1},{3,2},{4,3},{5,4},{6,5},{7,6},{32,33},{33,34},{3... | collective-permute-start | bytes 1769480 | tf_op jit(solution)/shard_map/ppermute | solution.py:129
  97.4 4.6 %collective-permute-start.2 = (bf16[1152,256]{1,0:T(8,128)(2,1)S(1)}, bf16[1152,256]{1,0:T(8,128)(2,1)S(1)}, u32[]{:S(2)}, u32[]{:S(2)}) collective-permute-start(bf16[1152,256]{1,0:T(8,128)(2,1)S(1)} %collective-permute-done), channel_id=1, source_target_pairs={{0,1},{1,2},{2,3},{3,4},{4,5},{5,6},{6,7},{7,0},{32,39},{33,32},{3... | collective-permute-start | bytes 1769480 | tf_op jit(solution)/shard_map/ppermute | solution.py:129
  102.9 6.1 %collective-permute-done.3 = bf16[1152,256]{1,0:T(8,128)(2,1)S(1)} collective-permute-done((bf16[1152,256]{1,0:T(8,128)(2,1)S(1)}, bf16[1152,256]{1,0:T(8,128)(2,1)S(1)}, u32[]{:S(2)}, u32[]{:S(2)}) %collective-permute-start.3) | collective-permute-done | bytes 589856 | tf_op jit(solution)/shard_map/ppermute | solution.py:129
  109.0 2.1 %collective-permute-start.5 = (bf16[1152,256]{1,0:T(8,128)(2,1)S(1)}, bf16[1152,256]{1,0:T(8,128)(2,1)S(1)}, u32[]{:S(2)}, u32[]{:S(2)}) collective-permute-start(bf16[1152,256]{1,0:T(8,128)(2,1)S(1)} %collective-permute-done.3), channel_id=1, source_target_pairs={{0,7},{1,0},{2,1},{3,2},{4,3},{5,4},{6,5},{7,6},{32,33},{33,34},{3... | collective-permute-start | bytes 1769480 | tf_op jit(solution)/shard_map/ppermute | solution.py:129
  111.1 1.9 %collective-permute-done.2 = bf16[1152,256]{1,0:T(8,128)(2,1)S(1)} collective-permute-done((bf16[1152,256]{1,0:T(8,128)(2,1)S(1)}, bf16[1152,256]{1,0:T(8,128)(2,1)S(1)}, u32[]{:S(2)}, u32[]{:S(2)}) %collective-permute-start.2) | collective-permute-done | bytes 589856 | tf_op jit(solution)/shard_map/ppermute | solution.py:129
  113.0 5.0 %collective-permute-start.4 = (bf16[1152,256]{1,0:T(8,128)(2,1)S(1)}, bf16[1152,256]{1,0:T(8,128)(2,1)S(1)}, u32[]{:S(2)}, u32[]{:S(2)}) collective-permute-start(bf16[1152,256]{1,0:T(8,128)(2,1)S(1)} %collective-permute-done.2), channel_id=1, source_target_pairs={{0,1},{1,2},{2,3},{3,4},{4,5},{5,6},{6,7},{7,0},{32,39},{33,32},{3... | collective-permute-start | bytes 1769480 | tf_op jit(solution)/shard_map/ppermute | solution.py:129
  119.0 11.2 %collective-permute-done.4 = bf16[1152,256]{1,0:T(8,128)(2,1)S(1)} collective-permute-done((bf16[1152,256]{1,0:T(8,128)(2,1)S(1)}, bf16[1152,256]{1,0:T(8,128)(2,1)S(1)}, u32[]{:S(2)}, u32[]{:S(2)}) %collective-permute-start.4) | collective-permute-done | bytes 589856 | tf_op jit(solution)/shard_map/ppermute | solution.py:129
  130.2 5.0 %collective-permute-start.6 = (bf16[1152,256]{1,0:T(8,128)(2,1)S(1)}, bf16[1152,256]{1,0:T(8,128)(2,1)S(1)}, u32[]{:S(2)}, u32[]{:S(2)}) collective-permute-start(bf16[1152,256]{1,0:T(8,128)(2,1)S(1)} %collective-permute-done.4), channel_id=1, source_target_pairs={{0,1},{1,2},{2,3},{3,4},{4,5},{5,6},{6,7},{7,0},{32,39},{33,32},{3... | collective-permute-start | bytes 1769480 | tf_op jit(solution)/shard_map/ppermute | solution.py:129
  136.2 5.8 %collective-permute-done.6 = bf16[1152,256]{1,0:T(8,128)(2,1)S(1)} collective-permute-done((bf16[1152,256]{1,0:T(8,128)(2,1)S(1)}, bf16[1152,256]{1,0:T(8,128)(2,1)S(1)}, u32[]{:S(2)}, u32[]{:S(2)}) %collective-permute-start.6) | collective-permute-done | bytes 589856 | tf_op jit(solution)/shard_map/ppermute | solution.py:129
  142.6 1.0 copy-done.3
  143.6 1.5 %convolution_convert_fusion.1 = bf16[6,512,192]{1,2,0:T(8,128)(2,1)} fusion(bf16[6,192,192]{2,1,0:T(8,128)(2,1)S(1)} %copy-done.3, bf16[6,192,512]{2,1,0:T(8,128)(2,1)S(1)} %bitcast.49), kind=kOutput, calls=%fused_computation.9 | convolution fusion | flops 227082240 | bytes 2801664 | tf_op jit(solution)/shard_map/bij,bjk->bik/dot_general | solution.py:134
  (36 shorter events, 7.1 us)
Async XLA Ops:
  0.0 0.9 copy-start
  0.9 47.3 %copy-start.5 = (bf16[576,32]{1,0:T(8,128)(2,1)S(1)}, bf16[576,32]{1,0:T(8,128)(2,1)}, u32[]{:S(2)}) copy-start(bf16[576,32]{1,0:T(8,128)(2,1)} %constant.179.clone) | copy-start | bytes 110596
  1.2 60.6 %copy-start.4 = (bf16[2,576,768]{2,1,0:T(8,128)(2,1)S(1)}, bf16[2,576,768]{2,1,0:T(8,128)(2,1)}, u32[]{:S(2)}) copy-start(bf16[2,576,768]{2,1,0:T(8,128)(2,1)} %constant.180.clone) | copy-start | bytes 5308420
  2.0 30.7 %all-to-all-start = ((bf16[32,24,128]{2,1,0:T(8,128)(2,1)}), bf16[32,24,128]{2,1,0:T(8,128)(2,1)S(1)}, u32[]{:S(2)}, u32[]{:S(2)}) async-start(bf16[32,24,128]{2,1,0:T(8,128)(2,1)} %bitcast.1), calls=%async_computation | async-start | bytes 393216 | tf_op jit(solution)/shard_map/all_to_all | solution.py:86
  24.7 37.4 %copy-start.2 = (bf16[576,768]{1,0:T(8,128)(2,1)S(1)}, bf16[576,768]{1,0:T(8,128)(2,1)}, u32[]{:S(2)}) copy-start(bf16[576,768]{1,0:T(8,128)(2,1)} %constant.181.clone) | copy-start | bytes 2654212
  35.4 26.4 %all-to-all-start.1 = ((bf16[32,24,128]{2,1,0:T(8,128)(2,1)}), bf16[32,24,128]{2,1,0:T(8,128)(2,1)S(1)}, u32[]{:S(2)}, u32[]{:S(2)}) async-start(bf16[32,24,128]{2,1,0:T(8,128)(2,1)} %bitcast.7), calls=%async_computation.1 | async-start | bytes 393216 | tf_op jit(solution)/shard_map/all_to_all | solution.py:90
  62.2 19.4 %copy-start.1 = (bf16[2048,512]{1,0:T(8,128)(2,1)S(1)}, bf16[2048,512]{1,0:T(8,128)(2,1)}, u32[]{:S(2)}) copy-start(bf16[2048,512]{1,0:T(8,128)(2,1)} %param.10) | copy-start | bytes 6291460
  76.3 21.1 %collective-permute-start = (bf16[1152,256]{1,0:T(8,128)(2,1)S(1)}, bf16[1152,256]{1,0:T(8,128)(2,1)S(1)}, u32[]{:S(2)}, u32[]{:S(2)}) collective-permute-start(bf16[1152,256]{1,0:T(8,128)(2,1)S(1)} %maximum_maximum_fusion), channel_id=1, source_target_pairs={{0,1},{1,2},{2,3},{3,4},{4,5},{5,6},{6,7},{7,0},{32,39},{33,32},{3... | collective-permute-start | bytes 1769480 | tf_op jit(solution)/shard_map/ppermute | solution.py:129
  78.6 16.8 %collective-permute-start.1 = (bf16[1152,256]{1,0:T(8,128)(2,1)S(1)}, bf16[1152,256]{1,0:T(8,128)(2,1)S(1)}, u32[]{:S(2)}, u32[]{:S(2)}) collective-permute-start(bf16[1152,256]{1,0:T(8,128)(2,1)S(1)} %maximum_maximum_fusion), channel_id=1, source_target_pairs={{0,7},{1,0},{2,1},{3,2},{4,3},{5,4},{6,5},{7,6},{32,33},{33,34},{3... | collective-permute-start | bytes 1769480 | tf_op jit(solution)/shard_map/ppermute | solution.py:129
  95.4 13.6 %collective-permute-start.3 = (bf16[1152,256]{1,0:T(8,128)(2,1)S(1)}, bf16[1152,256]{1,0:T(8,128)(2,1)S(1)}, u32[]{:S(2)}, u32[]{:S(2)}) collective-permute-start(bf16[1152,256]{1,0:T(8,128)(2,1)S(1)} %collective-permute-done.1), channel_id=1, source_target_pairs={{0,7},{1,0},{2,1},{3,2},{4,3},{5,4},{6,5},{7,6},{32,33},{33,34},{3... | collective-permute-start | bytes 1769480 | tf_op jit(solution)/shard_map/ppermute | solution.py:129
  97.4 15.7 %collective-permute-start.2 = (bf16[1152,256]{1,0:T(8,128)(2,1)S(1)}, bf16[1152,256]{1,0:T(8,128)(2,1)S(1)}, u32[]{:S(2)}, u32[]{:S(2)}) collective-permute-start(bf16[1152,256]{1,0:T(8,128)(2,1)S(1)} %collective-permute-done), channel_id=1, source_target_pairs={{0,1},{1,2},{2,3},{3,4},{4,5},{5,6},{6,7},{7,0},{32,39},{33,32},{3... | collective-permute-start | bytes 1769480 | tf_op jit(solution)/shard_map/ppermute | solution.py:129
  109.0 26.2 %collective-permute-start.5 = (bf16[1152,256]{1,0:T(8,128)(2,1)S(1)}, bf16[1152,256]{1,0:T(8,128)(2,1)S(1)}, u32[]{:S(2)}, u32[]{:S(2)}) collective-permute-start(bf16[1152,256]{1,0:T(8,128)(2,1)S(1)} %collective-permute-done.3), channel_id=1, source_target_pairs={{0,7},{1,0},{2,1},{3,2},{4,3},{5,4},{6,5},{7,6},{32,33},{33,34},{3... | collective-permute-start | bytes 1769480 | tf_op jit(solution)/shard_map/ppermute | solution.py:129
  113.0 17.2 %collective-permute-start.4 = (bf16[1152,256]{1,0:T(8,128)(2,1)S(1)}, bf16[1152,256]{1,0:T(8,128)(2,1)S(1)}, u32[]{:S(2)}, u32[]{:S(2)}) collective-permute-start(bf16[1152,256]{1,0:T(8,128)(2,1)S(1)} %collective-permute-done.2), channel_id=1, source_target_pairs={{0,1},{1,2},{2,3},{3,4},{4,5},{5,6},{6,7},{7,0},{32,39},{33,32},{3... | collective-permute-start | bytes 1769480 | tf_op jit(solution)/shard_map/ppermute | solution.py:129
  130.2 11.8 %collective-permute-start.6 = (bf16[1152,256]{1,0:T(8,128)(2,1)S(1)}, bf16[1152,256]{1,0:T(8,128)(2,1)S(1)}, u32[]{:S(2)}, u32[]{:S(2)}) collective-permute-start(bf16[1152,256]{1,0:T(8,128)(2,1)S(1)} %collective-permute-done.4), channel_id=1, source_target_pairs={{0,1},{1,2},{2,3},{3,4},{4,5},{5,6},{6,7},{7,0},{32,39},{33,32},{3... | collective-permute-start | bytes 1769480 | tf_op jit(solution)/shard_map/ppermute | solution.py:129
  142.5 1.1 copy-start.3

commit v9 on v4

--- a/solution.py
+++ b/solution.py
@@ -123,10 +123,13 @@
     front = [list(pieces), list(pieces)]
     totals = [term(c, 0) for c in pieces]
     for step in range(1, NZ // 2 + 1):
+        arrived = front[0][0]
         for i in range(2):
             for w in range(2):
                 if step == NZ // 2 and w != i:
                     continue
+                if step == NZ // 2 and i == 1:
+                    front[1][1], _ = lax.optimization_barrier((front[1][1], arrived))
                 front[w][i] = lax.ppermute(front[w][i], ("core", "z"), ways[w])
                 totals[i] = totals[i] + term(front[w][i], -step if w == 0 else step)
     both = jnp.concatenate([t.astype(bf).reshape(OCC, NP * HALF, cols) for t in totals], 1)

time: 143 us -> 143 us (level)
  transfers between devices with their start and end apart: 16 -> 16, of which waited for: 4 -> 5; matrix products, arithmetic and copies ran while one was open for 6% -> 6% of each run, Pallas kernels for 0% -> 0%
where the time goes in v9:
time: 143 us; the launch traced here: 142 us
  starting transfers between devices  78 us (55%)
  waiting for transfers between devices  31.1 us (22%)
  blocking collectives  16.1 us (11%)
  matrix products  10.1 us (7%)
  local copies, waits for them, and re-layouts  3.92 us (3%)
  other arithmetic  2.09 us (1%)
    ppermute x14, starting transfers between devices, body(): front[w][i] = lax.ppermute(front[w][i], ('core', 'z'), ways[w])  47.1 us
    all_to_all x1, starting transfers between devices, body(): held = lax.all_to_all(first, VIRT, split_axis=0, concat_axis=0, tiled=True)  20.5 us
    all_gather x1, blocking collectives, body(): gathered = lax.all_gather(diff, 'y', axis=0, tiled=False)  16.1 us
    all_to_all x1, waiting for transfers between devices, body(): lax.all_to_all(second, PAIR, split_axis=0, concat_axis=0, tiled=True)  12.5 us
    all_to_all x1, waiting for transfers between devices, body(): held = lax.all_to_all(first, VIRT, split_axis=0, concat_axis=0, tiled=True)  10.6 us
    all_to_all x1, starting transfers between devices, body(): lax.all_to_all(second, PAIR, split_axis=0, concat_axis=0, tiled=True)  10.5 us
    dot_general x21, matrix products, dot(): return jnp.dot(a, b, preferred_element_type=jnp.float32)  8.63 us
    ppermute x14, waiting for transfers between devices, body(): front[w][i] = lax.ppermute(front[w][i], ('core', 'z'), ways[w])  7.96 us
  transfers between devices with their start and end apart: 16, of which 5 were waited for; matrix products, arithmetic and copies ran while one was open for 6% of the time, Pallas kernels for 0%

profile of v9, /device:TPU:2, one launch (start us, length us, event | category | flops | bytes accessed | tf_op | source)
XLA Modules:
  0.0 141.8 jit_solution(13412451048064707685)
XLA Ops:
  2.0 20.5 %all-to-all-start = ((bf16[32,24,128]{2,1,0:T(8,128)(2,1)}), bf16[32,24,128]{2,1,0:T(8,128)(2,1)S(1)}, u32[]{:S(2)}, u32[]{:S(2)}) async-start(bf16[32,24,128]{2,1,0:T(8,128)(2,1)} %bitcast.1), calls=%async_computation | async-start | bytes 393216 | tf_op jit(solution)/shard_map/all_to_all | solution.py:86
  22.8 10.6 %all-to-all-done = bf16[32,24,128]{2,1,0:T(8,128)(2,1)S(1)} async-done(((bf16[32,24,128]{2,1,0:T(8,128)(2,1)}), bf16[32,24,128]{2,1,0:T(8,128)(2,1)S(1)}, u32[]{:S(2)}, u32[]{:S(2)}) %all-to-all-start) | async-done | bytes 196640 | tf_op jit(solution)/shard_map/all_to_all | solution.py:86
  34.8 10.5 %all-to-all-start.1 = ((bf16[32,24,128]{2,1,0:T(8,128)(2,1)}), bf16[32,24,128]{2,1,0:T(8,128)(2,1)S(1)}, u32[]{:S(2)}, u32[]{:S(2)}) async-start(bf16[32,24,128]{2,1,0:T(8,128)(2,1)} %bitcast.7), calls=%async_computation.1 | async-start | bytes 393216 | tf_op jit(solution)/shard_map/all_to_all | solution.py:90
  47.0 12.5 %all-to-all-done.1 = bf16[32,24,128]{2,1,0:T(8,128)(2,1)S(1)} async-done(((bf16[32,24,128]{2,1,0:T(8,128)(2,1)}), bf16[32,24,128]{2,1,0:T(8,128)(2,1)S(1)}, u32[]{:S(2)}, u32[]{:S(2)}) %all-to-all-start.1) | async-done | bytes 196640 | tf_op jit(solution)/shard_map/all_to_all | solution.py:90
  60.3 16.1 %all-gather = bf16[2304,128]{1,0:T(8,128)(2,1)S(1)} all-gather(bf16[576,128]{1,0:T(8,128)(2,1)S(1)} %fusion.12), channel_id=2, replica_groups=mesh['x'=8,'yh'=2,'core'=2,'y'=4,'z'=8] {'y'}, dimensions={0}, use_global_device_ids=true | all-gather | bytes 737280 | tf_op jit(solution)/shard_map/all_gather | solution.py:103
  77.1 3.2 %collective-permute-start = (bf16[576,256]{1,0:T(8,128)(2,1)}, bf16[576,256]{1,0:T(8,128)(2,1)S(1)}, u32[]{:S(2)}, u32[]{:S(2)}) collective-permute-start(bf16[576,256]{1,0:T(8,128)(2,1)} %pad_maximum_fusion), channel_id=1, source_target_pairs={{0,1},{1,2},{2,3},{3,4},{4,5},{5,6},{6,7},{7,0},{32,39},{33,32},{3... | collective-permute-start | bytes 884744 | tf_op jit(solution)/shard_map/ppermute | solution.py:133
  80.4 3.8 %collective-permute-start.1 = (bf16[576,256]{1,0:T(8,128)(2,1)}, bf16[576,256]{1,0:T(8,128)(2,1)}, u32[]{:S(2)}, u32[]{:S(2)}) collective-permute-start(bf16[576,256]{1,0:T(8,128)(2,1)} %pad_maximum_fusion), channel_id=1, source_target_pairs={{0,7},{1,0},{2,1},{3,2},{4,3},{5,4},{6,5},{7,6},{32,33},{33,34},{3... | collective-permute-start | bytes 884744 | tf_op jit(solution)/shard_map/ppermute | solution.py:133
  84.9 2.0 %collective-permute-start.7 = (bf16[576,256]{1,0:T(8,128)(2,1)}, bf16[576,256]{1,0:T(8,128)(2,1)S(1)}, u32[]{:S(2)}, u32[]{:S(2)}) collective-permute-start(bf16[576,256]{1,0:T(8,128)(2,1)} %pad_maximum_fusion.1), channel_id=1, source_target_pairs={{0,1},{1,2},{2,3},{3,4},{4,5},{5,6},{6,7},{7,0},{32,39},{33,32},{3... | collective-permute-start | bytes 884744 | tf_op jit(solution)/shard_map/ppermute | solution.py:133
  87.4 5.0 %collective-permute-start.8 = (bf16[576,256]{1,0:T(8,128)(2,1)}, bf16[576,256]{1,0:T(8,128)(2,1)S(1)}, u32[]{:S(2)}, u32[]{:S(2)}) collective-permute-start(bf16[576,256]{1,0:T(8,128)(2,1)} %pad_maximum_fusion.1), channel_id=1, source_target_pairs={{0,7},{1,0},{2,1},{3,2},{4,3},{5,4},{6,5},{7,6},{32,33},{33,34},{3... | collective-permute-start | bytes 884744 | tf_op jit(solution)/shard_map/ppermute | solution.py:133
  93.0 3.1 %collective-permute-start.3 = (bf16[576,256]{1,0:T(8,128)(2,1)}, bf16[576,256]{1,0:T(8,128)(2,1)S(1)}, u32[]{:S(2)}, u32[]{:S(2)}) collective-permute-start(bf16[576,256]{1,0:T(8,128)(2,1)} %collective-permute-done.1), channel_id=1, source_target_pairs={{0,7},{1,0},{2,1},{3,2},{4,3},{5,4},{6,5},{7,6},{32,33},{33,34},{3... | collective-permute-start | bytes 884744 | tf_op jit(solution)/shard_map/ppermute | solution.py:133
  96.2 2.7 %collective-permute-start.2 = (bf16[576,256]{1,0:T(8,128)(2,1)S(1)}, bf16[576,256]{1,0:T(8,128)(2,1)S(1)}, u32[]{:S(2)}, u32[]{:S(2)}) collective-permute-start(bf16[576,256]{1,0:T(8,128)(2,1)S(1)} %collective-permute-done), channel_id=1, source_target_pairs={{0,1},{1,2},{2,3},{3,4},{4,5},{5,6},{6,7},{7,0},{32,39},{33,32},{3... | collective-permute-start | bytes 884744 | tf_op jit(solution)/shard_map/ppermute | solution.py:133
  98.9 1.9 %collective-permute-start.9 = (bf16[576,256]{1,0:T(8,128)(2,1)S(1)}, bf16[576,256]{1,0:T(8,128)(2,1)S(1)}, u32[]{:S(2)}, u32[]{:S(2)}) collective-permute-start(bf16[576,256]{1,0:T(8,128)(2,1)S(1)} %collective-permute-done.7), channel_id=1, source_target_pairs={{0,1},{1,2},{2,3},{3,4},{4,5},{5,6},{6,7},{7,0},{32,39},{33,32},{3... | collective-permute-start | bytes 884744 | tf_op jit(solution)/shard_map/ppermute | solution.py:133
  101.5 5.1 %collective-permute-start.10 = (bf16[576,256]{1,0:T(8,128)(2,1)S(1)}, bf16[576,256]{1,0:T(8,128)(2,1)S(1)}, u32[]{:S(2)}, u32[]{:S(2)}) collective-permute-start(bf16[576,256]{1,0:T(8,128)(2,1)S(1)} %collective-permute-done.8), channel_id=1, source_target_pairs={{0,7},{1,0},{2,1},{3,2},{4,3},{5,4},{6,5},{7,6},{32,33},{33,34},{3... | collective-permute-start | bytes 884744 | tf_op jit(solution)/shard_map/ppermute | solution.py:133
  106.7 1.3 convolution_add_fusion.7
  108.3 3.6 %collective-permute-start.5 = (bf16[576,256]{1,0:T(8,128)(2,1)S(1)}, bf16[576,256]{1,0:T(8,128)(2,1)S(1)}, u32[]{:S(2)}, u32[]{:S(2)}) collective-permute-start(bf16[576,256]{1,0:T(8,128)(2,1)S(1)} %collective-permute-done.3), channel_id=1, source_target_pairs={{0,7},{1,0},{2,1},{3,2},{4,3},{5,4},{6,5},{7,6},{32,33},{33,34},{3... | collective-permute-start | bytes 884744 | tf_op jit(solution)/shard_map/ppermute | solution.py:133
  112.2 2.3 %collective-permute-start.4 = (bf16[576,256]{1,0:T(8,128)(2,1)S(1)}, bf16[576,256]{1,0:T(8,128)(2,1)S(1)}, u32[]{:S(2)}, u32[]{:S(2)}) collective-permute-start(bf16[576,256]{1,0:T(8,128)(2,1)S(1)} %collective-permute-done.2), channel_id=1, source_target_pairs={{0,1},{1,2},{2,3},{3,4},{4,5},{5,6},{6,7},{7,0},{32,39},{33,32},{3... | collective-permute-start | bytes 884744 | tf_op jit(solution)/shard_map/ppermute | solution.py:133
  114.5 4.8 %collective-permute-start.12 = (bf16[576,256]{1,0:T(8,128)(2,1)S(1)}, bf16[576,256]{1,0:T(8,128)(2,1)S(1)}, u32[]{:S(2)}, u32[]{:S(2)}) collective-permute-start(bf16[576,256]{1,0:T(8,128)(2,1)S(1)} %collective-permute-done.10), channel_id=1, source_target_pairs={{0,7},{1,0},{2,1},{3,2},{4,3},{5,4},{6,5},{7,6},{32,33},{33,34},{3... | collective-permute-start | bytes 884744 | tf_op jit(solution)/shard_map/ppermute | solution.py:133
  119.6 1.9 %collective-permute-start.11 = (bf16[576,256]{1,0:T(8,128)(2,1)S(1)}, bf16[576,256]{1,0:T(8,128)(2,1)S(1)}, u32[]{:S(2)}, u32[]{:S(2)}) collective-permute-start(bf16[576,256]{1,0:T(8,128)(2,1)S(1)} %collective-permute-done.9), channel_id=1, source_target_pairs={{0,1},{1,2},{2,3},{3,4},{4,5},{5,6},{6,7},{7,0},{32,39},{33,32},{3... | collective-permute-start | bytes 884744 | tf_op jit(solution)/shard_map/ppermute | solution.py:133
  122.2 1.3 collective-permute-done.12
  123.5 5.6 %collective-permute-start.13 = (bf16[576,256]{1,0:T(8,128)(2,1)S(1)}, bf16[576,256]{1,0:T(8,128)(2,1)S(1)}, u32[]{:S(2)}, u32[]{:S(2)}) collective-permute-start(bf16[576,256]{1,0:T(8,128)(2,1)S(1)} %collective-permute-done.12), channel_id=1, source_target_pairs={{0,7},{1,0},{2,1},{3,2},{4,3},{5,4},{6,5},{7,6},{32,33},{33,34},{3... | collective-permute-start | bytes 884744 | tf_op jit(solution)/shard_map/ppermute | solution.py:133
  129.1 1.9 %collective-permute-start.6 = (bf16[576,256]{1,0:T(8,128)(2,1)S(1)}, bf16[576,256]{1,0:T(8,128)(2,1)S(1)}, u32[]{:S(2)}, u32[]{:S(2)}) collective-permute-start(bf16[576,256]{1,0:T(8,128)(2,1)S(1)} %collective-permute-done.4), channel_id=1, source_target_pairs={{0,1},{1,2},{2,3},{3,4},{4,5},{5,6},{6,7},{7,0},{32,39},{33,32},{3... | collective-permute-start | bytes 884744 | tf_op jit(solution)/shard_map/ppermute | solution.py:133
  132.0 1.3 collective-permute-done.13
  133.6 5.3 %collective-permute-done.6 = bf16[576,256]{1,0:T(8,128)(2,1)S(1)} collective-permute-done((bf16[576,256]{1,0:T(8,128)(2,1)S(1)}, bf16[576,256]{1,0:T(8,128)(2,1)S(1)}, u32[]{:S(2)}, u32[]{:S(2)}) %collective-permute-start.6) | collective-permute-done | bytes 294944 | tf_op jit(solution)/shard_map/ppermute | solution.py:133
  140.3 1.5 %convolution_convert_fusion.1 = bf16[6,512,192]{1,2,0:T(8,128)(2,1)} fusion(bf16[6,192,192]{2,1,0:T(8,128)(2,1)S(1)} %copy-done.7, bf16[6,96,512]{2,1,0:T(8,128)(2,1)S(1)} %bitcast.55, bf16[6,96,512]{2,1,0:T(8,128)(2,1)S(1)} %bitcast.56), kind=kOutput, calls=%fused_computation.1 | convolution fusion | flops 229441536 | bytes 2801664 | tf_op jit(solution)/shard_map/bij,bjk->bik/dot_general | solution.py:136
  (62 shorter events, 13.4 us)
Async XLA Ops:
  0.0 0.9 copy-start
  0.0 33.5 %copy-start.2 = (bf16[768,768]{1,0:T(8,128)(2,1)S(1)}, bf16[768,768]{1,0:T(8,128)(2,1)}, u32[]{:S(2)}) copy-start(bf16[768,768]{1,0:T(8,128)(2,1)} %constant.180.clone) | copy-start | bytes 3538948
  0.0 22.5 %copy-start.6 = (s32[2,16]{1,0:T(2,128)S(1)}, s32[2,16]{1,0:T(2,128)}, u32[]{:S(2)}) copy-start(s32[2,16]{1,0:T(2,128)} %param.12) | copy-start | bytes 388
  0.0 22.7 %copy-start.5 = (s32[32,32,2]{1,2,0:T(2,128)S(1)}, s32[32,32,2]{1,2,0:T(2,128)}, u32[]{:S(2)}) copy-start(s32[32,32,2]{1,2,0:T(2,128)} %param.11) | copy-start | bytes 24580
  2.0 31.4 %all-to-all-start = ((bf16[32,24,128]{2,1,0:T(8,128)(2,1)}), bf16[32,24,128]{2,1,0:T(8,128)(2,1)S(1)}, u32[]{:S(2)}, u32[]{:S(2)}) async-start(bf16[32,24,128]{2,1,0:T(8,128)(2,1)} %bitcast.1), calls=%async_computation | async-start | bytes 393216 | tf_op jit(solution)/shard_map/all_to_all | solution.py:86
  33.5 26.0 %copy-start.4 = (bf16[2,576,768]{2,1,0:T(8,128)(2,1)S(1)}, bf16[2,576,768]{2,1,0:T(8,128)(2,1)}, u32[]{:S(2)}) copy-start(bf16[2,576,768]{2,1,0:T(8,128)(2,1)} %constant.182.clone) | copy-start | bytes 5308420
  34.0 25.8 %copy-start.3 = (bf16[576,768]{1,0:T(8,128)(2,1)S(1)}, bf16[576,768]{1,0:T(8,128)(2,1)}, u32[]{:S(2)}) copy-start(bf16[576,768]{1,0:T(8,128)(2,1)} %constant.183.clone) | copy-start | bytes 2654212
  34.8 24.6 %all-to-all-start.1 = ((bf16[32,24,128]{2,1,0:T(8,128)(2,1)}), bf16[32,24,128]{2,1,0:T(8,128)(2,1)S(1)}, u32[]{:S(2)}, u32[]{:S(2)}) async-start(bf16[32,24,128]{2,1,0:T(8,128)(2,1)} %bitcast.7), calls=%async_computation.1 | async-start | bytes 393216 | tf_op jit(solution)/shard_map/all_to_all | solution.py:90
  76.3 10.6 %copy-start.1 = (bf16[2048,512]{1,0:T(8,128)(2,1)S(1)}, bf16[2048,512]{1,0:T(8,128)(2,1)}, u32[]{:S(2)}) copy-start(bf16[2048,512]{1,0:T(8,128)(2,1)} %param.10) | copy-start | bytes 6291460
  77.1 19.1 %collective-permute-start = (bf16[576,256]{1,0:T(8,128)(2,1)}, bf16[576,256]{1,0:T(8,128)(2,1)S(1)}, u32[]{:S(2)}, u32[]{:S(2)}) collective-permute-start(bf16[576,256]{1,0:T(8,128)(2,1)} %pad_maximum_fusion), channel_id=1, source_target_pairs={{0,1},{1,2},{2,3},{3,4},{4,5},{5,6},{6,7},{7,0},{32,39},{33,32},{3... | collective-permute-start | bytes 884744 | tf_op jit(solution)/shard_map/ppermute | solution.py:133
  80.4 12.7 %collective-permute-start.1 = (bf16[576,256]{1,0:T(8,128)(2,1)}, bf16[576,256]{1,0:T(8,128)(2,1)}, u32[]{:S(2)}, u32[]{:S(2)}) collective-permute-start(bf16[576,256]{1,0:T(8,128)(2,1)} %pad_maximum_fusion), channel_id=1, source_target_pairs={{0,7},{1,0},{2,1},{3,2},{4,3},{5,4},{6,5},{7,6},{32,33},{33,34},{3... | collective-permute-start | bytes 884744 | tf_op jit(solution)/shard_map/ppermute | solution.py:133
  84.9 14.0 %collective-permute-start.7 = (bf16[576,256]{1,0:T(8,128)(2,1)}, bf16[576,256]{1,0:T(8,128)(2,1)S(1)}, u32[]{:S(2)}, u32[]{:S(2)}) collective-permute-start(bf16[576,256]{1,0:T(8,128)(2,1)} %pad_maximum_fusion.1), channel_id=1, source_target_pairs={{0,1},{1,2},{2,3},{3,4},{4,5},{5,6},{6,7},{7,0},{32,39},{33,32},{3... | collective-permute-start | bytes 884744 | tf_op jit(solution)/shard_map/ppermute | solution.py:133
  87.4 14.1 %collective-permute-start.8 = (bf16[576,256]{1,0:T(8,128)(2,1)}, bf16[576,256]{1,0:T(8,128)(2,1)S(1)}, u32[]{:S(2)}, u32[]{:S(2)}) collective-permute-start(bf16[576,256]{1,0:T(8,128)(2,1)} %pad_maximum_fusion.1), channel_id=1, source_target_pairs={{0,7},{1,0},{2,1},{3,2},{4,3},{5,4},{6,5},{7,6},{32,33},{33,34},{3... | collective-permute-start | bytes 884744 | tf_op jit(solution)/shard_map/ppermute | solution.py:133
  93.0 15.2 %collective-permute-start.3 = (bf16[576,256]{1,0:T(8,128)(2,1)}, bf16[576,256]{1,0:T(8,128)(2,1)S(1)}, u32[]{:S(2)}, u32[]{:S(2)}) collective-permute-start(bf16[576,256]{1,0:T(8,128)(2,1)} %collective-permute-done.1), channel_id=1, source_target_pairs={{0,7},{1,0},{2,1},{3,2},{4,3},{5,4},{6,5},{7,6},{32,33},{33,34},{3... | collective-permute-start | bytes 884744 | tf_op jit(solution)/shard_map/ppermute | solution.py:133
  96.2 16.0 %collective-permute-start.2 = (bf16[576,256]{1,0:T(8,128)(2,1)S(1)}, bf16[576,256]{1,0:T(8,128)(2,1)S(1)}, u32[]{:S(2)}, u32[]{:S(2)}) collective-permute-start(bf16[576,256]{1,0:T(8,128)(2,1)S(1)} %collective-permute-done), channel_id=1, source_target_pairs={{0,1},{1,2},{2,3},{3,4},{4,5},{5,6},{6,7},{7,0},{32,39},{33,32},{3... | collective-permute-start | bytes 884744 | tf_op jit(solution)/shard_map/ppermute | solution.py:133
  98.9 20.7 %collective-permute-start.9 = (bf16[576,256]{1,0:T(8,128)(2,1)S(1)}, bf16[576,256]{1,0:T(8,128)(2,1)S(1)}, u32[]{:S(2)}, u32[]{:S(2)}) collective-permute-start(bf16[576,256]{1,0:T(8,128)(2,1)S(1)} %collective-permute-done.7), channel_id=1, source_target_pairs={{0,1},{1,2},{2,3},{3,4},{4,5},{5,6},{6,7},{7,0},{32,39},{33,32},{3... | collective-permute-start | bytes 884744 | tf_op jit(solution)/shard_map/ppermute | solution.py:133
  101.5 13.0 %collective-permute-start.10 = (bf16[576,256]{1,0:T(8,128)(2,1)S(1)}, bf16[576,256]{1,0:T(8,128)(2,1)S(1)}, u32[]{:S(2)}, u32[]{:S(2)}) collective-permute-start(bf16[576,256]{1,0:T(8,128)(2,1)S(1)} %collective-permute-done.8), channel_id=1, source_target_pairs={{0,7},{1,0},{2,1},{3,2},{4,3},{5,4},{6,5},{7,6},{32,33},{33,34},{3... | collective-permute-start | bytes 884744 | tf_op jit(solution)/shard_map/ppermute | solution.py:133
  108.3 22.8 %collective-permute-start.5 = (bf16[576,256]{1,0:T(8,128)(2,1)S(1)}, bf16[576,256]{1,0:T(8,128)(2,1)S(1)}, u32[]{:S(2)}, u32[]{:S(2)}) collective-permute-start(bf16[576,256]{1,0:T(8,128)(2,1)S(1)} %collective-permute-done.3), channel_id=1, source_target_pairs={{0,7},{1,0},{2,1},{3,2},{4,3},{5,4},{6,5},{7,6},{32,33},{33,34},{3... | collective-permute-start | bytes 884744 | tf_op jit(solution)/shard_map/ppermute | solution.py:133
  112.2 10.0 %collective-permute-start.4 = (bf16[576,256]{1,0:T(8,128)(2,1)S(1)}, bf16[576,256]{1,0:T(8,128)(2,1)S(1)}, u32[]{:S(2)}, u32[]{:S(2)}) collective-permute-start(bf16[576,256]{1,0:T(8,128)(2,1)S(1)} %collective-permute-done.2), channel_id=1, source_target_pairs={{0,1},{1,2},{2,3},{3,4},{4,5},{5,6},{6,7},{7,0},{32,39},{33,32},{3... | collective-permute-start | bytes 884744 | tf_op jit(solution)/shard_map/ppermute | solution.py:133
  114.5 9.0 %collective-permute-start.12 = (bf16[576,256]{1,0:T(8,128)(2,1)S(1)}, bf16[576,256]{1,0:T(8,128)(2,1)S(1)}, u32[]{:S(2)}, u32[]{:S(2)}) collective-permute-start(bf16[576,256]{1,0:T(8,128)(2,1)S(1)} %collective-permute-done.10), channel_id=1, source_target_pairs={{0,7},{1,0},{2,1},{3,2},{4,3},{5,4},{6,5},{7,6},{32,33},{33,34},{3... | collective-permute-start | bytes 884744 | tf_op jit(solution)/shard_map/ppermute | solution.py:133
  119.6 19.7 %collective-permute-start.11 = (bf16[576,256]{1,0:T(8,128)(2,1)S(1)}, bf16[576,256]{1,0:T(8,128)(2,1)S(1)}, u32[]{:S(2)}, u32[]{:S(2)}) collective-permute-start(bf16[576,256]{1,0:T(8,128)(2,1)S(1)} %collective-permute-done.9), channel_id=1, source_target_pairs={{0,1},{1,2},{2,3},{3,4},{4,5},{5,6},{6,7},{7,0},{32,39},{33,32},{3... | collective-permute-start | bytes 884744 | tf_op jit(solution)/shard_map/ppermute | solution.py:133
  123.5 9.8 %collective-permute-start.13 = (bf16[576,256]{1,0:T(8,128)(2,1)S(1)}, bf16[576,256]{1,0:T(8,128)(2,1)S(1)}, u32[]{:S(2)}, u32[]{:S(2)}) collective-permute-start(bf16[576,256]{1,0:T(8,128)(2,1)S(1)} %collective-permute-done.12), channel_id=1, source_target_pairs={{0,7},{1,0},{2,1},{3,2},{4,3},{5,4},{6,5},{7,6},{32,33},{33,34},{3... | collective-permute-start | bytes 884744 | tf_op jit(solution)/shard_map/ppermute | solution.py:133
  129.1 9.8 %collective-permute-start.6 = (bf16[576,256]{1,0:T(8,128)(2,1)S(1)}, bf16[576,256]{1,0:T(8,128)(2,1)S(1)}, u32[]{:S(2)}, u32[]{:S(2)}) collective-permute-start(bf16[576,256]{1,0:T(8,128)(2,1)S(1)} %collective-permute-done.4), channel_id=1, source_target_pairs={{0,1},{1,2},{2,3},{3,4},{4,5},{5,6},{6,7},{7,0},{32,39},{33,32},{3... | collective-permute-start | bytes 884744 | tf_op jit(solution)/shard_map/ppermute | solution.py:133
  139.3 1.1 copy-start.7
